TPU v7x, 256 devices: a whole 4x4x8 slice. The times are simulated.
256 devices in a mesh: grp: 8 (over z_lo, core), row: 4 (over y), col: 8 (over z_hi, x).
Axes of the slice: x: 4, y: 4, z: 8 (z_hi: 2, z_lo: 4; z = z_hi * 4 + z_lo), core: 2. Of those that a mesh axis runs over, the one named last changes fastest.
Arguments:
- top_covariance: bfloat16 [12288, 1536], P(('grp', 'row', 'col')), parts along dimension 0, as said below
- first_panel: bfloat16 [256, 8, 128, 128], P(('grp', 'row', 'col')), parts along dimension 0, may hold values from -0.1796875 to 0.1796875
- first_inverse: bfloat16 [256, 128, 128], P(('grp', 'row', 'col')), parts along dimension 0, as said below
- first_index: int32 [256, 8], P(('grp', 'row', 'col')), parts along dimension 0, may hold values from 0 to 11, as said below
- second_panel: bfloat16 [8192, 4, 128, 128], P(('grp', 'row', 'col')), parts along dimension 0, may hold values from -0.1796875 to 0.1796875
- second_inverse: bfloat16 [8192, 128, 128], P(('grp', 'row', 'col')), parts along dimension 0, as said below
- second_positions: int32 [8192, 3], P(('grp', 'row', 'col')), parts along dimension 0, may hold values from 0 to 7, as said below
- row_order: int32 [1048576], P(('grp', 'row', 'col')), parts along dimension 0, may hold values from 0 to 4095, as said below
- sensitivity: bfloat16 [256, 256, 128], P(('grp', 'row', 'col')), parts along dimension 0, may hold values from -0.375 to 0.375
Outputs:
- first_cross: bfloat16 [256, 8, 128, 128], P(('grp', 'row', 'col')), parts along dimension 0
- first_diag: bfloat16 [256, 128, 128], P(('grp', 'row', 'col')), parts along dimension 0
- second_cross: bfloat16 [8192, 4, 128, 128], P(('grp', 'row', 'col')), parts along dimension 0
- second_diag: bfloat16 [8192, 128, 128], P(('grp', 'row', 'col')), parts along dimension 0
- tile_products: bfloat16 [1048576, 128], P(('grp', 'row', 'col')), parts along dimension 0
There are 8 independent parts, one for each index of `grp`. A program takes and returns all parts, laid end to end along the dimension named above; each array names one. Nothing has to cross between parts.
Inputs may be any that keep to these rules, and one draw needn't show every extreme that they name: `first_index`: each row holds 8 distinct block numbers in increasing order. `second_positions`: each row holds 3 distinct positions in increasing order. `row_order`: for every t, entries t * 32 * 128 to (t + 1) * 32 * 128 - 1 are a permutation of 0 to 4095. `top_covariance`: symmetric and positive definite. `first_inverse`: lower triangular with a diagonal of 0.8 to 1.25. `second_inverse`: lower triangular with a diagonal of 0.8 to 1.25.
All inputs are finite; a program needn't handle non-finite values.
Results may differ from a plain program's by a relative error of at most 0.006.
Values may be sent and summed in bfloat16 or wider, within the bound.
No kernel may reach another device: no remote copies, remote signals or barrier semaphores. Data moves between devices by JAX's collectives and lax.ppermute only.
A program may use at most 192 MiB of HBM per device.

v0:
```python
import jax
import jax.numpy as jnp
from jax import lax
from jax.sharding import PartitionSpec as P


def pick_blocks(full_top, index_row, block_rows):
    top_count = full_top.shape[1] // block_rows
    shaped = full_top.reshape(top_count, block_rows, top_count, block_rows)
    return jnp.take(jnp.take(shaped, index_row, axis=0), index_row, axis=2)


def child_fronts(sub_top, second_positions, rest_u):
    child_sub = jax.vmap(
        lambda pos_row: jnp.take(jnp.take(sub_top, pos_row, axis=0), pos_row, axis=2)
    )(second_positions)
    return jnp.einsum("crxqy,cqyz->crxz", child_sub, rest_u, preferred_element_type=jnp.float32)


def local(
    top_covariance,
    first_panel,
    first_inverse,
    first_index,
    second_panel,
    second_inverse,
    second_positions,
    row_order,
    sensitivity,
):
    block_rows = second_inverse.shape[-1]
    child_count = second_panel.shape[0]
    index_row = first_index[0]
    first_u = jnp.einsum(
        "pxy,yz->pxz", first_panel[0], first_inverse[0], preferred_element_type=jnp.float32
    ).astype(jnp.bfloat16)
    second_u = jnp.einsum(
        "ckxy,cyz->ckxz", second_panel, second_inverse, preferred_element_type=jnp.float32
    ).astype(jnp.bfloat16)
    rest_u = second_u[:, 1:]
    full_top = lax.all_gather(top_covariance, ("row", "col"), axis=0, tiled=True)
    sub_top = pick_blocks(full_top, index_row, block_rows)
    front_first = jnp.einsum("pxqy,qyz->pxz", sub_top, first_u, preferred_element_type=jnp.float32)
    front_second = child_fronts(sub_top, second_positions, rest_u)
    first_cross = (-front_first).astype(jnp.bfloat16)
    first_diag = (
        jnp.einsum(
            "yx,yz->xz", first_inverse[0], first_inverse[0], preferred_element_type=jnp.float32
        )
        - jnp.einsum("pyx,pyz->xz", first_u, first_cross, preferred_element_type=jnp.float32)
    ).astype(jnp.bfloat16)
    picked_cross = jnp.take(first_cross, second_positions, axis=0)
    cross_zero = -(
        jnp.einsum("xy,cyz->cxz", first_diag, second_u[:, 0], preferred_element_type=jnp.float32)
        + jnp.einsum("cqyx,cqyz->cxz", picked_cross, rest_u, preferred_element_type=jnp.float32)
    )
    cross_rest = -(
        jnp.einsum(
            "cqxy,cyz->cqxz", picked_cross, second_u[:, 0], preferred_element_type=jnp.float32
        )
        + front_second
    )
    second_cross = jnp.concatenate([cross_zero[:, None], cross_rest], axis=1).astype(jnp.bfloat16)
    second_diag = (
        jnp.einsum(
            "cyx,cyz->cxz", second_inverse, second_inverse, preferred_element_type=jnp.float32
        )
        - jnp.einsum("ckyx,ckyz->cxz", second_u, second_cross, preferred_element_type=jnp.float32)
    ).astype(jnp.bfloat16)
    cov_rows = jnp.concatenate([second_diag, second_cross[:, 0]], axis=-1).reshape(
        child_count * block_rows, 2 * block_rows
    )
    ordered = jnp.take(cov_rows, row_order, axis=0)
    received = lax.all_to_all(ordered, ("row", "col"), split_axis=0, concat_axis=0, tiled=True)
    tile_products = jnp.dot(received, sensitivity[0], preferred_element_type=jnp.float32).astype(
        jnp.bfloat16
    )
    return (first_cross[None], first_diag[None], second_cross, second_diag, tile_products)


def solution(mesh):
    return jax.shard_map(
        local,
        mesh=mesh,
        in_specs=(
            P(("grp", "row", "col"), None),
            P(("grp", "row", "col"), None, None, None),
            P(("grp", "row", "col"), None, None),
            P(("grp", "row", "col"), None),
            P(("grp", "row", "col"), None, None, None),
            P(("grp", "row", "col"), None, None),
            P(("grp", "row", "col"), None),
            P(("grp", "row", "col")),
            P(("grp", "row", "col"), None, None),
        ),
        out_specs=(
            P(("grp", "row", "col"), None, None, None),
            P(("grp", "row", "col"), None, None),
            P(("grp", "row", "col"), None, None, None),
            P(("grp", "row", "col"), None, None),
            P(("grp", "row", "col"), None),
        ),
        check_vma=False,
    )
```

profile of v0, /device:TPU:34, one launch (start us, length us, event | category | flops | bytes accessed | tf_op | source)
XLA Modules:
  0.0 312.1 jit_solution(2235903783247023106)
XLA Ops:
  7.2 0.0 copy-start
  7.2 0.0 all-gather.2.cloned.1.call-start
  7.2 0.7 all-gather.2.cloned.1.call-update
  7.9 0.7 compare_select_fusion.1
  8.6 0.1 copy.39
  8.7 0.1 reshape.89
  8.8 0.7 compare_and_fusion
  9.5 0.1 copy.38
  9.6 0.7 bitcast_or_fusion
  10.3 0.1 copy.43
  10.4 0.1 reshape.111
  10.5 0.8 fusion.35
  11.3 0.8 compare_and_fusion.1
  12.2 0.7 and_bitcast_fusion
  12.9 0.7 fusion.34
  13.6 1.2 convolution_convert_fusion.2
  14.8 1.9 fusion.39
  16.7 3.3 %convolution_convert_fusion.1 = bf16[32,4,128,128]{3,2,1,0:T(8,128)(2,1)} fusion(bf16[32,4,128,128]{3,2,1,0:T(8,128)(2,1)S(1)} %copy-done.7, bf16[32,128,128]{2,1,0:T(8,128)(2,1)S(1)} %copy-done), kind=kOutput, calls=%fused_computation.24 | convolution fusion | flops 538968064 | bytes 9437184 | tf_op jit(solution)/shard_map/ckxy,cyz->ckxz/dot_general | solution.py:37
  20.0 108.7 %all-gather.2.cloned.1.call-done = bf16[1536,1536]{1,0:T(8,128)(2,1)} async-done(((bf16[48,1536]{1,0:T(8,128)(2,1)}), bf16[1536,1536]{1,0:T(8,128)(2,1)}) %all-gather.2.cloned.1.call-update) | async-done | bytes 4718608 | tf_op jit(solution)/shard_map/all_gather | solution.py:41
  128.7 9.4 %reshape.70 = bf16[12,128,12,128]{3,2,1,0:T(8,128)(2,1)} reshape(bf16[1536,1536]{1,0:T(8,128)(2,1)} %all-gather.2.cloned.1.call-done) | data formatting | bytes 9437184 | tf_op jit(solution)/shard_map/reshape | solution.py:9
  138.1 6.4 %copy.36 = bf16[12,128,12,128]{3,1,2,0:T(8,128)(2,1)} copy(bf16[12,128,12,128]{3,2,1,0:T(8,128)(2,1)} %reshape.70) | data formatting | bytes 9437184 | tf_op jit(solution)/shard_map/reshape | solution.py:9
  144.5 4.9 %gather_fusion = bf16[8,128,12,128]{3,1,2,0:T(8,128)(2,1)} fusion(bf16[12,128,12,128]{3,1,2,0:T(8,128)(2,1)} %copy.36, s32[1024]{0:T(1024)S(1)} %pad_clamp_fusion.1), kind=kCustom, calls=%fused_computation | custom fusion | bytes 6291488 | tf_op jit(solution)/shard_map/jit(_take)/gather | solution.py:10
  149.4 3.9 %broadcast_select_fusion.1 = bf16[8,128,12,128]{3,1,2,0:T(8,128)(2,1)} fusion(bf16[8,128,12,128]{3,1,2,0:T(8,128)(2,1)} %gather_fusion, pred[8]{0:T(512)(128)(4,1)S(1)} %compare_and_fusion.1), kind=kLoop, calls=%fused_computation.18 | loop fusion | flops 1572864 | bytes 6291464 | tf_op jit(solution)/shard_map/jit(_take)/select_n | solution.py:10
  153.3 4.1 %gather_fusion.1 = bf16[8,8,128,128]{3,2,1,0:T(8,128)(2,1)} fusion(bf16[8,128,12,128]{3,1,2,0:T(8,128)(2,1)} %broadcast_select_fusion.1, s32[1024]{0:T(1024)S(1)} %pad_clamp_fusion.1), kind=kCustom, calls=%fused_computation.1 | custom fusion | bytes 4194336 | tf_op jit(solution)/shard_map/jit(_take)/gather | solution.py:10
  157.4 1.9 select_bitcast_fusion
  159.2 0.7 fusion.20
  159.9 0.0 copy-start.2
  159.9 0.3 convolution_bitcast_fusion.1
  160.2 10.2 %gather_fusion.3 = bf16[96,128,8,128]{3,1,2,0:T(8,128)(2,1)} fusion(bf16[8,128,8,128]{3,1,0,2:T(8,128)(2,1)S(1)} %select_bitcast_fusion, s32[1024]{0:T(1024)S(1)} %pad_clamp_fusion), kind=kCustom, calls=%fused_computation.3 | custom fusion | bytes 50332032 | tf_op jit(solution)/shard_map/vmap(jit(_take))/gather | solution.py:15
  170.5 2.7 gather_fusion.2
  173.1 0.2 fusion.21
  173.3 0.0 copy-start.9
  173.3 21.2 %broadcast_select_fusion = bf16[32,3,128,8,128]{4,2,3,1,0:T(8,128)(2,1)} fusion(bf16[32,3,128,8,128]{4,2,3,1,0:T(8,128)(2,1)} %bitcast.109, pred[32,3]{1,0:T(8,128)(4,1)S(1)} %copy.38), kind=kLoop, calls=%fused_computation.6 | loop fusion | flops 12582912 | bytes 50331744 | tf_op jit(solution)/shard_map/vmap(jit(_take))/select_n | solution.py:15
  194.5 16.2 %gather_fusion.5 = bf16[96,3,128,128]{3,2,1,0:T(8,128)(2,1)} fusion(bf16[32,3,128,8,128]{4,2,3,1,0:T(8,128)(2,1)} %broadcast_select_fusion, s32[96]{0:T(128)S(1)} %reshape.111), kind=kCustom, calls=%fused_computation.5 | custom fusion | bytes 18875136 | tf_op jit(solution)/shard_map/vmap(jit(_take))/gather | solution.py:15
  210.7 6.6 %fusion = f32[32,3,128,128,1]{3,2,1,4,0:T(8,128)S(1)} fusion(bf16[32,3,3,128,128]{4,3,2,1,0:T(8,128)(2,1)} %bitcast.112, pred[32,3]{1,0:T(8,128)(4,1)S(1)} %copy.38, bf16[32,4,128,128]{3,2,1,0:T(8,128)(2,1)} %convolution_convert_fusion.1), kind=kOutput, calls=%fused_computation.7 | convolution fusion | flops 1212678144 | bytes 18874464 | tf_op jit(solution)/shard_map/crxqy,cqyz->crxz/dot_general | solution.py:17
  217.3 0.4 fusion.24
  217.8 1.5 copy-done.5
  219.2 1.2 fusion.5
  220.4 1.5 fusion.14
  221.9 0.4 pad_maximum_fusion
  222.3 1.2 copy-done.6
  223.5 1.5 fusion.12
  225.0 0.5 copy-done.4
  225.5 0.2 pad_maximum_fusion.1
  225.7 17.0 %gather_fusion.4 = bf16[4096,256]{1,0:T(8,128)(2,1)} fusion(bf16[4096,256]{1,0:T(8,128)(2,1)S(1)} %pad_maximum_fusion.1, s32[4096]{0:T(1024)S(1)} %fusion.34), kind=kCustom, calls=%fused_computation.4 | custom fusion | bytes 4210688 | tf_op jit(solution)/shard_map/jit(_take)/gather | solution.py:73
  242.8 1.9 broadcast_select_fusion.7
  244.7 58.8 %all_to_all.9 = bf16[32,128,256]{2,1,0:T(8,128)(2,1)S(1)} all-to-all(bf16[32,128,256]{2,1,0:T(8,128)(2,1)S(1)} %broadcast_select_fusion.7), channel_id=1, replica_groups=mesh['grp'=8,'row'=4,'col'=8] {'row','col'}, dimensions={0} | all-to-all | bytes 4194304 | tf_op jit(solution)/shard_map/all_to_all | solution.py:74
  303.5 1.7 convolution_convert_fusion
  (20 shorter events, 0.1 us)
Async XLA Ops:
  7.2 7.6 %copy-start = (bf16[32,128,128]{2,1,0:T(8,128)(2,1)S(1)}, bf16[32,128,128]{2,1,0:T(8,128)(2,1)}, u32[]{:S(2)}) copy-start(bf16[32,128,128]{2,1,0:T(8,128)(2,1)} %param.14) | copy-start | bytes 3145732
  7.2 121.5 %all-gather.2.cloned.1.call-start = ((), (), s32[]{:S(2)}) async-start(), calls=%async_computation.1 | async-start | bytes 4866048 | tf_op jit(solution)/shard_map/all_gather | solution.py:41
  10.5 6.2 %copy-start.7 = (bf16[32,4,128,128]{3,2,1,0:T(8,128)(2,1)S(1)}, bf16[32,4,128,128]{3,2,1,0:T(8,128)(2,1)}, u32[]{:S(2)}) copy-start(bf16[32,4,128,128]{3,2,1,0:T(8,128)(2,1)} %param.13) | copy-start | bytes 12582916
  159.9 10.5 %copy-start.2 = (bf16[8,128,128]{2,1,0:T(8,128)(2,1)}, bf16[8,128,128]{2,1,0:T(8,128)(2,1)S(1)}, u32[]{:S(2)}) copy-start(bf16[8,128,128]{2,1,0:T(8,128)(2,1)S(1)} %fusion.20) | copy-start | bytes 786436
  170.5 2.7 copy-start.10
  173.3 44.0 %copy-start.9 = (bf16[128,128]{1,0:T(8,128)(2,1)}, bf16[128,128]{1,0:T(8,128)(2,1)S(1)}, u32[]{:S(2)}) copy-start(bf16[128,128]{1,0:T(8,128)(2,1)S(1)} %fusion.21) | copy-start | bytes 98308
  210.7 6.6 %copy-start.3 = (bf16[32,4,128,128]{3,2,1,0:T(8,128)(2,1)S(1)}, bf16[32,4,128,128]{3,2,1,0:T(8,128)(2,1)}, u32[]{:S(2)}) copy-start(bf16[32,4,128,128]{3,2,1,0:T(8,128)(2,1)} %convolution_convert_fusion.1) | copy-start | bytes 12582916
  217.3 1.9 copy-start.5
  221.9 1.6 copy-start.6
  223.5 2.0 copy-start.4
  225.5 17.3 %copy-start.8 = (bf16[32,128,128]{2,1,0:T(8,128)(2,1)}, bf16[32,128,128]{2,1,0:T(8,128)(2,1)S(1)}, u32[]{:S(2)}) copy-start(bf16[32,128,128]{2,1,0:T(8,128)(2,1)S(1)} %fusion.12) | copy-start | bytes 3145732
  244.7 58.8 %copy-start.11 = (bf16[1,256,128]{2,1,0:T(8,128)(2,1)S(1)}, bf16[1,256,128]{2,1,0:T(8,128)(2,1)}, u32[]{:S(2)}) copy-start(bf16[1,256,128]{2,1,0:T(8,128)(2,1)} %param.17) | copy-start | bytes 196612
  244.7 60.5 %copy-start.1 = (bf16[32,128,128]{2,1,0:T(8,128)(2,1)S(1)}, bf16[32,128,128]{2,1,0:T(8,128)(2,1)}, u32[]{:S(2)}) copy-start(bf16[32,128,128]{2,1,0:T(8,128)(2,1)} %param.14) | copy-start | bytes 3145732
Sparse Core Ops, SparseCore 0:
  11.4 117.2 all-gather.1
where the time goes:
time: 314 us; the launch traced here: 312 us
  waiting for transfers between devices  109 us (35%)
  local copies, waits for them, and re-layouts  74.7 us (24%)
  blocking collectives  58.8 us (19%)
  other arithmetic  34.6 us (11%)
  matrix products  20.3 us (6%)
  between operations  14.2 us (5%)
    all_gather x1, waiting for transfers between devices, local(): lax.all_gather(top_covariance, ('row', 'col'), axis=0, tiled=True)  109 us
    all_to_all x1, blocking collectives, local(): lax.all_to_all(ordered, ('row', 'col'), split_axis=0, concat_axis=0, tile...  58.8 us
    select_n x1, other arithmetic, child_fronts(): jnp.take(sub_top, pos_row, axis=0)  21.2 us
    gather x1, local copies, waits for them, and re-layouts, local(): ordered = jnp.take(cov_rows, row_order, axis=0)  17 us
    gather x3, local copies, waits for them, and re-layouts, child_fronts(): jnp.take(jnp.take(sub_top, pos_row, axis=0), pos_row, axis=2)  16.4 us
    reshape x2, local copies, waits for them, and re-layouts, pick_blocks(): shaped = full_top.reshape(top_count, block_rows, top_count, block_rows)  15.8 us
    gather x1, local copies, waits for them, and re-layouts, child_fronts(): jnp.take(sub_top, pos_row, axis=0)  10.2 us
    gather x2, local copies, waits for them, and re-layouts, pick_blocks(): return jnp.take(jnp.take(shaped, index_row, axis=0), index_row, axis=2)  8.99 us
  transfers between devices with their start and end apart: 1, of which 1 were waited for; matrix products, arithmetic and copies ran while one was open for 4% of the time, Pallas kernels for 0%

commit v1 on v0

v1 whole, which is shorter than its diff:
```python
import functools

import jax
import jax.numpy as jnp
from jax import lax
from jax.experimental import pallas as pl
from jax.experimental.pallas import tpu as pltpu
from jax.sharding import PartitionSpec as P

B = 128
NA = 12
PS = 8
Q = 3
WIN = 8
SHARD = 48
F32 = jnp.float32
BF = jnp.bfloat16
REL = (0, 1, -1, 2)


def mm(a, b):
    return jnp.dot(a, b, preferred_element_type=F32)


def mm_tn(a, b):
    return lax.dot_general(a, b, (((0,), (0,)), ((), ())), preferred_element_type=F32)


def mm_tt(a, b):
    return lax.dot_general(a, b, (((0,), (1,)), ((), ())), preferred_element_type=F32)


def flip(x):
    return x.astype(F32).T.astype(BF)


def pack_kernel(pos, x_ref, o_ref):
    first = (3 * pos[0]) // 8
    for k in range(WIN):
        col = lax.rem(first + k, NA)
        o_ref[k // 4, k % 4] = x_ref[:, pl.ds(pl.multiple_of(col * B, B), B)]


def pack(x, me):
    return pl.pallas_call(
        pack_kernel,
        out_shape=jax.ShapeDtypeStruct((2, 4, SHARD, B), BF),
        in_specs=[
            pl.BlockSpec(memory_space=pltpu.SMEM),
            pl.BlockSpec(memory_space=pltpu.VMEM),
        ],
        out_specs=pl.BlockSpec(memory_space=pltpu.VMEM),
        name="pack",
    )(me.reshape(1), x)


KIDS = 4


def early_kernel(fp, fi, sp, si, fu, fut, fw, su, sut, sw):
    @pl.when(pl.program_id(0) == 0)
    def _():
        inv = fi[0]
        pan = fp[0].reshape(PS * B, B)
        fu[...] = mm(pan, inv).astype(BF)
        fut[...] = mm_tt(inv, pan).astype(BF)
        fw[...] = mm_tn(inv, inv)

    for c in range(KIDS):
        inv = si[c]
        pan = sp[c].reshape((Q + 1) * B, B)
        su[c] = mm(pan, inv).astype(BF)
        sut[c] = mm_tt(inv, pan).astype(BF)
        sw[c] = mm_tn(inv, inv)


def early(fp, fi, sp, si):
    n = sp.shape[0]
    whole = lambda *s: pl.BlockSpec(s, lambda i: (0,) * len(s))
    part = lambda *s: pl.BlockSpec((KIDS,) + s, lambda i: (i,) + (0,) * len(s))
    return pl.pallas_call(
        early_kernel,
        grid=(n // KIDS,),
        out_shape=(
            jax.ShapeDtypeStruct((PS * B, B), BF),
            jax.ShapeDtypeStruct((B, PS * B), BF),
            jax.ShapeDtypeStruct((B, B), F32),
            jax.ShapeDtypeStruct((n, (Q + 1) * B, B), BF),
            jax.ShapeDtypeStruct((n, B, (Q + 1) * B), BF),
            jax.ShapeDtypeStruct((n, B, B), F32),
        ),
        in_specs=[
            whole(1, PS, B, B),
            whole(1, B, B),
            part(Q + 1, B, B),
            part(B, B),
        ],
        out_specs=(
            whole(PS * B, B),
            whole(B, PS * B),
            whole(B, B),
            part((Q + 1) * B, B),
            part(B, (Q + 1) * B),
            part(B, B),
        ),
        cost_estimate=pl.CostEstimate(
            flops=300 * 2 * B**3, bytes_accessed=20 * 2**20, transcendentals=0
        ),
        compiler_params=pltpu.CompilerParams(vmem_limit_bytes=32 * 2**20),
        name="early",
    )(fp, fi, sp, si)


def late_kernel(
    steps, pos, fidx, spos, order,
    a0, a1, a2, a3, b0, b1, b2, b3, fu, fut, fw, su, sut, sw,
    fc_o, fd_o, sc_o, sd_o, rows_o,
    full, tmat, cov, got,
):
    step = pl.program_id(0)

    @pl.when(step == 0)
    def _():
        me = pos[0]
        row, zh, x = me // 8, (me // 4) % 2, me % 4
        for half, group in enumerate(((a0, a1, a2, a3), (b0, b1, b2, b3))):
            for t in range(4):
                for u in range(4):
                    dr, dx = (REL[t], REL[u]) if half == 0 else (REL[u], REL[t])
                    r = lax.rem(row - dr + 4, 4)
                    xx = lax.rem(x - dx + 4, 4)
                    for z in range(2):
                        src = r * 8 + lax.rem(zh + z, 2) * 4 + xx
                        first = (3 * src) // 8
                        at = pl.multiple_of(src * SHARD, 16)
                        for k in range(4):
                            col = lax.rem(first + half * 4 + k, NA)
                            full[pl.ds(at, SHARD), pl.ds(pl.multiple_of(col * B, B), B)] = (
                                group[t][u, z, k]
                            )

        def block(p, q):
            return full[
                pl.ds(pl.multiple_of(p * B, B), B), pl.ds(pl.multiple_of(q * B, B), B)
            ]

        for p in range(PS):
            ap = fidx[0, p]
            tmat[(1 + p) * B:(2 + p) * B, (1 + p) * B:(2 + p) * B] = block(ap, ap)
            for q in range(p + 1, PS):
                aq = fidx[0, q]
                near = aq - ap <= 6
                i, j = jnp.where(near, p, q), jnp.where(near, q, p)
                held = block(jnp.where(near, ap, aq), jnp.where(near, aq, ap))
                ri = pl.ds(pl.multiple_of((1 + i) * B, B), B)
                rj = pl.ds(pl.multiple_of((1 + j) * B, B), B)
                tmat[ri, rj] = held
                tmat[rj, ri] = flip(held)
        cross = (-mm(tmat[B:, B:], fu[...])).astype(BF)
        fc_o[...] = cross.reshape(1, PS, B, B)
        tmat[B:, :B] = cross
        for p in range(PS):
            tmat[:B, (1 + p) * B:(2 + p) * B] = flip(cross[p * B:(p + 1) * B])
        diag = (fw[...] - mm(fut[...], cross)).astype(BF)
        fd_o[0] = diag
        tmat[:B, :B] = diag

    @pl.when(step < steps)
    def _():
        for c in range(KIDS):
            kid = step * KIDS + c
            at = [0] + [(1 + spos[kid * Q + q]) * B for q in range(Q)]
            at = [pl.ds(pl.multiple_of(v, B), B) for v in at]
            u = su[c]
            ws = []
            for r in range(Q + 1):
                line = jnp.concatenate([tmat[at[r], at[q]] for q in range(Q + 1)], axis=1)
                w = (-mm(line, u)).astype(BF)
                sc_o[c, r] = w
                ws.append(w)
            d = (sw[c] - mm(sut[c], jnp.concatenate(ws, axis=0))).astype(BF)
            sd_o[c] = d
            base = kid * 2 * B
            cov[pl.ds(base, B, stride=2), :] = d.astype(F32)
            cov[pl.ds(base + 1, B, stride=2), :] = ws[0].astype(F32)

    @pl.when(step >= steps)
    def _():
        n = KIDS * B
        base = (step - steps) * n

        def body(g, carry):
            for j in range(16):
                src = order[base + g * 16 + j]
                got[pl.ds(pl.multiple_of(g * 32, 32) + 2 * j, 2), :] = cov[
                    pl.ds(pl.multiple_of(src * 2, 2), 2), :
                ]
            return carry

        lax.fori_loop(0, n // 16, body, 0)
        rows_o[:, :B] = got[pl.ds(0, n, stride=2), :].astype(BF)
        rows_o[:, B:] = got[pl.ds(1, n, stride=2), :].astype(BF)


def late(me, fidx, spos, order, ga, gb, fu, fut, fw, su, sut, sw):
    n = su.shape[0]
    steps = n // KIDS
    whole = lambda *s: pl.BlockSpec(s, lambda i: (0,) * len(s))
    part = lambda *s: pl.BlockSpec(
        (KIDS,) + s, lambda i: (jnp.minimum(i, steps - 1),) + (0,) * len(s)
    )
    smem = pl.BlockSpec(memory_space=pltpu.SMEM)
    return pl.pallas_call(
        functools.partial(late_kernel, steps),
        grid=(2 * steps,),
        out_shape=(
            jax.ShapeDtypeStruct((1, PS, B, B), BF),
            jax.ShapeDtypeStruct((1, B, B), BF),
            jax.ShapeDtypeStruct((n, Q + 1, B, B), BF),
            jax.ShapeDtypeStruct((n, B, B), BF),
            jax.ShapeDtypeStruct((n * B, 2 * B), BF),
        ),
        in_specs=[smem] * 4
        + [whole(4, 2, 4, SHARD, B)] * 8
        + [
            whole(PS * B, B),
            whole(B, PS * B),
            whole(B, B),
            part((Q + 1) * B, B),
            part(B, (Q + 1) * B),
            part(B, B),
        ],
        out_specs=(
            whole(1, PS, B, B),
            whole(1, B, B),
            part(Q + 1, B, B),
            part(B, B),
            pl.BlockSpec((KIDS * B, 2 * B), lambda i: (jnp.maximum(i - steps, 0), 0)),
        ),
        scratch_shapes=[
            pltpu.VMEM((NA * B, NA * B), BF),
            pltpu.VMEM(((PS + 1) * B, (PS + 1) * B), BF),
            pltpu.VMEM((2 * n * B, B), F32),
            pltpu.VMEM((2 * KIDS * B, B), F32),
        ],
        cost_estimate=pl.CostEstimate(
            flops=720 * 2 * B**3, bytes_accessed=20 * 2**20, transcendentals=0
        ),
        compiler_params=pltpu.CompilerParams(vmem_limit_bytes=48 * 2**20),
        name="late",
    )(me.reshape(1), fidx, spos.reshape(-1), order, *ga, *gb, fu, fut, fw, su, sut, sw)


def along_x(v, k):
    return lax.ppermute(
        v, "col", [(z * 4 + x, z * 4 + (x + k) % 4) for z in range(2) for x in range(4)]
    )


def along_row(v, k):
    return lax.ppermute(v, "row", [(r, (r + k) % 4) for r in range(4)])


def spread(v, move):
    return [v] + [move(v, k) for k in REL[1:]]


def local(
    top_covariance,
    first_panel,
    first_inverse,
    first_index,
    second_panel,
    second_inverse,
    second_positions,
    row_order,
    sensitivity,
):
    me = (lax.axis_index("row") * 8 + lax.axis_index("col")).astype(jnp.int32)
    mine = pack(top_covariance, me)
    other = lax.ppermute(mine, "col", [(c, (c + 4) % 8) for c in range(8)])
    half_a = jnp.stack([mine[0], other[0]])
    half_b = jnp.stack([mine[1], other[1]])
    ga = spread(jnp.stack(spread(half_a, along_x)), along_row)
    gb = spread(jnp.stack(spread(half_b, along_row)), along_x)
    fu, fut, fw, su, sut, sw = early(first_panel, first_inverse, second_panel, second_inverse)
    first_cross, first_diag, second_cross, second_diag, ordered = late(
        me, first_index, second_positions, row_order, ga, gb, fu, fut, fw, su, sut, sw
    )
    received = lax.all_to_all(ordered, ("row", "col"), split_axis=0, concat_axis=0, tiled=True)
    tile_products = jnp.dot(received, sensitivity[0], preferred_element_type=F32).astype(BF)
    return (first_cross, first_diag, second_cross, second_diag, tile_products)


def solution(mesh):
    own = ("grp", "row", "col")
    return jax.shard_map(
        local,
        mesh=mesh,
        in_specs=(
            P(own, None),
            P(own, None, None, None),
            P(own, None, None),
            P(own, None),
            P(own, None, None, None),
            P(own, None, None),
            P(own, None),
            P(own),
            P(own, None, None),
        ),
        out_specs=(
            P(own, None, None, None),
            P(own, None, None),
            P(own, None, None, None),
            P(own, None, None),
            P(own, None),
        ),
        check_vma=False,
    )
```

time: 314 us -> 144 us (0.46)
  the two profiles are of different devices: /device:TPU:34 before, /device:TPU:66 now
where the time goes in v1:
time: 144 us
  blocking collectives  60 us (42%)
  Pallas kernels  29.5 us (20%)
  starting transfers between devices  25 us (17%)
  waiting for transfers between devices  17.1 us (12%)
  local copies, waits for them, and re-layouts  9.55 us (7%)
  matrix products  1.68 us (1%)
    all_to_all x1, blocking collectives, local(): lax.all_to_all(ordered, ('row', 'col'), split_axis=0, concat_axis=0, tile...  60 us
    pallas_call x1, Pallas kernels, late(): pl.pallas_call(functools.partial(late_kernel, steps), grid=(2 * steps,),...  23.6 us
    ppermute x6, starting transfers between devices, along_x(): lax.ppermute(v, 'col', [(z * 4 + x, z * 4 + (x + k) % 4) for z in range(2...  10.9 us
    ppermute x6, starting transfers between devices, along_row(): return lax.ppermute(v, 'row', [(r, (r + k) % 4) for r in range(4)])  8.74 us
    unnamed x23, local copies, waits for them, and re-layouts  8.6 us
    ppermute x6, waiting for transfers between devices, along_row(): return lax.ppermute(v, 'row', [(r, (r + k) % 4) for r in range(4)])  7.35 us
    ppermute x1, starting transfers between devices, local(): other = lax.ppermute(mine, 'col', [(c, (c + 4) % 8) for c in range(8)])  5.39 us
    ppermute x6, waiting for transfers between devices, along_x(): lax.ppermute(v, 'col', [(z * 4 + x, z * 4 + (x + k) % 4) for z in range(2...  5.15 us
  transfers between devices with their start and end apart: 13, of which 6 were waited for; matrix products, arithmetic and copies ran while one was open for 1% of the time, Pallas kernels for 3%

profile of v1, /device:TPU:66, one launch (start us, length us, event | category | flops | bytes accessed | tf_op | source)
XLA Modules:
  0.0 143.8 jit_solution(8224595792420493962)
XLA Ops:
  0.6 0.0 copy-start
  0.6 0.0 copy-start.10
  0.7 0.0 copy-start.5
  0.7 0.0 copy-start.7
  0.7 1.7 %pack.1 = bf16[2,4,48,128]{3,2,1,0:T(8,128)(2,1)} custom-call(s32[1]{0:T(128)} %bitcast.pos, bf16[48,1536]{1,0:T(8,128)(2,1)} %x_ref.1), custom_call_target="tpu_custom_call" | custom-call | tf_op jit(solution)/shard_map/pack/pallas_call | solution.py:45
  2.3 5.4 %collective-permute-start = (bf16[2,4,48,128]{3,2,1,0:T(8,128)(2,1)}, bf16[2,4,48,128]{3,2,1,0:T(8,128)(2,1)S(1)}, u32[]{:S(2)}, u32[]{:S(2)}) collective-permute-start(bf16[2,4,48,128]{3,2,1,0:T(8,128)(2,1)} %pack.1), channel_id=1, source_target_pairs={{0,4},{1,5},{2,6},{3,7},{4,0},{5,1},{6,2},{7,3},{8,12},{9,13},{10,... | collective-permute-start | bytes 294920 | tf_op jit(solution)/shard_map/ppermute | solution.py:281
  7.7 0.8 fusion.3
  8.6 4.6 %collective-permute-done = bf16[2,4,48,128]{3,2,1,0:T(8,128)(2,1)S(1)} collective-permute-done((bf16[2,4,48,128]{3,2,1,0:T(8,128)(2,1)}, bf16[2,4,48,128]{3,2,1,0:T(8,128)(2,1)S(1)}, u32[]{:S(2)}, u32[]{:S(2)}) %collective-permute-start) | collective-permute-done | bytes 98336 | tf_op jit(solution)/shard_map/ppermute | solution.py:281
  13.2 0.6 collective-permute-start.2
  13.9 1.5 %collective-permute-start.1 = (bf16[2,4,48,128]{3,2,1,0:T(8,128)(2,1)S(1)}, bf16[2,4,48,128]{3,2,1,0:T(8,128)(2,1)S(1)}, u32[]{:S(2)}, u32[]{:S(2)}) collective-permute-start(bf16[2,4,48,128]{3,2,1,0:T(8,128)(2,1)S(1)} %get-tuple-element.34), channel_id=1, source_target_pairs={{0,1},{1,2},{2,3},{3,0},{4,5},{5,6},{6,7},{7,4},{8,9},{9,10},{10,1... | collective-permute-start | bytes 294920 | tf_op jit(solution)/shard_map/ppermute | solution.py:255
  15.3 3.3 %collective-permute-start.3 = (bf16[2,4,48,128]{3,2,1,0:T(8,128)(2,1)S(1)}, bf16[2,4,48,128]{3,2,1,0:T(8,128)(2,1)S(1)}, u32[]{:S(2)}, u32[]{:S(2)}) collective-permute-start(bf16[2,4,48,128]{3,2,1,0:T(8,128)(2,1)S(1)} %get-tuple-element.34), channel_id=1, source_target_pairs={{0,2},{1,3},{2,0},{3,1},{4,6},{5,7},{6,4},{7,5},{8,10},{9,11},{10,... | collective-permute-start | bytes 294920 | tf_op jit(solution)/shard_map/ppermute | solution.py:255
  18.7 0.0 collective-permute-done.2
  18.7 1.5 %collective-permute-done.1 = bf16[2,4,48,128]{3,2,1,0:T(8,128)(2,1)S(1)} collective-permute-done((bf16[2,4,48,128]{3,2,1,0:T(8,128)(2,1)S(1)}, bf16[2,4,48,128]{3,2,1,0:T(8,128)(2,1)S(1)}, u32[]{:S(2)}, u32[]{:S(2)}) %collective-permute-start.1) | collective-permute-done | bytes 98336 | tf_op jit(solution)/shard_map/ppermute | solution.py:255
  20.2 1.2 collective-permute-done.3
  21.5 0.1 pad_maximum_fusion.a0
  21.5 3.3 %collective-permute-start.6 = (bf16[4,2,4,48,128]{4,3,2,1,0:T(8,128)(2,1)S(1)}, bf16[4,2,4,48,128]{4,3,2,1,0:T(8,128)(2,1)S(1)}, u32[]{:S(2)}, u32[]{:S(2)}) collective-permute-start(bf16[4,2,4,48,128]{4,3,2,1,0:T(8,128)(2,1)S(1)} %pad_maximum_fusion.a0), channel_id=1, source_target_pairs={{0,16},{8,24},{16,0},{24,8},{1,17},{9,25},{17,1},{25,9},{2,18},{10... | collective-permute-start | bytes 1179656 | tf_op jit(solution)/shard_map/ppermute | solution.py:261
  24.8 1.1 collective-permute-start.8
  26.0 1.0 collective-permute-start.7
  26.9 0.7 collective-permute-start.9
  27.7 2.6 %collective-permute-start.5 = (bf16[4,2,4,48,128]{4,3,2,1,0:T(8,128)(2,1)S(1)}, bf16[4,2,4,48,128]{4,3,2,1,0:T(8,128)(2,1)S(1)}, u32[]{:S(2)}, u32[]{:S(2)}) collective-permute-start(bf16[4,2,4,48,128]{4,3,2,1,0:T(8,128)(2,1)S(1)} %pad_maximum_fusion.a0), channel_id=1, source_target_pairs={{0,24},{8,0},{16,8},{24,16},{1,25},{9,1},{17,9},{25,17},{2,26},{10... | collective-permute-start | bytes 1179656 | tf_op jit(solution)/shard_map/ppermute | solution.py:261
  30.3 7.3 %collective-permute-done.8 = bf16[2,4,48,128]{3,2,1,0:T(8,128)(2,1)S(1)} collective-permute-done((bf16[2,4,48,128]{3,2,1,0:T(8,128)(2,1)S(1)}, bf16[2,4,48,128]{3,2,1,0:T(8,128)(2,1)S(1)}, u32[]{:S(2)}, u32[]{:S(2)}) %collective-permute-start.8) | collective-permute-done | bytes 98336 | tf_op jit(solution)/shard_map/ppermute | solution.py:261
  37.6 0.0 collective-permute-start.4
  37.6 0.0 collective-permute-done.7
  37.6 0.0 collective-permute-done.9
  37.6 0.1 pad_maximum_fusion.1.b0
  37.7 3.4 %collective-permute-start.12 = (bf16[4,2,4,48,128]{4,3,2,1,0:T(8,128)(2,1)S(1)}, bf16[4,2,4,48,128]{4,3,2,1,0:T(8,128)(2,1)S(1)}, u32[]{:S(2)}, u32[]{:S(2)}) collective-permute-start(bf16[4,2,4,48,128]{4,3,2,1,0:T(8,128)(2,1)S(1)} %pad_maximum_fusion.1.b0), channel_id=1, source_target_pairs={{0,2},{1,3},{2,0},{3,1},{4,6},{5,7},{6,4},{7,5},{8,10},{9,11},{10,... | collective-permute-start | bytes 1179656 | tf_op jit(solution)/shard_map/ppermute | solution.py:255
  41.1 0.2 collective-permute-start.11
  41.4 0.0 collective-permute-done.6.a3
  41.4 1.8 %collective-permute-start.10 = (bf16[4,2,4,48,128]{4,3,2,1,0:T(8,128)(2,1)S(1)}, bf16[4,2,4,48,128]{4,3,2,1,0:T(8,128)(2,1)}, u32[]{:S(2)}, u32[]{:S(2)}) collective-permute-start(bf16[4,2,4,48,128]{4,3,2,1,0:T(8,128)(2,1)S(1)} %pad_maximum_fusion.1.b0), channel_id=1, source_target_pairs={{0,1},{1,2},{2,3},{3,0},{4,5},{5,6},{6,7},{7,4},{8,9},{9,10},{10,1... | collective-permute-start | bytes 1179656 | tf_op jit(solution)/shard_map/ppermute | solution.py:255
  43.2 0.1 copy.15
  43.2 0.1 reshape.20.spos
  43.4 0.0 copy-start.3
  43.4 2.2 %copy-done.3 = bf16[32,4,128,128]{3,2,1,0:T(8,128)(2,1)S(1)} copy-done((bf16[32,4,128,128]{3,2,1,0:T(8,128)(2,1)S(1)}, bf16[32,4,128,128]{3,2,1,0:T(8,128)(2,1)}, u32[]{:S(2)}) %copy-start.3) | copy-done | bytes 4194328
  45.6 0.9 copy-done.6
  46.5 4.2 %early.1 = (bf16[1024,128]{1,0:T(8,128)(2,1)S(1)}, bf16[128,1024]{1,0:T(8,128)(2,1)S(1)}, f32[128,128]{1,0:T(8,128)S(1)}, bf16[32,512,128]{2,1,0:T(8,128)(2,1)S(...) custom-call(bf16[1,8,128,128]{3,2,1,0:T(8,128)(2,1)S(1)} %copy-done.6, ...), custom_call_target="tpu_custom_call" | custom-call | flops 1258291200 | bytes 20971520 | tf_op jit(solution)/shard_map/early/pallas_call | solution.py:81
  50.7 0.0 copy-start.1
  50.8 1.9 %copy-done.1 = bf16[32,512,128]{2,1,0:T(8,128)(2,1)} copy-done((bf16[32,512,128]{2,1,0:T(8,128)(2,1)}, bf16[32,512,128]{2,1,0:T(8,128)(2,1)S(1)}, u32[]{:S(2)}) %copy-start.1) | copy-done | bytes 4194328
  52.7 2.0 %copy-done.2 = bf16[32,128,512]{2,1,0:T(8,128)(2,1)} copy-done((bf16[32,128,512]{2,1,0:T(8,128)(2,1)}, bf16[32,128,512]{2,1,0:T(8,128)(2,1)S(1)}, u32[]{:S(2)}) %copy-start.2) | copy-done | bytes 4194328
  54.7 1.4 copy-done.4
  56.1 0.0 collective-permute-done.5.a2
  56.1 0.0 collective-permute-done.4.a1
  56.1 0.0 collective-permute-done.12.b3
  56.1 2.0 %collective-permute-done.11.b2 = bf16[4,2,4,48,128]{4,3,2,1,0:T(8,128)(2,1)} collective-permute-done((bf16[4,2,4,48,128]{4,3,2,1,0:T(8,128)(2,1)S(1)}, bf16[4,2,4,48,128]{4,3,2,1,0:T(8,128)(2,1)}, u32[]{:S(2)}, u32[]{:S(2)}) %collective-permute-start.11) | collective-permute-done | bytes 393248 | tf_op jit(solution)/shard_map/ppermute | solution.py:255
  58.1 0.4 collective-permute-done.10.b1
  58.5 0.0 copy-done.9
  58.5 23.6 %late.1 = (bf16[1,8,128,128]{3,2,1,0:T(8,128)(2,1)}, bf16[1,128,128]{2,1,0:T(8,128)(2,1)}, bf16[32,4,128,128]{3,2,1,0:T(8,128)(2,1)}, bf16[32,128,128]{2,1,0:T(8,128)(2,1)}, bf16[4096,256]{1,0:T(8,128)(2,1)S(1)}) custom-call(s32[1]{0:T(128)} %bitcast.pos, s32[1,8]{1,0:T(1,128)S(1)} %copy-done.9, s32[96]{0:T(128)S(1)} %reshape.20.spos, s32[4096]{0:T(1024)S(1)} %copy-done.8, ...), custom_call_target="tpu_custom_call" | custom-call | flops 3019898880 | bytes 20971520 | tf_op jit(solution)/shard_map/late/pallas_call | solution.py:213
  82.1 60.0 %all_to_all.12 = bf16[32,128,256]{2,1,0:T(8,128)(2,1)S(1)} all-to-all(bf16[32,128,256]{2,1,0:T(8,128)(2,1)S(1)} %bitcast.17), channel_id=1, replica_groups=mesh['grp'=8,'row'=4,'col'=8] {'row','col'}, dimensions={0} | all-to-all | bytes 4194304 | tf_op jit(solution)/shard_map/all_to_all | solution.py:290
  142.1 1.7 %convolution_convert_fusion = bf16[4096,128]{1,0:T(8,128)(2,1)} fusion(bf16[4096,256]{1,0:T(8,128)(2,1)S(1)} %bitcast.18, bf16[1,256,128]{2,1,0:T(8,128)(2,1)S(1)} %copy-done), kind=kOutput, calls=%fused_computation | convolution fusion | flops 268959744 | bytes 3211264 | tf_op jit(solution)/shard_map/dot_general | solution.py:291
  (13 shorter events, 0.1 us)
Async XLA Ops:
  0.6 141.5 %copy-start = (bf16[1,256,128]{2,1,0:T(8,128)(2,1)S(1)}, bf16[1,256,128]{2,1,0:T(8,128)(2,1)}, u32[]{:S(2)}) copy-start(bf16[1,256,128]{2,1,0:T(8,128)(2,1)} %param.17) | copy-start | bytes 196612
  0.6 42.5 %copy-start.10 = (s32[32,3]{0,1:T(4,128)S(1)}, s32[32,3]{0,1:T(4,128)}, u32[]{:S(2)}) copy-start(s32[32,3]{0,1:T(4,128)} %param.15) | copy-start | bytes 1156
  0.7 42.7 %copy-start.5 = (bf16[32,128,128]{2,1,0:T(8,128)(2,1)S(1)}, bf16[32,128,128]{2,1,0:T(8,128)(2,1)}, u32[]{:S(2)}) copy-start(bf16[32,128,128]{2,1,0:T(8,128)(2,1)} %si.1) | copy-start | bytes 3145732
  0.7 42.7 %copy-start.7 = (bf16[1,128,128]{2,1,0:T(8,128)(2,1)S(1)}, bf16[1,128,128]{2,1,0:T(8,128)(2,1)}, u32[]{:S(2)}) copy-start(bf16[1,128,128]{2,1,0:T(8,128)(2,1)} %fi.1) | copy-start | bytes 98308
  2.3 10.9 %collective-permute-start = (bf16[2,4,48,128]{3,2,1,0:T(8,128)(2,1)}, bf16[2,4,48,128]{3,2,1,0:T(8,128)(2,1)S(1)}, u32[]{:S(2)}, u32[]{:S(2)}) collective-permute-start(bf16[2,4,48,128]{3,2,1,0:T(8,128)(2,1)} %pack.1), channel_id=1, source_target_pairs={{0,4},{1,5},{2,6},{3,7},{4,0},{5,1},{6,2},{7,3},{8,12},{9,13},{10,... | collective-permute-start | bytes 294920 | tf_op jit(solution)/shard_map/ppermute | solution.py:281
  13.2 5.4 %collective-permute-start.2 = (bf16[2,4,48,128]{3,2,1,0:T(8,128)(2,1)S(1)}, bf16[2,4,48,128]{3,2,1,0:T(8,128)(2,1)S(1)}, u32[]{:S(2)}, u32[]{:S(2)}) collective-permute-start(bf16[2,4,48,128]{3,2,1,0:T(8,128)(2,1)S(1)} %get-tuple-element.34), channel_id=1, source_target_pairs={{0,3},{1,0},{2,1},{3,2},{4,7},{5,4},{6,5},{7,6},{8,11},{9,8},{10,9... | collective-permute-start | bytes 294920 | tf_op jit(solution)/shard_map/ppermute | solution.py:255
  13.9 6.3 %collective-permute-start.1 = (bf16[2,4,48,128]{3,2,1,0:T(8,128)(2,1)S(1)}, bf16[2,4,48,128]{3,2,1,0:T(8,128)(2,1)S(1)}, u32[]{:S(2)}, u32[]{:S(2)}) collective-permute-start(bf16[2,4,48,128]{3,2,1,0:T(8,128)(2,1)S(1)} %get-tuple-element.34), channel_id=1, source_target_pairs={{0,1},{1,2},{2,3},{3,0},{4,5},{5,6},{6,7},{7,4},{8,9},{9,10},{10,1... | collective-permute-start | bytes 294920 | tf_op jit(solution)/shard_map/ppermute | solution.py:255
  15.3 6.1 %collective-permute-start.3 = (bf16[2,4,48,128]{3,2,1,0:T(8,128)(2,1)S(1)}, bf16[2,4,48,128]{3,2,1,0:T(8,128)(2,1)S(1)}, u32[]{:S(2)}, u32[]{:S(2)}) collective-permute-start(bf16[2,4,48,128]{3,2,1,0:T(8,128)(2,1)S(1)} %get-tuple-element.34), channel_id=1, source_target_pairs={{0,2},{1,3},{2,0},{3,1},{4,6},{5,7},{6,4},{7,5},{8,10},{9,11},{10,... | collective-permute-start | bytes 294920 | tf_op jit(solution)/shard_map/ppermute | solution.py:255
  21.5 19.8 %collective-permute-start.6 = (bf16[4,2,4,48,128]{4,3,2,1,0:T(8,128)(2,1)S(1)}, bf16[4,2,4,48,128]{4,3,2,1,0:T(8,128)(2,1)S(1)}, u32[]{:S(2)}, u32[]{:S(2)}) collective-permute-start(bf16[4,2,4,48,128]{4,3,2,1,0:T(8,128)(2,1)S(1)} %pad_maximum_fusion.a0), channel_id=1, source_target_pairs={{0,16},{8,24},{16,0},{24,8},{1,17},{9,25},{17,1},{25,9},{2,18},{10... | collective-permute-start | bytes 1179656 | tf_op jit(solution)/shard_map/ppermute | solution.py:261
  24.8 12.8 %collective-permute-start.8 = (bf16[2,4,48,128]{3,2,1,0:T(8,128)(2,1)S(1)}, bf16[2,4,48,128]{3,2,1,0:T(8,128)(2,1)S(1)}, u32[]{:S(2)}, u32[]{:S(2)}) collective-permute-start(bf16[2,4,48,128]{3,2,1,0:T(8,128)(2,1)S(1)} %get-tuple-element.28), channel_id=1, source_target_pairs={{0,24},{8,0},{16,8},{24,16},{1,25},{9,1},{17,9},{25,17},{2,26},{10... | collective-permute-start | bytes 294920 | tf_op jit(solution)/shard_map/ppermute | solution.py:261
  26.0 11.7 %collective-permute-start.7 = (bf16[2,4,48,128]{3,2,1,0:T(8,128)(2,1)S(1)}, bf16[2,4,48,128]{3,2,1,0:T(8,128)(2,1)S(1)}, u32[]{:S(2)}, u32[]{:S(2)}) collective-permute-start(bf16[2,4,48,128]{3,2,1,0:T(8,128)(2,1)S(1)} %get-tuple-element.28), channel_id=1, source_target_pairs={{0,8},{8,16},{16,24},{24,0},{1,9},{9,17},{17,25},{25,1},{2,10},{10... | collective-permute-start | bytes 294920 | tf_op jit(solution)/shard_map/ppermute | solution.py:261
  26.9 10.7 %collective-permute-start.9 = (bf16[2,4,48,128]{3,2,1,0:T(8,128)(2,1)S(1)}, bf16[2,4,48,128]{3,2,1,0:T(8,128)(2,1)S(1)}, u32[]{:S(2)}, u32[]{:S(2)}) collective-permute-start(bf16[2,4,48,128]{3,2,1,0:T(8,128)(2,1)S(1)} %get-tuple-element.28), channel_id=1, source_target_pairs={{0,16},{8,24},{16,0},{24,8},{1,17},{9,25},{17,1},{25,9},{2,18},{10... | collective-permute-start | bytes 294920 | tf_op jit(solution)/shard_map/ppermute | solution.py:261
  27.7 28.5 %collective-permute-start.5 = (bf16[4,2,4,48,128]{4,3,2,1,0:T(8,128)(2,1)S(1)}, bf16[4,2,4,48,128]{4,3,2,1,0:T(8,128)(2,1)S(1)}, u32[]{:S(2)}, u32[]{:S(2)}) collective-permute-start(bf16[4,2,4,48,128]{4,3,2,1,0:T(8,128)(2,1)S(1)} %pad_maximum_fusion.a0), channel_id=1, source_target_pairs={{0,24},{8,0},{16,8},{24,16},{1,25},{9,1},{17,9},{25,17},{2,26},{10... | collective-permute-start | bytes 1179656 | tf_op jit(solution)/shard_map/ppermute | solution.py:261
  37.6 18.5 %collective-permute-start.4 = (bf16[4,2,4,48,128]{4,3,2,1,0:T(8,128)(2,1)S(1)}, bf16[4,2,4,48,128]{4,3,2,1,0:T(8,128)(2,1)S(1)}, u32[]{:S(2)}, u32[]{:S(2)}) collective-permute-start(bf16[4,2,4,48,128]{4,3,2,1,0:T(8,128)(2,1)S(1)} %pad_maximum_fusion.a0), channel_id=1, source_target_pairs={{0,8},{8,16},{16,24},{24,0},{1,9},{9,17},{17,25},{25,1},{2,10},{10... | collective-permute-start | bytes 1179656 | tf_op jit(solution)/shard_map/ppermute | solution.py:261
  37.7 18.4 %collective-permute-start.12 = (bf16[4,2,4,48,128]{4,3,2,1,0:T(8,128)(2,1)S(1)}, bf16[4,2,4,48,128]{4,3,2,1,0:T(8,128)(2,1)S(1)}, u32[]{:S(2)}, u32[]{:S(2)}) collective-permute-start(bf16[4,2,4,48,128]{4,3,2,1,0:T(8,128)(2,1)S(1)} %pad_maximum_fusion.1.b0), channel_id=1, source_target_pairs={{0,2},{1,3},{2,0},{3,1},{4,6},{5,7},{6,4},{7,5},{8,10},{9,11},{10,... | collective-permute-start | bytes 1179656 | tf_op jit(solution)/shard_map/ppermute | solution.py:255
  41.1 17.0 %collective-permute-start.11 = (bf16[4,2,4,48,128]{4,3,2,1,0:T(8,128)(2,1)S(1)}, bf16[4,2,4,48,128]{4,3,2,1,0:T(8,128)(2,1)}, u32[]{:S(2)}, u32[]{:S(2)}) collective-permute-start(bf16[4,2,4,48,128]{4,3,2,1,0:T(8,128)(2,1)S(1)} %pad_maximum_fusion.1.b0), channel_id=1, source_target_pairs={{0,3},{1,0},{2,1},{3,2},{4,7},{5,4},{6,5},{7,6},{8,11},{9,8},{10,9... | collective-permute-start | bytes 1179656 | tf_op jit(solution)/shard_map/ppermute | solution.py:255
  41.4 17.1 %collective-permute-start.10 = (bf16[4,2,4,48,128]{4,3,2,1,0:T(8,128)(2,1)S(1)}, bf16[4,2,4,48,128]{4,3,2,1,0:T(8,128)(2,1)}, u32[]{:S(2)}, u32[]{:S(2)}) collective-permute-start(bf16[4,2,4,48,128]{4,3,2,1,0:T(8,128)(2,1)S(1)} %pad_maximum_fusion.1.b0), channel_id=1, source_target_pairs={{0,1},{1,2},{2,3},{3,0},{4,5},{5,6},{6,7},{7,4},{8,9},{9,10},{10,1... | collective-permute-start | bytes 1179656 | tf_op jit(solution)/shard_map/ppermute | solution.py:255
  43.4 2.2 %copy-start.3 = (bf16[32,4,128,128]{3,2,1,0:T(8,128)(2,1)S(1)}, bf16[32,4,128,128]{3,2,1,0:T(8,128)(2,1)}, u32[]{:S(2)}) copy-start(bf16[32,4,128,128]{3,2,1,0:T(8,128)(2,1)} %sp.1) | copy-start | bytes 12582916
  45.6 0.9 copy-start.6
  46.5 12.0 %copy-start.8 = (s32[4096]{0:T(1024)S(1)}, s32[4096]{0:T(1024)}, u32[]{:S(2)}) copy-start(s32[4096]{0:T(1024)} %order.1) | copy-start | bytes 49156
  46.5 12.0 %copy-start.9 = (s32[1,8]{1,0:T(1,128)S(1)}, s32[1,8]{1,0:T(1,128)}, u32[]{:S(2)}) copy-start(s32[1,8]{1,0:T(1,128)} %fidx.1) | copy-start | bytes 100
  50.7 2.0 %copy-start.1 = (bf16[32,512,128]{2,1,0:T(8,128)(2,1)}, bf16[32,512,128]{2,1,0:T(8,128)(2,1)S(1)}, u32[]{:S(2)}) copy-start(bf16[32,512,128]{2,1,0:T(8,128)(2,1)S(1)} %get-tuple-element.19.su) | copy-start | bytes 12582916
  52.7 2.0 %copy-start.2 = (bf16[32,128,512]{2,1,0:T(8,128)(2,1)}, bf16[32,128,512]{2,1,0:T(8,128)(2,1)S(1)}, u32[]{:S(2)}) copy-start(bf16[32,128,512]{2,1,0:T(8,128)(2,1)S(1)} %get-tuple-element.20.sut) | copy-start | bytes 12582916
  54.7 1.4 copy-start.4

commit v2 on v1

--- a/solution.py
+++ b/solution.py
@@ -13,6 +13,8 @@
 Q = 3
 WIN = 8
 SHARD = 48
+SENT = 4 * SHARD + B
+TILES = 32
 F32 = jnp.float32
 BF = jnp.bfloat16
 REL = (0, 1, -1, 2)
@@ -34,27 +36,32 @@
     return x.astype(F32).T.astype(BF)
 
 
-def pack_kernel(pos, x_ref, o_ref):
+def pack_kernel(pos, x_ref, s_ref, o_ref):
     first = (3 * pos[0]) // 8
     for k in range(WIN):
         col = lax.rem(first + k, NA)
-        o_ref[k // 4, k % 4] = x_ref[:, pl.ds(pl.multiple_of(col * B, B), B)]
-
-
-def pack(x, me):
+        at = (k % 4) * SHARD
+        o_ref[k // 4, at:at + SHARD] = x_ref[:, pl.ds(pl.multiple_of(col * B, B), B)]
+    for h in range(2):
+        o_ref[h, 4 * SHARD:] = s_ref[0, h * B:(h + 1) * B]
+
+
+def pack(x, sens, me):
     return pl.pallas_call(
         pack_kernel,
-        out_shape=jax.ShapeDtypeStruct((2, 4, SHARD, B), BF),
+        out_shape=jax.ShapeDtypeStruct((2, SENT, B), BF),
         in_specs=[
             pl.BlockSpec(memory_space=pltpu.SMEM),
+            pl.BlockSpec(memory_space=pltpu.VMEM),
             pl.BlockSpec(memory_space=pltpu.VMEM),
         ],
         out_specs=pl.BlockSpec(memory_space=pltpu.VMEM),
         name="pack",
-    )(me.reshape(1), x)
+    )(me.reshape(1), x, sens)
 
 
 KIDS = 4
+CHUNK = 8
 
 
 def early_kernel(fp, fi, sp, si, fu, fut, fw, su, sut, sw):
@@ -106,7 +113,7 @@
         cost_estimate=pl.CostEstimate(
             flops=300 * 2 * B**3, bytes_accessed=20 * 2**20, transcendentals=0
         ),
-        compiler_params=pltpu.CompilerParams(vmem_limit_bytes=32 * 2**20),
+        compiler_params=pltpu.CompilerParams(vmem_limit_bytes=12 * 2**20),
         name="early",
     )(fp, fi, sp, si)
 
@@ -115,7 +122,7 @@
     steps, pos, fidx, spos, order,
     a0, a1, a2, a3, b0, b1, b2, b3, fu, fut, fw, su, sut, sw,
     fc_o, fd_o, sc_o, sd_o, rows_o,
-    full, tmat, cov, got,
+    full, tmat, cov, got, sens, landed, sems,
 ):
     step = pl.program_id(0)
 
@@ -123,8 +130,16 @@
     def _():
         me = pos[0]
         row, zh, x = me // 8, (me // 4) % 2, me % 4
-        for half, group in enumerate(((a0, a1, a2, a3), (b0, b1, b2, b3))):
+        copies = [
+            pltpu.make_async_copy(ref, landed.at[n], sems.at[n])
+            for n, ref in enumerate((a0, a1, a2, a3, b0, b1, b2, b3))
+        ]
+        for copy in copies:
+            copy.start()
+        for half in range(2):
             for t in range(4):
+                group = half * 4 + t
+                copies[group].wait()
                 for u in range(4):
                     dr, dx = (REL[t], REL[u]) if half == 0 else (REL[u], REL[t])
                     r = lax.rem(row - dr + 4, 4)
@@ -136,8 +151,9 @@
                         for k in range(4):
                             col = lax.rem(first + half * 4 + k, NA)
                             full[pl.ds(at, SHARD), pl.ds(pl.multiple_of(col * B, B), B)] = (
-                                group[t][u, z, k]
+                                landed[group, u, z, k * SHARD:(k + 1) * SHARD]
                             )
+                        sens[src, half * B:(half + 1) * B] = landed[group, u, z, 4 * SHARD:]
 
         def block(p, q):
             return full[
@@ -180,26 +196,37 @@
                 ws.append(w)
             d = (sw[c] - mm(sut[c], jnp.concatenate(ws, axis=0))).astype(BF)
             sd_o[c] = d
-            base = kid * 2 * B
+            base = pl.multiple_of(kid * 2 * B, 2 * B)
             cov[pl.ds(base, B, stride=2), :] = d.astype(F32)
             cov[pl.ds(base + 1, B, stride=2), :] = ws[0].astype(F32)
 
-    @pl.when(step >= steps)
+    @pl.when(step == steps)
     def _():
-        n = KIDS * B
-        base = (step - steps) * n
-
-        def body(g, carry):
-            for j in range(16):
-                src = order[base + g * 16 + j]
-                got[pl.ds(pl.multiple_of(g * 32, 32) + 2 * j, 2), :] = cov[
-                    pl.ds(pl.multiple_of(src * 2, 2), 2), :
-                ]
+        rows = CHUNK * B
+
+        def chunk(k, carry):
+            def move(g, inner):
+                for j in range(16):
+                    src = order[k * rows + g * 16 + j]
+                    got[pl.ds(pl.multiple_of(g * 32, 32) + 2 * j, 2), :] = cov[
+                        pl.ds(pl.multiple_of(src * 2, 2), 2), :
+                    ]
+                return inner
+
+            lax.fori_loop(0, rows // 16, move, 0)
+            for t in range(CHUNK):
+                line = jnp.concatenate(
+                    [
+                        got[pl.ds(t * 2 * B, B, stride=2), :],
+                        got[pl.ds(t * 2 * B + 1, B, stride=2), :],
+                    ],
+                    axis=1,
+                ).astype(BF)
+                at = pl.multiple_of((k * CHUNK + t) * B, B)
+                rows_o[pl.ds(at, B)] = mm(line, sens[k * CHUNK + t]).astype(BF)
             return carry
 
-        lax.fori_loop(0, n // 16, body, 0)
-        rows_o[:, :B] = got[pl.ds(0, n, stride=2), :].astype(BF)
-        rows_o[:, B:] = got[pl.ds(1, n, stride=2), :].astype(BF)
+        lax.fori_loop(0, TILES // CHUNK, chunk, 0)
 
 
 def late(me, fidx, spos, order, ga, gb, fu, fut, fw, su, sut, sw):
@@ -212,16 +239,16 @@
     smem = pl.BlockSpec(memory_space=pltpu.SMEM)
     return pl.pallas_call(
         functools.partial(late_kernel, steps),
-        grid=(2 * steps,),
+        grid=(steps + 1,),
         out_shape=(
             jax.ShapeDtypeStruct((1, PS, B, B), BF),
             jax.ShapeDtypeStruct((1, B, B), BF),
             jax.ShapeDtypeStruct((n, Q + 1, B, B), BF),
             jax.ShapeDtypeStruct((n, B, B), BF),
-            jax.ShapeDtypeStruct((n * B, 2 * B), BF),
+            jax.ShapeDtypeStruct((n * B, B), BF),
         ),
         in_specs=[smem] * 4
-        + [whole(4, 2, 4, SHARD, B)] * 8
+        + [pl.BlockSpec(memory_space=pl.ANY)] * 8
         + [
             whole(PS * B, B),
             whole(B, PS * B),
@@ -235,18 +262,21 @@
             whole(1, B, B),
             part(Q + 1, B, B),
             part(B, B),
-            pl.BlockSpec((KIDS * B, 2 * B), lambda i: (jnp.maximum(i - steps, 0), 0)),
+            whole(n * B, B),
         ),
         scratch_shapes=[
             pltpu.VMEM((NA * B, NA * B), BF),
             pltpu.VMEM(((PS + 1) * B, (PS + 1) * B), BF),
             pltpu.VMEM((2 * n * B, B), F32),
-            pltpu.VMEM((2 * KIDS * B, B), F32),
+            pltpu.VMEM((2 * CHUNK * B, B), F32),
+            pltpu.VMEM((TILES, 2 * B, B), BF),
+            pltpu.VMEM((8, 4, 2, SENT, B), BF),
+            pltpu.SemaphoreType.DMA((8,)),
         ],
         cost_estimate=pl.CostEstimate(
             flops=720 * 2 * B**3, bytes_accessed=20 * 2**20, transcendentals=0
         ),
-        compiler_params=pltpu.CompilerParams(vmem_limit_bytes=48 * 2**20),
+        compiler_params=pltpu.CompilerParams(vmem_limit_bytes=30 * 2**20),
         name="late",
     )(me.reshape(1), fidx, spos.reshape(-1), order, *ga, *gb, fu, fut, fw, su, sut, sw)
 
@@ -277,18 +307,20 @@
     sensitivity,
 ):
     me = (lax.axis_index("row") * 8 + lax.axis_index("col")).astype(jnp.int32)
-    mine = pack(top_covariance, me)
+    fixed = lax.optimization_barrier
+    mine = pack(top_covariance, sensitivity, me)
     other = lax.ppermute(mine, "col", [(c, (c + 4) % 8) for c in range(8)])
-    half_a = jnp.stack([mine[0], other[0]])
-    half_b = jnp.stack([mine[1], other[1]])
-    ga = spread(jnp.stack(spread(half_a, along_x)), along_row)
-    gb = spread(jnp.stack(spread(half_b, along_row)), along_x)
+    half_a, half_b = fixed((jnp.stack([mine[0], other[0]]), jnp.stack([mine[1], other[1]])))
+    near_a, near_b = fixed((spread(half_a, along_x), spread(half_b, along_row)))
+    near_a, near_b = fixed((jnp.stack(near_a), jnp.stack(near_b)))
+    ga, gb = spread(near_a, along_row), spread(near_b, along_x)
     fu, fut, fw, su, sut, sw = early(first_panel, first_inverse, second_panel, second_inverse)
-    first_cross, first_diag, second_cross, second_diag, ordered = late(
+    first_cross, first_diag, second_cross, second_diag, products = late(
         me, first_index, second_positions, row_order, ga, gb, fu, fut, fw, su, sut, sw
     )
-    received = lax.all_to_all(ordered, ("row", "col"), split_axis=0, concat_axis=0, tiled=True)
-    tile_products = jnp.dot(received, sensitivity[0], preferred_element_type=F32).astype(BF)
+    tile_products = lax.all_to_all(
+        products, ("row", "col"), split_axis=0, concat_axis=0, tiled=True
+    )
     return (first_cross, first_diag, second_cross, second_diag, tile_products)
 
 

time: 144 us -> 131 us (0.910)
  the two profiles are of different devices: /device:TPU:66 before, /device:TPU:34 now
where the time goes in v2:
time: 131 us; the launch traced here: 130 us
  blocking collectives  39.3 us (30%)
  Pallas kernels  30.3 us (23%)
  waiting for transfers between devices  29.3 us (22%)
  starting transfers between devices  25.5 us (19%)
  local copies, waits for them, and re-layouts  4.36 us (3%)
    all_to_all x1, blocking collectives, local(): lax.all_to_all(products, ('row', 'col'), split_axis=0, concat_axis=0, til...  39.3 us
    pallas_call x1, Pallas kernels, late(): pl.pallas_call(functools.partial(late_kernel, steps), grid=(steps + 1,),...  24.3 us
    ppermute x6, waiting for transfers between devices, along_row(): return lax.ppermute(v, 'row', [(r, (r + k) % 4) for r in range(4)])  18.9 us
    ppermute x6, starting transfers between devices, along_row(): return lax.ppermute(v, 'row', [(r, (r + k) % 4) for r in range(4)])  9.92 us
    ppermute x6, starting transfers between devices, along_x(): lax.ppermute(v, 'col', [(z * 4 + x, z * 4 + (x + k) % 4) for z in range(2...  9.28 us
    ppermute x1, waiting for transfers between devices, local(): other = lax.ppermute(mine, 'col', [(c, (c + 4) % 8) for c in range(8)])  6.7 us
    ppermute x1, starting transfers between devices, local(): other = lax.ppermute(mine, 'col', [(c, (c + 4) % 8) for c in range(8)])  6.29 us
    pallas_call x1, Pallas kernels, early(): pl.pallas_call(early_kernel, grid=(n // KIDS,), out_shape=(jax.ShapeDtype...  4.23 us
  transfers between devices with their start and end apart: 13, of which 9 were waited for; matrix products, arithmetic and copies ran while one was open for 1% of the time, Pallas kernels for 3%

profile of v2, /device:TPU:34, one launch (start us, length us, event | category | flops | bytes accessed | tf_op | source)
XLA Modules:
  0.0 129.7 jit_solution(8113602291553133872)
XLA Ops:
  0.6 0.0 copy-start.6
  0.6 0.0 copy-start.1
  0.7 0.0 copy-start.3
  0.7 0.0 copy-start.2
  0.7 1.7 %pack.1 = bf16[2,320,128]{2,1,0:T(8,128)(2,1)} custom-call(s32[1]{0:T(128)} %bitcast.pos, bf16[48,1536]{1,0:T(8,128)(2,1)} %x_ref.1, bf16[1,256,128]{2,1,0:T(8,128)(2,1)} %s_ref.1), custom_call_target="tpu_custom_call" | custom-call | tf_op jit(solution)/shard_map/pack/pallas_call | solution.py:50
  2.4 6.3 %collective-permute-start = (bf16[2,320,128]{2,1,0:T(8,128)(2,1)}, bf16[2,320,128]{2,1,0:T(8,128)(2,1)S(1)}, u32[]{:S(2)}, u32[]{:S(2)}) collective-permute-start(bf16[2,320,128]{2,1,0:T(8,128)(2,1)} %pack.1), channel_id=1, source_target_pairs={{0,4},{1,5},{2,6},{3,7},{4,0},{5,1},{6,2},{7,3},{8,12},{9,13},{10,... | collective-permute-start | bytes 491528 | tf_op jit(solution)/shard_map/ppermute | solution.py:312
  8.7 1.0 fusion
  9.7 6.7 %collective-permute-done = bf16[2,320,128]{2,1,0:T(8,128)(2,1)S(1)} collective-permute-done((bf16[2,320,128]{2,1,0:T(8,128)(2,1)}, bf16[2,320,128]{2,1,0:T(8,128)(2,1)S(1)}, u32[]{:S(2)}, u32[]{:S(2)}) %collective-permute-start) | collective-permute-done | bytes 163872 | tf_op jit(solution)/shard_map/ppermute | solution.py:312
  16.4 0.0 copy-start.4
  16.4 0.0 copy-start.5
  16.4 2.2 %collective-permute-start.3 = (bf16[2,320,128]{2,1,0:T(8,128)(2,1)S(1)}, bf16[2,320,128]{2,1,0:T(8,128)(2,1)S(1)}, u32[]{:S(2)}, u32[]{:S(2)}) collective-permute-start(bf16[2,320,128]{2,1,0:T(8,128)(2,1)S(1)} %get-tuple-element.30), channel_id=1, source_target_pairs={{0,2},{1,3},{2,0},{3,1},{4,6},{5,7},{6,4},{7,5},{8,10},{9,11},{10,... | collective-permute-start | bytes 491528 | tf_op jit(solution)/shard_map/ppermute | solution.py:285
  18.6 1.4 %collective-permute-start.2 = (bf16[2,320,128]{2,1,0:T(8,128)(2,1)S(1)}, bf16[2,320,128]{2,1,0:T(8,128)(2,1)S(1)}, u32[]{:S(2)}, u32[]{:S(2)}) collective-permute-start(bf16[2,320,128]{2,1,0:T(8,128)(2,1)S(1)} %get-tuple-element.30), channel_id=1, source_target_pairs={{0,3},{1,0},{2,1},{3,2},{4,7},{5,4},{6,5},{7,6},{8,11},{9,8},{10,9... | collective-permute-start | bytes 491528 | tf_op jit(solution)/shard_map/ppermute | solution.py:285
  20.1 0.6 collective-permute-start.1
  20.7 3.2 %collective-permute-start.6 = (bf16[2,320,128]{2,1,0:T(8,128)(2,1)S(1)}, bf16[2,320,128]{2,1,0:T(8,128)(2,1)S(1)}, u32[]{:S(2)}, u32[]{:S(2)}) collective-permute-start(bf16[2,320,128]{2,1,0:T(8,128)(2,1)S(1)} %get-tuple-element.34), channel_id=1, source_target_pairs={{0,16},{8,24},{16,0},{24,8},{1,17},{9,25},{17,1},{25,9},{2,18},{10... | collective-permute-start | bytes 491528 | tf_op jit(solution)/shard_map/ppermute | solution.py:291
  23.9 1.1 collective-permute-start.5
  24.9 0.1 collective-permute-done.3
  25.0 1.6 %collective-permute-start.4 = (bf16[2,320,128]{2,1,0:T(8,128)(2,1)S(1)}, bf16[2,320,128]{2,1,0:T(8,128)(2,1)S(1)}, u32[]{:S(2)}, u32[]{:S(2)}) collective-permute-start(bf16[2,320,128]{2,1,0:T(8,128)(2,1)S(1)} %get-tuple-element.34), channel_id=1, source_target_pairs={{0,8},{8,16},{16,24},{24,0},{1,9},{9,17},{17,25},{25,1},{2,10},{10... | collective-permute-start | bytes 491528 | tf_op jit(solution)/shard_map/ppermute | solution.py:291
  26.6 0.2 collective-permute-done.2
  26.8 0.0 collective-permute-done.1
  26.8 1.7 %collective-permute-done.6 = bf16[2,320,128]{2,1,0:T(8,128)(2,1)S(1)} collective-permute-done((bf16[2,320,128]{2,1,0:T(8,128)(2,1)S(1)}, bf16[2,320,128]{2,1,0:T(8,128)(2,1)S(1)}, u32[]{:S(2)}, u32[]{:S(2)}) %collective-permute-start.6) | collective-permute-done | bytes 163872 | tf_op jit(solution)/shard_map/ppermute | solution.py:291
  28.5 1.9 %collective-permute-done.5 = bf16[2,320,128]{2,1,0:T(8,128)(2,1)S(1)} collective-permute-done((bf16[2,320,128]{2,1,0:T(8,128)(2,1)S(1)}, bf16[2,320,128]{2,1,0:T(8,128)(2,1)S(1)}, u32[]{:S(2)}, u32[]{:S(2)}) %collective-permute-start.5) | collective-permute-done | bytes 163872 | tf_op jit(solution)/shard_map/ppermute | solution.py:291
  30.4 1.1 collective-permute-done.4
  31.6 0.1 pad_maximum_fusion.a0
  31.6 0.1 pad_maximum_fusion.1.b0
  31.7 2.1 %collective-permute-start.9 = (bf16[4,2,320,128]{3,2,1,0:T(8,128)(2,1)S(1)}, bf16[4,2,320,128]{3,2,1,0:T(8,128)(2,1)S(1)}, u32[]{:S(2)}, u32[]{:S(2)}) collective-permute-start(bf16[4,2,320,128]{3,2,1,0:T(8,128)(2,1)S(1)} %pad_maximum_fusion.a0), channel_id=1, source_target_pairs={{0,16},{8,24},{16,0},{24,8},{1,17},{9,25},{17,1},{25,9},{2,18},{10... | collective-permute-start | bytes 1966088 | tf_op jit(solution)/shard_map/ppermute | solution.py:291
  33.8 1.1 collective-permute-start.8
  34.9 1.0 collective-permute-start.7
  35.8 2.4 %collective-permute-start.12 = (bf16[4,2,320,128]{3,2,1,0:T(8,128)(2,1)S(1)}, bf16[4,2,320,128]{3,2,1,0:T(8,128)(2,1)}, u32[]{:S(2)}, u32[]{:S(2)}) collective-permute-start(bf16[4,2,320,128]{3,2,1,0:T(8,128)(2,1)S(1)} %pad_maximum_fusion.1.b0), channel_id=1, source_target_pairs={{0,2},{1,3},{2,0},{3,1},{4,6},{5,7},{6,4},{7,5},{8,10},{9,11},{10,... | collective-permute-start | bytes 1966088 | tf_op jit(solution)/shard_map/ppermute | solution.py:285
  38.2 1.2 collective-permute-start.11
  39.4 11.7 %collective-permute-done.9.a3 = bf16[4,2,320,128]{3,2,1,0:T(8,128)(2,1)S(1)} collective-permute-done((bf16[4,2,320,128]{3,2,1,0:T(8,128)(2,1)S(1)}, bf16[4,2,320,128]{3,2,1,0:T(8,128)(2,1)S(1)}, u32[]{:S(2)}, u32[]{:S(2)}) %collective-permute-start.9) | collective-permute-done | bytes 655392 | tf_op jit(solution)/shard_map/ppermute | solution.py:291
  51.0 1.5 %collective-permute-start.10 = (bf16[4,2,320,128]{3,2,1,0:T(8,128)(2,1)S(1)}, bf16[4,2,320,128]{3,2,1,0:T(8,128)(2,1)}, u32[]{:S(2)}, u32[]{:S(2)}) collective-permute-start(bf16[4,2,320,128]{3,2,1,0:T(8,128)(2,1)S(1)} %pad_maximum_fusion.1.b0), channel_id=1, source_target_pairs={{0,1},{1,2},{2,3},{3,0},{4,5},{5,6},{6,7},{7,4},{8,9},{9,10},{10,1... | collective-permute-start | bytes 1966088 | tf_op jit(solution)/shard_map/ppermute | solution.py:285
  52.5 0.0 copy-done.6
  52.5 0.1 copy.15
  52.6 0.1 reshape.20.spos
  52.7 0.0 copy-done.1
  52.7 0.0 copy-done.3
  52.8 0.0 copy-done.2
  52.8 0.0 copy-start
  52.8 2.2 %copy-done = bf16[32,4,128,128]{3,2,1,0:T(8,128)(2,1)S(1)} copy-done((bf16[32,4,128,128]{3,2,1,0:T(8,128)(2,1)S(1)}, bf16[32,4,128,128]{3,2,1,0:T(8,128)(2,1)}, u32[]{:S(2)}) %copy-start) | copy-done | bytes 4194328
  55.0 4.2 %early.1 = (bf16[1024,128]{1,0:T(8,128)(2,1)S(1)}, bf16[128,1024]{1,0:T(8,128)(2,1)S(1)}, f32[128,128]{1,0:T(8,128)S(1)}, bf16[32,512,128]{2,1,0:T(8,128)(2,1)S(...) custom-call(bf16[1,8,128,128]{3,2,1,0:T(8,128)(2,1)S(1)} %copy-done.2, ...), custom_call_target="tpu_custom_call" | custom-call | flops 1258291200 | bytes 20971520 | tf_op jit(solution)/shard_map/early/pallas_call | solution.py:88
  59.2 2.5 %collective-permute-done.8.a2 = bf16[4,2,320,128]{3,2,1,0:T(8,128)(2,1)} collective-permute-done((bf16[4,2,320,128]{3,2,1,0:T(8,128)(2,1)S(1)}, bf16[4,2,320,128]{3,2,1,0:T(8,128)(2,1)}, u32[]{:S(2)}, u32[]{:S(2)}) %collective-permute-start.8) | collective-permute-done | bytes 655392 | tf_op jit(solution)/shard_map/ppermute | solution.py:291
  61.7 0.0 collective-permute-done.7.a1
  61.7 0.0 collective-permute-done.12.b3
  61.7 3.4 %collective-permute-done.11.b2 = bf16[4,2,320,128]{3,2,1,0:T(8,128)(2,1)} collective-permute-done((bf16[4,2,320,128]{3,2,1,0:T(8,128)(2,1)S(1)}, bf16[4,2,320,128]{3,2,1,0:T(8,128)(2,1)}, u32[]{:S(2)}, u32[]{:S(2)}) %collective-permute-start.11) | collective-permute-done | bytes 655392 | tf_op jit(solution)/shard_map/ppermute | solution.py:285
  65.0 0.0 collective-permute-done.10.b1
  65.1 24.3 %late.1 = (bf16[1,8,128,128]{3,2,1,0:T(8,128)(2,1)}, bf16[1,128,128]{2,1,0:T(8,128)(2,1)}, bf16[32,4,128,128]{3,2,1,0:T(8,128)(2,1)}, bf16[32,128,128]{2,1,0:T(8,128)(2,1)}, bf16[4096,128]{1,0:T(8,128)(2,1)S(1)}) custom-call(s32[1]{0:T(128)} %bitcast.pos, s32[1,8]{1,0:T(1,128)S(1)} %copy-done.5, s32[96]{0:T(128)S(1)} %reshape.20.spos, s32[4096]{0:T(1024)S(1)} %copy-done.4, ...), custom_call_target="tpu_custom_call" | custom-call | flops 3019898880 | bytes 20971520 | tf_op jit(solution)/shard_map/late/pallas_call | solution.py:240
  89.4 39.3 %all_to_all.12 = bf16[32,128,128]{2,1,0:T(8,128)(2,1)S(1)} all-to-all(bf16[32,128,128]{2,1,0:T(8,128)(2,1)S(1)} %bitcast.11), channel_id=1, replica_groups=mesh['grp'=8,'row'=4,'col'=8] {'row','col'}, dimensions={0} | all-to-all | bytes 2097152 | tf_op jit(solution)/shard_map/all_to_all | solution.py:321
  128.7 1.0 copy.17
  (4 shorter events, 0.0 us)
Async XLA Ops:
  0.6 51.9 %copy-start.6 = (s32[32,3]{0,1:T(4,128)S(1)}, s32[32,3]{0,1:T(4,128)}, u32[]{:S(2)}) copy-start(s32[32,3]{0,1:T(4,128)} %param.15) | copy-start | bytes 1156
  0.6 52.1 %copy-start.1 = (bf16[32,128,128]{2,1,0:T(8,128)(2,1)S(1)}, bf16[32,128,128]{2,1,0:T(8,128)(2,1)}, u32[]{:S(2)}) copy-start(bf16[32,128,128]{2,1,0:T(8,128)(2,1)} %si.1) | copy-start | bytes 3145732
  0.7 52.1 %copy-start.3 = (bf16[1,128,128]{2,1,0:T(8,128)(2,1)S(1)}, bf16[1,128,128]{2,1,0:T(8,128)(2,1)}, u32[]{:S(2)}) copy-start(bf16[1,128,128]{2,1,0:T(8,128)(2,1)} %fi.1) | copy-start | bytes 98308
  0.7 52.1 %copy-start.2 = (bf16[1,8,128,128]{3,2,1,0:T(8,128)(2,1)S(1)}, bf16[1,8,128,128]{3,2,1,0:T(8,128)(2,1)}, u32[]{:S(2)}) copy-start(bf16[1,8,128,128]{3,2,1,0:T(8,128)(2,1)} %fp.1) | copy-start | bytes 786436
  2.4 14.0 %collective-permute-start = (bf16[2,320,128]{2,1,0:T(8,128)(2,1)}, bf16[2,320,128]{2,1,0:T(8,128)(2,1)S(1)}, u32[]{:S(2)}, u32[]{:S(2)}) collective-permute-start(bf16[2,320,128]{2,1,0:T(8,128)(2,1)} %pack.1), channel_id=1, source_target_pairs={{0,4},{1,5},{2,6},{3,7},{4,0},{5,1},{6,2},{7,3},{8,12},{9,13},{10,... | collective-permute-start | bytes 491528 | tf_op jit(solution)/shard_map/ppermute | solution.py:312
  16.4 48.6 %copy-start.4 = (s32[4096]{0:T(1024)S(1)}, s32[4096]{0:T(1024)}, u32[]{:S(2)}) copy-start(s32[4096]{0:T(1024)} %order.1) | copy-start | bytes 49156
  16.4 48.6 %copy-start.5 = (s32[1,8]{1,0:T(1,128)S(1)}, s32[1,8]{1,0:T(1,128)}, u32[]{:S(2)}) copy-start(s32[1,8]{1,0:T(1,128)} %fidx.1) | copy-start | bytes 100
  16.4 8.6 %collective-permute-start.3 = (bf16[2,320,128]{2,1,0:T(8,128)(2,1)S(1)}, bf16[2,320,128]{2,1,0:T(8,128)(2,1)S(1)}, u32[]{:S(2)}, u32[]{:S(2)}) collective-permute-start(bf16[2,320,128]{2,1,0:T(8,128)(2,1)S(1)} %get-tuple-element.30), channel_id=1, source_target_pairs={{0,2},{1,3},{2,0},{3,1},{4,6},{5,7},{6,4},{7,5},{8,10},{9,11},{10,... | collective-permute-start | bytes 491528 | tf_op jit(solution)/shard_map/ppermute | solution.py:285
  18.6 8.1 %collective-permute-start.2 = (bf16[2,320,128]{2,1,0:T(8,128)(2,1)S(1)}, bf16[2,320,128]{2,1,0:T(8,128)(2,1)S(1)}, u32[]{:S(2)}, u32[]{:S(2)}) collective-permute-start(bf16[2,320,128]{2,1,0:T(8,128)(2,1)S(1)} %get-tuple-element.30), channel_id=1, source_target_pairs={{0,3},{1,0},{2,1},{3,2},{4,7},{5,4},{6,5},{7,6},{8,11},{9,8},{10,9... | collective-permute-start | bytes 491528 | tf_op jit(solution)/shard_map/ppermute | solution.py:285
  20.1 6.7 %collective-permute-start.1 = (bf16[2,320,128]{2,1,0:T(8,128)(2,1)S(1)}, bf16[2,320,128]{2,1,0:T(8,128)(2,1)S(1)}, u32[]{:S(2)}, u32[]{:S(2)}) collective-permute-start(bf16[2,320,128]{2,1,0:T(8,128)(2,1)S(1)} %get-tuple-element.30), channel_id=1, source_target_pairs={{0,1},{1,2},{2,3},{3,0},{4,5},{5,6},{6,7},{7,4},{8,9},{9,10},{10,1... | collective-permute-start | bytes 491528 | tf_op jit(solution)/shard_map/ppermute | solution.py:285
  20.7 7.9 %collective-permute-start.6 = (bf16[2,320,128]{2,1,0:T(8,128)(2,1)S(1)}, bf16[2,320,128]{2,1,0:T(8,128)(2,1)S(1)}, u32[]{:S(2)}, u32[]{:S(2)}) collective-permute-start(bf16[2,320,128]{2,1,0:T(8,128)(2,1)S(1)} %get-tuple-element.34), channel_id=1, source_target_pairs={{0,16},{8,24},{16,0},{24,8},{1,17},{9,25},{17,1},{25,9},{2,18},{10... | collective-permute-start | bytes 491528 | tf_op jit(solution)/shard_map/ppermute | solution.py:291
  23.9 6.6 %collective-permute-start.5 = (bf16[2,320,128]{2,1,0:T(8,128)(2,1)S(1)}, bf16[2,320,128]{2,1,0:T(8,128)(2,1)S(1)}, u32[]{:S(2)}, u32[]{:S(2)}) collective-permute-start(bf16[2,320,128]{2,1,0:T(8,128)(2,1)S(1)} %get-tuple-element.34), channel_id=1, source_target_pairs={{0,24},{8,0},{16,8},{24,16},{1,25},{9,1},{17,9},{25,17},{2,26},{10... | collective-permute-start | bytes 491528 | tf_op jit(solution)/shard_map/ppermute | solution.py:291
  25.0 6.5 %collective-permute-start.4 = (bf16[2,320,128]{2,1,0:T(8,128)(2,1)S(1)}, bf16[2,320,128]{2,1,0:T(8,128)(2,1)S(1)}, u32[]{:S(2)}, u32[]{:S(2)}) collective-permute-start(bf16[2,320,128]{2,1,0:T(8,128)(2,1)S(1)} %get-tuple-element.34), channel_id=1, source_target_pairs={{0,8},{8,16},{16,24},{24,0},{1,9},{9,17},{17,25},{25,1},{2,10},{10... | collective-permute-start | bytes 491528 | tf_op jit(solution)/shard_map/ppermute | solution.py:291
  31.7 19.3 %collective-permute-start.9 = (bf16[4,2,320,128]{3,2,1,0:T(8,128)(2,1)S(1)}, bf16[4,2,320,128]{3,2,1,0:T(8,128)(2,1)S(1)}, u32[]{:S(2)}, u32[]{:S(2)}) collective-permute-start(bf16[4,2,320,128]{3,2,1,0:T(8,128)(2,1)S(1)} %pad_maximum_fusion.a0), channel_id=1, source_target_pairs={{0,16},{8,24},{16,0},{24,8},{1,17},{9,25},{17,1},{25,9},{2,18},{10... | collective-permute-start | bytes 1966088 | tf_op jit(solution)/shard_map/ppermute | solution.py:291
  33.8 27.9 %collective-permute-start.8 = (bf16[4,2,320,128]{3,2,1,0:T(8,128)(2,1)S(1)}, bf16[4,2,320,128]{3,2,1,0:T(8,128)(2,1)}, u32[]{:S(2)}, u32[]{:S(2)}) collective-permute-start(bf16[4,2,320,128]{3,2,1,0:T(8,128)(2,1)S(1)} %pad_maximum_fusion.a0), channel_id=1, source_target_pairs={{0,24},{8,0},{16,8},{24,16},{1,25},{9,1},{17,9},{25,17},{2,26},{10... | collective-permute-start | bytes 1966088 | tf_op jit(solution)/shard_map/ppermute | solution.py:291
  34.9 26.8 %collective-permute-start.7 = (bf16[4,2,320,128]{3,2,1,0:T(8,128)(2,1)S(1)}, bf16[4,2,320,128]{3,2,1,0:T(8,128)(2,1)}, u32[]{:S(2)}, u32[]{:S(2)}) collective-permute-start(bf16[4,2,320,128]{3,2,1,0:T(8,128)(2,1)S(1)} %pad_maximum_fusion.a0), channel_id=1, source_target_pairs={{0,8},{8,16},{16,24},{24,0},{1,9},{9,17},{17,25},{25,1},{2,10},{10... | collective-permute-start | bytes 1966088 | tf_op jit(solution)/shard_map/ppermute | solution.py:291
  35.8 25.8 %collective-permute-start.12 = (bf16[4,2,320,128]{3,2,1,0:T(8,128)(2,1)S(1)}, bf16[4,2,320,128]{3,2,1,0:T(8,128)(2,1)}, u32[]{:S(2)}, u32[]{:S(2)}) collective-permute-start(bf16[4,2,320,128]{3,2,1,0:T(8,128)(2,1)S(1)} %pad_maximum_fusion.1.b0), channel_id=1, source_target_pairs={{0,2},{1,3},{2,0},{3,1},{4,6},{5,7},{6,4},{7,5},{8,10},{9,11},{10,... | collective-permute-start | bytes 1966088 | tf_op jit(solution)/shard_map/ppermute | solution.py:285
  38.2 26.9 %collective-permute-start.11 = (bf16[4,2,320,128]{3,2,1,0:T(8,128)(2,1)S(1)}, bf16[4,2,320,128]{3,2,1,0:T(8,128)(2,1)}, u32[]{:S(2)}, u32[]{:S(2)}) collective-permute-start(bf16[4,2,320,128]{3,2,1,0:T(8,128)(2,1)S(1)} %pad_maximum_fusion.1.b0), channel_id=1, source_target_pairs={{0,3},{1,0},{2,1},{3,2},{4,7},{5,4},{6,5},{7,6},{8,11},{9,8},{10,9... | collective-permute-start | bytes 1966088 | tf_op jit(solution)/shard_map/ppermute | solution.py:285
  51.0 14.0 %collective-permute-start.10 = (bf16[4,2,320,128]{3,2,1,0:T(8,128)(2,1)S(1)}, bf16[4,2,320,128]{3,2,1,0:T(8,128)(2,1)}, u32[]{:S(2)}, u32[]{:S(2)}) collective-permute-start(bf16[4,2,320,128]{3,2,1,0:T(8,128)(2,1)S(1)} %pad_maximum_fusion.1.b0), channel_id=1, source_target_pairs={{0,1},{1,2},{2,3},{3,0},{4,5},{5,6},{6,7},{7,4},{8,9},{9,10},{10,1... | collective-permute-start | bytes 1966088 | tf_op jit(solution)/shard_map/ppermute | solution.py:285
  52.8 2.2 %copy-start = (bf16[32,4,128,128]{3,2,1,0:T(8,128)(2,1)S(1)}, bf16[32,4,128,128]{3,2,1,0:T(8,128)(2,1)}, u32[]{:S(2)}) copy-start(bf16[32,4,128,128]{3,2,1,0:T(8,128)(2,1)} %sp.1) | copy-start | bytes 12582916

commit v3 on v2

--- a/solution.py
+++ b/solution.py
@@ -60,8 +60,7 @@
     )(me.reshape(1), x, sens)
 
 
-KIDS = 4
-CHUNK = 8
+KIDS = 8
 
 
 def early_kernel(fp, fi, sp, si, fu, fut, fw, su, sut, sw):
@@ -122,7 +121,7 @@
     steps, pos, fidx, spos, order,
     a0, a1, a2, a3, b0, b1, b2, b3, fu, fut, fw, su, sut, sw,
     fc_o, fd_o, sc_o, sd_o, rows_o,
-    full, tmat, cov, got, sens, landed, sems,
+    full, tmat, cov, even, odd, sens, landed, sems,
 ):
     step = pl.program_id(0)
 
@@ -187,46 +186,40 @@
             kid = step * KIDS + c
             at = [0] + [(1 + spos[kid * Q + q]) * B for q in range(Q)]
             at = [pl.ds(pl.multiple_of(v, B), B) for v in at]
-            u = su[c]
-            ws = []
             for r in range(Q + 1):
                 line = jnp.concatenate([tmat[at[r], at[q]] for q in range(Q + 1)], axis=1)
-                w = (-mm(line, u)).astype(BF)
-                sc_o[c, r] = w
-                ws.append(w)
-            d = (sw[c] - mm(sut[c], jnp.concatenate(ws, axis=0))).astype(BF)
+                sc_o[c, r] = (-mm(line, su[c])).astype(BF)
+        for c in range(KIDS):
+            w = sc_o[c].reshape((Q + 1) * B, B)
+            d = (sw[c] - mm(sut[c], w)).astype(BF)
             sd_o[c] = d
-            base = pl.multiple_of(kid * 2 * B, 2 * B)
+            base = pl.multiple_of((step * KIDS + c) * 2 * B, 2 * B)
             cov[pl.ds(base, B, stride=2), :] = d.astype(F32)
-            cov[pl.ds(base + 1, B, stride=2), :] = ws[0].astype(F32)
+            cov[pl.ds(base + 1, B, stride=2), :] = w[:B].astype(F32)
 
     @pl.when(step == steps)
     def _():
-        rows = CHUNK * B
-
-        def chunk(k, carry):
-            def move(g, inner):
-                for j in range(16):
-                    src = order[k * rows + g * 16 + j]
-                    got[pl.ds(pl.multiple_of(g * 32, 32) + 2 * j, 2), :] = cov[
-                        pl.ds(pl.multiple_of(src * 2, 2), 2), :
-                    ]
-                return inner
-
-            lax.fori_loop(0, rows // 16, move, 0)
-            for t in range(CHUNK):
-                line = jnp.concatenate(
-                    [
-                        got[pl.ds(t * 2 * B, B, stride=2), :],
-                        got[pl.ds(t * 2 * B + 1, B, stride=2), :],
-                    ],
-                    axis=1,
-                ).astype(BF)
-                at = pl.multiple_of((k * CHUNK + t) * B, B)
-                rows_o[pl.ds(at, B)] = mm(line, sens[k * CHUNK + t]).astype(BF)
+        def move(t, got):
+            for m in range(B):
+                src = order[t * B + m]
+                got[2 * m:2 * m + 2, :] = cov[pl.ds(pl.multiple_of(src * 2, 2), 2), :]
+
+        def product(t, got):
+            line = jnp.concatenate(
+                [got[pl.ds(0, B, stride=2), :], got[pl.ds(1, B, stride=2), :]], axis=1
+            ).astype(BF)
+            rows_o[pl.ds(pl.multiple_of(t * B, B), B)] = mm(line, sens[t]).astype(BF)
+
+        move(0, even)
+
+        def pair(i, carry):
+            move(2 * i + 1, odd)
+            product(2 * i, even)
+            move(jnp.minimum(2 * i + 2, TILES - 1), even)
+            product(2 * i + 1, odd)
             return carry
 
-        lax.fori_loop(0, TILES // CHUNK, chunk, 0)
+        lax.fori_loop(0, TILES // 2, pair, 0)
 
 
 def late(me, fidx, spos, order, ga, gb, fu, fut, fw, su, sut, sw):
@@ -268,7 +261,8 @@
             pltpu.VMEM((NA * B, NA * B), BF),
             pltpu.VMEM(((PS + 1) * B, (PS + 1) * B), BF),
             pltpu.VMEM((2 * n * B, B), F32),
-            pltpu.VMEM((2 * CHUNK * B, B), F32),
+            pltpu.VMEM((2 * B, B), F32),
+            pltpu.VMEM((2 * B, B), F32),
             pltpu.VMEM((TILES, 2 * B, B), BF),
             pltpu.VMEM((8, 4, 2, SENT, B), BF),
             pltpu.SemaphoreType.DMA((8,)),

time: 131 us -> 126 us (0.962)
  Pallas kernels: 30.3 us -> 24.4 us
    pallas_call x1, Pallas kernels: 24.3 us -> 19 us  [late(): pl.pallas_call(functools.partial(late_kernel, steps), grid=(steps + 1,),...]
where the time goes in v3:
time: 126 us; the launch traced here: 124 us
  blocking collectives  39 us (31%)
  waiting for transfers between devices  29.8 us (24%)
  starting transfers between devices  25.5 us (20%)
  Pallas kernels  24.4 us (19%)
  local copies, waits for them, and re-layouts  4.36 us (3%)
    all_to_all x1, blocking collectives, local(): lax.all_to_all(products, ('row', 'col'), split_axis=0, concat_axis=0, til...  39 us
    ppermute x6, waiting for transfers between devices, along_row(): return lax.ppermute(v, 'row', [(r, (r + k) % 4) for r in range(4)])  19.5 us
    pallas_call x1, Pallas kernels, late(): pl.pallas_call(functools.partial(late_kernel, steps), grid=(steps + 1,),...  19 us
    ppermute x6, starting transfers between devices, along_row(): return lax.ppermute(v, 'row', [(r, (r + k) % 4) for r in range(4)])  9.92 us
    ppermute x6, starting transfers between devices, along_x(): lax.ppermute(v, 'col', [(z * 4 + x, z * 4 + (x + k) % 4) for z in range(2...  9.28 us
    ppermute x1, waiting for transfers between devices, local(): other = lax.ppermute(mine, 'col', [(c, (c + 4) % 8) for c in range(8)])  6.7 us
    ppermute x1, starting transfers between devices, local(): other = lax.ppermute(mine, 'col', [(c, (c + 4) % 8) for c in range(8)])  6.29 us
    ppermute x6, waiting for transfers between devices, along_x(): lax.ppermute(v, 'col', [(z * 4 + x, z * 4 + (x + k) % 4) for z in range(2...  3.69 us
  transfers between devices with their start and end apart: 13, of which 9 were waited for; matrix products, arithmetic and copies ran while one was open for 1% of the time, Pallas kernels for 3%

profile of v3, /device:TPU:34, one launch (start us, length us, event | category | flops | bytes accessed | tf_op | source)
XLA Modules:
  0.0 124.1 jit_solution(16919029096931285027)
XLA Ops:
  0.6 0.0 copy-start.6
  0.6 0.0 copy-start.1
  0.7 0.0 copy-start.3
  0.7 0.0 copy-start.2
  0.7 1.7 %pack.1 = bf16[2,320,128]{2,1,0:T(8,128)(2,1)} custom-call(s32[1]{0:T(128)} %bitcast.pos, bf16[48,1536]{1,0:T(8,128)(2,1)} %x_ref.1, bf16[1,256,128]{2,1,0:T(8,128)(2,1)} %s_ref.1), custom_call_target="tpu_custom_call" | custom-call | tf_op jit(solution)/shard_map/pack/pallas_call | solution.py:50
  2.4 6.3 %collective-permute-start = (bf16[2,320,128]{2,1,0:T(8,128)(2,1)}, bf16[2,320,128]{2,1,0:T(8,128)(2,1)S(1)}, u32[]{:S(2)}, u32[]{:S(2)}) collective-permute-start(bf16[2,320,128]{2,1,0:T(8,128)(2,1)} %pack.1), channel_id=1, source_target_pairs={{0,4},{1,5},{2,6},{3,7},{4,0},{5,1},{6,2},{7,3},{8,12},{9,13},{10,... | collective-permute-start | bytes 491528 | tf_op jit(solution)/shard_map/ppermute | solution.py:306
  8.7 1.0 fusion
  9.7 6.7 %collective-permute-done = bf16[2,320,128]{2,1,0:T(8,128)(2,1)S(1)} collective-permute-done((bf16[2,320,128]{2,1,0:T(8,128)(2,1)}, bf16[2,320,128]{2,1,0:T(8,128)(2,1)S(1)}, u32[]{:S(2)}, u32[]{:S(2)}) %collective-permute-start) | collective-permute-done | bytes 163872 | tf_op jit(solution)/shard_map/ppermute | solution.py:306
  16.4 0.0 copy-start.4
  16.4 0.0 copy-start.5
  16.4 2.2 %collective-permute-start.3 = (bf16[2,320,128]{2,1,0:T(8,128)(2,1)S(1)}, bf16[2,320,128]{2,1,0:T(8,128)(2,1)S(1)}, u32[]{:S(2)}, u32[]{:S(2)}) collective-permute-start(bf16[2,320,128]{2,1,0:T(8,128)(2,1)S(1)} %get-tuple-element.30), channel_id=1, source_target_pairs={{0,2},{1,3},{2,0},{3,1},{4,6},{5,7},{6,4},{7,5},{8,10},{9,11},{10,... | collective-permute-start | bytes 491528 | tf_op jit(solution)/shard_map/ppermute | solution.py:279
  18.6 1.4 %collective-permute-start.2 = (bf16[2,320,128]{2,1,0:T(8,128)(2,1)S(1)}, bf16[2,320,128]{2,1,0:T(8,128)(2,1)S(1)}, u32[]{:S(2)}, u32[]{:S(2)}) collective-permute-start(bf16[2,320,128]{2,1,0:T(8,128)(2,1)S(1)} %get-tuple-element.30), channel_id=1, source_target_pairs={{0,3},{1,0},{2,1},{3,2},{4,7},{5,4},{6,5},{7,6},{8,11},{9,8},{10,9... | collective-permute-start | bytes 491528 | tf_op jit(solution)/shard_map/ppermute | solution.py:279
  20.1 0.6 collective-permute-start.1
  20.7 3.2 %collective-permute-start.6 = (bf16[2,320,128]{2,1,0:T(8,128)(2,1)S(1)}, bf16[2,320,128]{2,1,0:T(8,128)(2,1)S(1)}, u32[]{:S(2)}, u32[]{:S(2)}) collective-permute-start(bf16[2,320,128]{2,1,0:T(8,128)(2,1)S(1)} %get-tuple-element.34), channel_id=1, source_target_pairs={{0,16},{8,24},{16,0},{24,8},{1,17},{9,25},{17,1},{25,9},{2,18},{10... | collective-permute-start | bytes 491528 | tf_op jit(solution)/shard_map/ppermute | solution.py:285
  23.9 1.1 collective-permute-start.5
  24.9 0.1 collective-permute-done.3
  25.0 1.6 %collective-permute-start.4 = (bf16[2,320,128]{2,1,0:T(8,128)(2,1)S(1)}, bf16[2,320,128]{2,1,0:T(8,128)(2,1)S(1)}, u32[]{:S(2)}, u32[]{:S(2)}) collective-permute-start(bf16[2,320,128]{2,1,0:T(8,128)(2,1)S(1)} %get-tuple-element.34), channel_id=1, source_target_pairs={{0,8},{8,16},{16,24},{24,0},{1,9},{9,17},{17,25},{25,1},{2,10},{10... | collective-permute-start | bytes 491528 | tf_op jit(solution)/shard_map/ppermute | solution.py:285
  26.6 0.2 collective-permute-done.2
  26.8 0.0 collective-permute-done.1
  26.8 1.7 %collective-permute-done.6 = bf16[2,320,128]{2,1,0:T(8,128)(2,1)S(1)} collective-permute-done((bf16[2,320,128]{2,1,0:T(8,128)(2,1)S(1)}, bf16[2,320,128]{2,1,0:T(8,128)(2,1)S(1)}, u32[]{:S(2)}, u32[]{:S(2)}) %collective-permute-start.6) | collective-permute-done | bytes 163872 | tf_op jit(solution)/shard_map/ppermute | solution.py:285
  28.5 1.9 %collective-permute-done.5 = bf16[2,320,128]{2,1,0:T(8,128)(2,1)S(1)} collective-permute-done((bf16[2,320,128]{2,1,0:T(8,128)(2,1)S(1)}, bf16[2,320,128]{2,1,0:T(8,128)(2,1)S(1)}, u32[]{:S(2)}, u32[]{:S(2)}) %collective-permute-start.5) | collective-permute-done | bytes 163872 | tf_op jit(solution)/shard_map/ppermute | solution.py:285
  30.4 1.1 collective-permute-done.4
  31.6 0.1 pad_maximum_fusion.a0
  31.6 0.1 pad_maximum_fusion.1.b0
  31.7 2.1 %collective-permute-start.9 = (bf16[4,2,320,128]{3,2,1,0:T(8,128)(2,1)S(1)}, bf16[4,2,320,128]{3,2,1,0:T(8,128)(2,1)S(1)}, u32[]{:S(2)}, u32[]{:S(2)}) collective-permute-start(bf16[4,2,320,128]{3,2,1,0:T(8,128)(2,1)S(1)} %pad_maximum_fusion.a0), channel_id=1, source_target_pairs={{0,16},{8,24},{16,0},{24,8},{1,17},{9,25},{17,1},{25,9},{2,18},{10... | collective-permute-start | bytes 1966088 | tf_op jit(solution)/shard_map/ppermute | solution.py:285
  33.8 1.1 collective-permute-start.8
  34.9 1.0 collective-permute-start.7
  35.8 2.4 %collective-permute-start.12 = (bf16[4,2,320,128]{3,2,1,0:T(8,128)(2,1)S(1)}, bf16[4,2,320,128]{3,2,1,0:T(8,128)(2,1)}, u32[]{:S(2)}, u32[]{:S(2)}) collective-permute-start(bf16[4,2,320,128]{3,2,1,0:T(8,128)(2,1)S(1)} %pad_maximum_fusion.1.b0), channel_id=1, source_target_pairs={{0,2},{1,3},{2,0},{3,1},{4,6},{5,7},{6,4},{7,5},{8,10},{9,11},{10,... | collective-permute-start | bytes 1966088 | tf_op jit(solution)/shard_map/ppermute | solution.py:279
  38.2 1.2 collective-permute-start.11
  39.4 11.7 %collective-permute-done.9.a3 = bf16[4,2,320,128]{3,2,1,0:T(8,128)(2,1)S(1)} collective-permute-done((bf16[4,2,320,128]{3,2,1,0:T(8,128)(2,1)S(1)}, bf16[4,2,320,128]{3,2,1,0:T(8,128)(2,1)S(1)}, u32[]{:S(2)}, u32[]{:S(2)}) %collective-permute-start.9) | collective-permute-done | bytes 655392 | tf_op jit(solution)/shard_map/ppermute | solution.py:285
  51.0 1.5 %collective-permute-start.10 = (bf16[4,2,320,128]{3,2,1,0:T(8,128)(2,1)S(1)}, bf16[4,2,320,128]{3,2,1,0:T(8,128)(2,1)}, u32[]{:S(2)}, u32[]{:S(2)}) collective-permute-start(bf16[4,2,320,128]{3,2,1,0:T(8,128)(2,1)S(1)} %pad_maximum_fusion.1.b0), channel_id=1, source_target_pairs={{0,1},{1,2},{2,3},{3,0},{4,5},{5,6},{6,7},{7,4},{8,9},{9,10},{10,1... | collective-permute-start | bytes 1966088 | tf_op jit(solution)/shard_map/ppermute | solution.py:279
  52.5 0.0 copy-done.6
  52.5 0.1 copy.15
  52.6 0.1 reshape.20.spos
  52.7 0.0 copy-done.1
  52.7 0.0 copy-done.3
  52.8 0.0 copy-start
  52.8 2.2 %copy-done = bf16[32,4,128,128]{3,2,1,0:T(8,128)(2,1)S(1)} copy-done((bf16[32,4,128,128]{3,2,1,0:T(8,128)(2,1)S(1)}, bf16[32,4,128,128]{3,2,1,0:T(8,128)(2,1)}, u32[]{:S(2)}) %copy-start) | copy-done | bytes 4194328
  55.0 3.7 %early.1 = (bf16[1024,128]{1,0:T(8,128)(2,1)S(1)}, bf16[128,1024]{1,0:T(8,128)(2,1)S(1)}, f32[128,128]{1,0:T(8,128)S(1)}, bf16[32,512,128]{2,1,0:T(8,128)(2,1)S(...) custom-call(bf16[1,8,128,128]{3,2,1,0:T(8,128)(2,1)S(1)} %copy-done.2, ...), custom_call_target="tpu_custom_call" | custom-call | flops 1258291200 | bytes 20971520 | tf_op jit(solution)/shard_map/early/pallas_call | solution.py:87
  58.6 3.0 %collective-permute-done.8.a2 = bf16[4,2,320,128]{3,2,1,0:T(8,128)(2,1)} collective-permute-done((bf16[4,2,320,128]{3,2,1,0:T(8,128)(2,1)S(1)}, bf16[4,2,320,128]{3,2,1,0:T(8,128)(2,1)}, u32[]{:S(2)}, u32[]{:S(2)}) %collective-permute-start.8) | collective-permute-done | bytes 655392 | tf_op jit(solution)/shard_map/ppermute | solution.py:285
  61.7 0.0 collective-permute-done.7.a1
  61.7 0.0 collective-permute-done.12.b3
  61.7 3.4 %collective-permute-done.11.b2 = bf16[4,2,320,128]{3,2,1,0:T(8,128)(2,1)} collective-permute-done((bf16[4,2,320,128]{3,2,1,0:T(8,128)(2,1)S(1)}, bf16[4,2,320,128]{3,2,1,0:T(8,128)(2,1)}, u32[]{:S(2)}, u32[]{:S(2)}) %collective-permute-start.11) | collective-permute-done | bytes 655392 | tf_op jit(solution)/shard_map/ppermute | solution.py:279
  65.0 0.0 collective-permute-done.10.b1
  65.1 0.0 copy-done.4
  65.1 19.0 %late.1 = (bf16[1,8,128,128]{3,2,1,0:T(8,128)(2,1)}, bf16[1,128,128]{2,1,0:T(8,128)(2,1)}, bf16[32,4,128,128]{3,2,1,0:T(8,128)(2,1)}, bf16[32,128,128]{2,1,0:T(8,128)(2,1)}, bf16[4096,128]{1,0:T(8,128)(2,1)S(1)}) custom-call(s32[1]{0:T(128)} %bitcast.pos, s32[1,8]{1,0:T(1,128)S(1)} %copy-done.5, s32[96]{0:T(128)S(1)} %reshape.20.spos, s32[4096]{0:T(1024)S(1)} %copy-done.4, ...), custom_call_target="tpu_custom_call" | custom-call | flops 3019898880 | bytes 20971520 | tf_op jit(solution)/shard_map/late/pallas_call | solution.py:233
  84.1 39.0 %all_to_all.12 = bf16[32,128,128]{2,1,0:T(8,128)(2,1)S(1)} all-to-all(bf16[32,128,128]{2,1,0:T(8,128)(2,1)S(1)} %bitcast.11), channel_id=1, replica_groups=mesh['grp'=8,'row'=4,'col'=8] {'row','col'}, dimensions={0} | all-to-all | bytes 2097152 | tf_op jit(solution)/shard_map/all_to_all | solution.py:315
  123.1 1.0 copy.17
  (4 shorter events, 0.0 us)
Async XLA Ops:
  0.6 51.9 %copy-start.6 = (s32[32,3]{0,1:T(4,128)S(1)}, s32[32,3]{0,1:T(4,128)}, u32[]{:S(2)}) copy-start(s32[32,3]{0,1:T(4,128)} %param.15) | copy-start | bytes 1156
  0.6 52.1 %copy-start.1 = (bf16[32,128,128]{2,1,0:T(8,128)(2,1)S(1)}, bf16[32,128,128]{2,1,0:T(8,128)(2,1)}, u32[]{:S(2)}) copy-start(bf16[32,128,128]{2,1,0:T(8,128)(2,1)} %si.1) | copy-start | bytes 3145732
  0.7 52.1 %copy-start.3 = (bf16[1,128,128]{2,1,0:T(8,128)(2,1)S(1)}, bf16[1,128,128]{2,1,0:T(8,128)(2,1)}, u32[]{:S(2)}) copy-start(bf16[1,128,128]{2,1,0:T(8,128)(2,1)} %fi.1) | copy-start | bytes 98308
  0.7 52.1 %copy-start.2 = (bf16[1,8,128,128]{3,2,1,0:T(8,128)(2,1)S(1)}, bf16[1,8,128,128]{3,2,1,0:T(8,128)(2,1)}, u32[]{:S(2)}) copy-start(bf16[1,8,128,128]{3,2,1,0:T(8,128)(2,1)} %fp.1) | copy-start | bytes 786436
  2.4 14.0 %collective-permute-start = (bf16[2,320,128]{2,1,0:T(8,128)(2,1)}, bf16[2,320,128]{2,1,0:T(8,128)(2,1)S(1)}, u32[]{:S(2)}, u32[]{:S(2)}) collective-permute-start(bf16[2,320,128]{2,1,0:T(8,128)(2,1)} %pack.1), channel_id=1, source_target_pairs={{0,4},{1,5},{2,6},{3,7},{4,0},{5,1},{6,2},{7,3},{8,12},{9,13},{10,... | collective-permute-start | bytes 491528 | tf_op jit(solution)/shard_map/ppermute | solution.py:306
  16.4 48.6 %copy-start.4 = (s32[4096]{0:T(1024)S(1)}, s32[4096]{0:T(1024)}, u32[]{:S(2)}) copy-start(s32[4096]{0:T(1024)} %order.1) | copy-start | bytes 49156
  16.4 48.6 %copy-start.5 = (s32[1,8]{1,0:T(1,128)S(1)}, s32[1,8]{1,0:T(1,128)}, u32[]{:S(2)}) copy-start(s32[1,8]{1,0:T(1,128)} %fidx.1) | copy-start | bytes 100
  16.4 8.6 %collective-permute-start.3 = (bf16[2,320,128]{2,1,0:T(8,128)(2,1)S(1)}, bf16[2,320,128]{2,1,0:T(8,128)(2,1)S(1)}, u32[]{:S(2)}, u32[]{:S(2)}) collective-permute-start(bf16[2,320,128]{2,1,0:T(8,128)(2,1)S(1)} %get-tuple-element.30), channel_id=1, source_target_pairs={{0,2},{1,3},{2,0},{3,1},{4,6},{5,7},{6,4},{7,5},{8,10},{9,11},{10,... | collective-permute-start | bytes 491528 | tf_op jit(solution)/shard_map/ppermute | solution.py:279
  18.6 8.1 %collective-permute-start.2 = (bf16[2,320,128]{2,1,0:T(8,128)(2,1)S(1)}, bf16[2,320,128]{2,1,0:T(8,128)(2,1)S(1)}, u32[]{:S(2)}, u32[]{:S(2)}) collective-permute-start(bf16[2,320,128]{2,1,0:T(8,128)(2,1)S(1)} %get-tuple-element.30), channel_id=1, source_target_pairs={{0,3},{1,0},{2,1},{3,2},{4,7},{5,4},{6,5},{7,6},{8,11},{9,8},{10,9... | collective-permute-start | bytes 491528 | tf_op jit(solution)/shard_map/ppermute | solution.py:279
  20.1 6.7 %collective-permute-start.1 = (bf16[2,320,128]{2,1,0:T(8,128)(2,1)S(1)}, bf16[2,320,128]{2,1,0:T(8,128)(2,1)S(1)}, u32[]{:S(2)}, u32[]{:S(2)}) collective-permute-start(bf16[2,320,128]{2,1,0:T(8,128)(2,1)S(1)} %get-tuple-element.30), channel_id=1, source_target_pairs={{0,1},{1,2},{2,3},{3,0},{4,5},{5,6},{6,7},{7,4},{8,9},{9,10},{10,1... | collective-permute-start | bytes 491528 | tf_op jit(solution)/shard_map/ppermute | solution.py:279
  20.7 7.9 %collective-permute-start.6 = (bf16[2,320,128]{2,1,0:T(8,128)(2,1)S(1)}, bf16[2,320,128]{2,1,0:T(8,128)(2,1)S(1)}, u32[]{:S(2)}, u32[]{:S(2)}) collective-permute-start(bf16[2,320,128]{2,1,0:T(8,128)(2,1)S(1)} %get-tuple-element.34), channel_id=1, source_target_pairs={{0,16},{8,24},{16,0},{24,8},{1,17},{9,25},{17,1},{25,9},{2,18},{10... | collective-permute-start | bytes 491528 | tf_op jit(solution)/shard_map/ppermute | solution.py:285
  23.9 6.6 %collective-permute-start.5 = (bf16[2,320,128]{2,1,0:T(8,128)(2,1)S(1)}, bf16[2,320,128]{2,1,0:T(8,128)(2,1)S(1)}, u32[]{:S(2)}, u32[]{:S(2)}) collective-permute-start(bf16[2,320,128]{2,1,0:T(8,128)(2,1)S(1)} %get-tuple-element.34), channel_id=1, source_target_pairs={{0,24},{8,0},{16,8},{24,16},{1,25},{9,1},{17,9},{25,17},{2,26},{10... | collective-permute-start | bytes 491528 | tf_op jit(solution)/shard_map/ppermute | solution.py:285
  25.0 6.5 %collective-permute-start.4 = (bf16[2,320,128]{2,1,0:T(8,128)(2,1)S(1)}, bf16[2,320,128]{2,1,0:T(8,128)(2,1)S(1)}, u32[]{:S(2)}, u32[]{:S(2)}) collective-permute-start(bf16[2,320,128]{2,1,0:T(8,128)(2,1)S(1)} %get-tuple-element.34), channel_id=1, source_target_pairs={{0,8},{8,16},{16,24},{24,0},{1,9},{9,17},{17,25},{25,1},{2,10},{10... | collective-permute-start | bytes 491528 | tf_op jit(solution)/shard_map/ppermute | solution.py:285
  31.7 19.3 %collective-permute-start.9 = (bf16[4,2,320,128]{3,2,1,0:T(8,128)(2,1)S(1)}, bf16[4,2,320,128]{3,2,1,0:T(8,128)(2,1)S(1)}, u32[]{:S(2)}, u32[]{:S(2)}) collective-permute-start(bf16[4,2,320,128]{3,2,1,0:T(8,128)(2,1)S(1)} %pad_maximum_fusion.a0), channel_id=1, source_target_pairs={{0,16},{8,24},{16,0},{24,8},{1,17},{9,25},{17,1},{25,9},{2,18},{10... | collective-permute-start | bytes 1966088 | tf_op jit(solution)/shard_map/ppermute | solution.py:285
  33.8 27.9 %collective-permute-start.8 = (bf16[4,2,320,128]{3,2,1,0:T(8,128)(2,1)S(1)}, bf16[4,2,320,128]{3,2,1,0:T(8,128)(2,1)}, u32[]{:S(2)}, u32[]{:S(2)}) collective-permute-start(bf16[4,2,320,128]{3,2,1,0:T(8,128)(2,1)S(1)} %pad_maximum_fusion.a0), channel_id=1, source_target_pairs={{0,24},{8,0},{16,8},{24,16},{1,25},{9,1},{17,9},{25,17},{2,26},{10... | collective-permute-start | bytes 1966088 | tf_op jit(solution)/shard_map/ppermute | solution.py:285
  34.9 26.8 %collective-permute-start.7 = (bf16[4,2,320,128]{3,2,1,0:T(8,128)(2,1)S(1)}, bf16[4,2,320,128]{3,2,1,0:T(8,128)(2,1)}, u32[]{:S(2)}, u32[]{:S(2)}) collective-permute-start(bf16[4,2,320,128]{3,2,1,0:T(8,128)(2,1)S(1)} %pad_maximum_fusion.a0), channel_id=1, source_target_pairs={{0,8},{8,16},{16,24},{24,0},{1,9},{9,17},{17,25},{25,1},{2,10},{10... | collective-permute-start | bytes 1966088 | tf_op jit(solution)/shard_map/ppermute | solution.py:285
  35.8 25.8 %collective-permute-start.12 = (bf16[4,2,320,128]{3,2,1,0:T(8,128)(2,1)S(1)}, bf16[4,2,320,128]{3,2,1,0:T(8,128)(2,1)}, u32[]{:S(2)}, u32[]{:S(2)}) collective-permute-start(bf16[4,2,320,128]{3,2,1,0:T(8,128)(2,1)S(1)} %pad_maximum_fusion.1.b0), channel_id=1, source_target_pairs={{0,2},{1,3},{2,0},{3,1},{4,6},{5,7},{6,4},{7,5},{8,10},{9,11},{10,... | collective-permute-start | bytes 1966088 | tf_op jit(solution)/shard_map/ppermute | solution.py:279
  38.2 26.9 %collective-permute-start.11 = (bf16[4,2,320,128]{3,2,1,0:T(8,128)(2,1)S(1)}, bf16[4,2,320,128]{3,2,1,0:T(8,128)(2,1)}, u32[]{:S(2)}, u32[]{:S(2)}) collective-permute-start(bf16[4,2,320,128]{3,2,1,0:T(8,128)(2,1)S(1)} %pad_maximum_fusion.1.b0), channel_id=1, source_target_pairs={{0,3},{1,0},{2,1},{3,2},{4,7},{5,4},{6,5},{7,6},{8,11},{9,8},{10,9... | collective-permute-start | bytes 1966088 | tf_op jit(solution)/shard_map/ppermute | solution.py:279
  51.0 14.0 %collective-permute-start.10 = (bf16[4,2,320,128]{3,2,1,0:T(8,128)(2,1)S(1)}, bf16[4,2,320,128]{3,2,1,0:T(8,128)(2,1)}, u32[]{:S(2)}, u32[]{:S(2)}) collective-permute-start(bf16[4,2,320,128]{3,2,1,0:T(8,128)(2,1)S(1)} %pad_maximum_fusion.1.b0), channel_id=1, source_target_pairs={{0,1},{1,2},{2,3},{3,0},{4,5},{5,6},{6,7},{7,4},{8,9},{9,10},{10,1... | collective-permute-start | bytes 1966088 | tf_op jit(solution)/shard_map/ppermute | solution.py:279
  52.8 2.2 %copy-start = (bf16[32,4,128,128]{3,2,1,0:T(8,128)(2,1)S(1)}, bf16[32,4,128,128]{3,2,1,0:T(8,128)(2,1)}, u32[]{:S(2)}) copy-start(bf16[32,4,128,128]{3,2,1,0:T(8,128)(2,1)} %sp.1) | copy-start | bytes 12582916

commit v4 on v3

--- a/solution.py
+++ b/solution.py
@@ -1,5 +1,3 @@
-import functools
-
 import jax
 import jax.numpy as jnp
 from jax import lax
@@ -13,7 +11,8 @@
 Q = 3
 WIN = 8
 SHARD = 48
-SENT = 4 * SHARD + B
+PART = 4 * SHARD
+SENT = PART + B
 TILES = 32
 F32 = jnp.float32
 BF = jnp.bfloat16
@@ -58,6 +57,34 @@
         out_specs=pl.BlockSpec(memory_space=pltpu.VMEM),
         name="pack",
     )(me.reshape(1), x, sens)
+
+
+def sort_near_kernel(*refs):
+    parts, outs, sems = refs[:8], refs[8:12], refs[12]
+    copies = []
+    for n, ref in enumerate(parts):
+        half, t = n // 4, n % 4
+        copies += [
+            pltpu.make_async_copy(ref.at[:, pl.ds(0, PART)], outs[half].at[t], sems.at[n]),
+            pltpu.make_async_copy(ref.at[:, pl.ds(PART, B)], outs[2 + half].at[t], sems.at[8 + n]),
+        ]
+    for copy in copies:
+        copy.start()
+    for copy in copies:
+        copy.wait()
+
+
+def sort_near(near_a, near_b):
+    any_ = pl.BlockSpec(memory_space=pl.ANY)
+    return pl.pallas_call(
+        sort_near_kernel,
+        out_shape=[jax.ShapeDtypeStruct((4, 2, n, B), BF) for n in (PART, PART, B, B)],
+        in_specs=[any_] * 8,
+        out_specs=[any_] * 4,
+        scratch_shapes=[pltpu.SemaphoreType.DMA((16,))],
+        compiler_params=pltpu.CompilerParams(vmem_limit_bytes=2**20),
+        name="sort_near",
+    )(*near_a, *near_b)
 
 
 KIDS = 8
@@ -118,10 +145,10 @@
 
 
 def late_kernel(
-    steps, pos, fidx, spos, order,
+    pos, fidx, spos,
     a0, a1, a2, a3, b0, b1, b2, b3, fu, fut, fw, su, sut, sw,
-    fc_o, fd_o, sc_o, sd_o, rows_o,
-    full, tmat, cov, even, odd, sens, landed, sems,
+    fc_o, fd_o, sc_o, sd_o, cov_o,
+    full, tmat, landed, sems,
 ):
     step = pl.program_id(0)
 
@@ -152,7 +179,6 @@
                             full[pl.ds(at, SHARD), pl.ds(pl.multiple_of(col * B, B), B)] = (
                                 landed[group, u, z, k * SHARD:(k + 1) * SHARD]
                             )
-                        sens[src, half * B:(half + 1) * B] = landed[group, u, z, 4 * SHARD:]
 
         def block(p, q):
             return full[
@@ -180,67 +206,110 @@
         fd_o[0] = diag
         tmat[:B, :B] = diag
 
-    @pl.when(step < steps)
-    def _():
-        for c in range(KIDS):
-            kid = step * KIDS + c
-            at = [0] + [(1 + spos[kid * Q + q]) * B for q in range(Q)]
-            at = [pl.ds(pl.multiple_of(v, B), B) for v in at]
-            for r in range(Q + 1):
-                line = jnp.concatenate([tmat[at[r], at[q]] for q in range(Q + 1)], axis=1)
-                sc_o[c, r] = (-mm(line, su[c])).astype(BF)
-        for c in range(KIDS):
-            w = sc_o[c].reshape((Q + 1) * B, B)
-            d = (sw[c] - mm(sut[c], w)).astype(BF)
-            sd_o[c] = d
-            base = pl.multiple_of((step * KIDS + c) * 2 * B, 2 * B)
-            cov[pl.ds(base, B, stride=2), :] = d.astype(F32)
-            cov[pl.ds(base + 1, B, stride=2), :] = w[:B].astype(F32)
-
-    @pl.when(step == steps)
-    def _():
-        def move(t, got):
-            for m in range(B):
-                src = order[t * B + m]
-                got[2 * m:2 * m + 2, :] = cov[pl.ds(pl.multiple_of(src * 2, 2), 2), :]
-
-        def product(t, got):
-            line = jnp.concatenate(
-                [got[pl.ds(0, B, stride=2), :], got[pl.ds(1, B, stride=2), :]], axis=1
-            ).astype(BF)
-            rows_o[pl.ds(pl.multiple_of(t * B, B), B)] = mm(line, sens[t]).astype(BF)
-
-        move(0, even)
-
-        def pair(i, carry):
-            move(2 * i + 1, odd)
-            product(2 * i, even)
-            move(jnp.minimum(2 * i + 2, TILES - 1), even)
-            product(2 * i + 1, odd)
-            return carry
-
-        lax.fori_loop(0, TILES // 2, pair, 0)
-
-
-def late(me, fidx, spos, order, ga, gb, fu, fut, fw, su, sut, sw):
+    for c in range(KIDS):
+        kid = step * KIDS + c
+        at = [0] + [(1 + spos[kid * Q + q]) * B for q in range(Q)]
+        at = [pl.ds(pl.multiple_of(v, B), B) for v in at]
+        for r in range(Q + 1):
+            line = jnp.concatenate([tmat[at[r], at[q]] for q in range(Q + 1)], axis=1)
+            sc_o[c, r] = (-mm(line, su[c])).astype(BF)
+    for c in range(KIDS):
+        w = sc_o[c].reshape((Q + 1) * B, B)
+        d = (sw[c] - mm(sut[c], w)).astype(BF)
+        sd_o[c] = d
+        cov_o[pl.ds(c * 2 * B, B, stride=2), :] = d.astype(F32)
+        cov_o[pl.ds(c * 2 * B + 1, B, stride=2), :] = w[:B].astype(F32)
+
+
+def final_kernel(
+    pos, order, a0, a1, a2, a3, b0, b1, b2, b3, cov_in, rows_o, cov, even, odd, landed, sems
+):
+    me = pos[0]
+    whole = pltpu.make_async_copy(cov_in, cov, sems.at[8])
+    whole.start()
+    copies = [
+        pltpu.make_async_copy(ref, landed.at[n], sems.at[n])
+        for n, ref in enumerate((a0, a1, a2, a3, b0, b1, b2, b3))
+    ]
+    for copy in copies:
+        copy.start()
+    whole.wait()
+
+    def place(diff):
+        diff = lax.rem(diff + 4, 4)
+        return jnp.where(diff < 2, diff, 5 - diff)
+
+    def move(t, got):
+        for m in range(B):
+            src = order[t * B + m]
+            got[2 * m:2 * m + 2, :] = cov[pl.ds(pl.multiple_of(src * 2, 2), 2), :]
+
+    def product(t, got):
+        line = jnp.concatenate(
+            [got[pl.ds(0, B, stride=2), :], got[pl.ds(1, B, stride=2), :]], axis=1
+        ).astype(BF)
+        by_row = place(me // 8 - t // 8)
+        by_x = place(me % 4 - t % 4)
+        z = lax.rem((me // 4) % 2 + (t // 4) % 2, 2)
+        sens = jnp.concatenate([landed[by_row, by_x, z], landed[4 + by_x, by_row, z]], axis=0)
+        rows_o[pl.ds(pl.multiple_of(t * B, B), B)] = mm(line, sens).astype(BF)
+
+    move(0, even)
+    for copy in copies:
+        copy.wait()
+
+    def pair(i, carry):
+        move(2 * i + 1, odd)
+        product(2 * i, even)
+        move(jnp.minimum(2 * i + 2, TILES - 1), even)
+        product(2 * i + 1, odd)
+        return carry
+
+    lax.fori_loop(0, TILES // 2, pair, 0)
+
+
+def final(me, order, ta, tb, cov):
+    smem = pl.BlockSpec(memory_space=pltpu.SMEM)
+    n = cov.shape[0]
+    return pl.pallas_call(
+        final_kernel,
+        out_shape=jax.ShapeDtypeStruct((n // 2, B), BF),
+        in_specs=[smem] * 2 + [pl.BlockSpec(memory_space=pl.ANY)] * 9,
+        out_specs=pl.BlockSpec(memory_space=pltpu.VMEM),
+        scratch_shapes=[
+            pltpu.VMEM((n, B), F32),
+            pltpu.VMEM((2 * B, B), F32),
+            pltpu.VMEM((2 * B, B), F32),
+            pltpu.VMEM((8, 4, 2, B, B), BF),
+            pltpu.SemaphoreType.DMA((9,)),
+        ],
+        cost_estimate=pl.CostEstimate(
+            flops=64 * 2 * B**3, bytes_accessed=12 * 2**20, transcendentals=0
+        ),
+        compiler_params=pltpu.CompilerParams(vmem_limit_bytes=12 * 2**20),
+        name="final",
+    )(me.reshape(1), order, *ta, *tb, cov)
+
+
+def late(me, fidx, spos, ga, gb, fu, fut, fw, su, sut, sw):
     n = su.shape[0]
     steps = n // KIDS
     whole = lambda *s: pl.BlockSpec(s, lambda i: (0,) * len(s))
     part = lambda *s: pl.BlockSpec(
-        (KIDS,) + s, lambda i: (jnp.minimum(i, steps - 1),) + (0,) * len(s)
+        (KIDS,) + s, lambda i: (i,) + (0,) * len(s)
     )
     smem = pl.BlockSpec(memory_space=pltpu.SMEM)
     return pl.pallas_call(
-        functools.partial(late_kernel, steps),
-        grid=(steps + 1,),
+        late_kernel,
+        grid=(steps,),
         out_shape=(
             jax.ShapeDtypeStruct((1, PS, B, B), BF),
             jax.ShapeDtypeStruct((1, B, B), BF),
             jax.ShapeDtypeStruct((n, Q + 1, B, B), BF),
             jax.ShapeDtypeStruct((n, B, B), BF),
-            jax.ShapeDtypeStruct((n * B, B), BF),
-        ),
-        in_specs=[smem] * 4
+            jax.ShapeDtypeStruct((2 * n * B, B), F32),
+        ),
+        in_specs=[smem] * 3
         + [pl.BlockSpec(memory_space=pl.ANY)] * 8
         + [
             whole(PS * B, B),
@@ -255,24 +324,20 @@
             whole(1, B, B),
             part(Q + 1, B, B),
             part(B, B),
-            whole(n * B, B),
+            pl.BlockSpec((2 * KIDS * B, B), lambda i: (i, 0)),
         ),
         scratch_shapes=[
             pltpu.VMEM((NA * B, NA * B), BF),
             pltpu.VMEM(((PS + 1) * B, (PS + 1) * B), BF),
-            pltpu.VMEM((2 * n * B, B), F32),
-            pltpu.VMEM((2 * B, B), F32),
-            pltpu.VMEM((2 * B, B), F32),
-            pltpu.VMEM((TILES, 2 * B, B), BF),
-            pltpu.VMEM((8, 4, 2, SENT, B), BF),
+            pltpu.VMEM((8, 4, 2, PART, B), BF),
             pltpu.SemaphoreType.DMA((8,)),
         ],
         cost_estimate=pl.CostEstimate(
-            flops=720 * 2 * B**3, bytes_accessed=20 * 2**20, transcendentals=0
-        ),
-        compiler_params=pltpu.CompilerParams(vmem_limit_bytes=30 * 2**20),
+            flops=720 * 2 * B**3, bytes_accessed=32 * 2**20, transcendentals=0
+        ),
+        compiler_params=pltpu.CompilerParams(vmem_limit_bytes=26 * 2**20),
         name="late",
-    )(me.reshape(1), fidx, spos.reshape(-1), order, *ga, *gb, fu, fut, fw, su, sut, sw)
+    )(me.reshape(1), fidx, spos.reshape(-1), *ga, *gb, fu, fut, fw, su, sut, sw)
 
 
 def along_x(v, k):
@@ -306,12 +371,15 @@
     other = lax.ppermute(mine, "col", [(c, (c + 4) % 8) for c in range(8)])
     half_a, half_b = fixed((jnp.stack([mine[0], other[0]]), jnp.stack([mine[1], other[1]])))
     near_a, near_b = fixed((spread(half_a, along_x), spread(half_b, along_row)))
-    near_a, near_b = fixed((jnp.stack(near_a), jnp.stack(near_b)))
+    near_a, near_b, sens_a, sens_b = sort_near(near_a, near_b)
     ga, gb = spread(near_a, along_row), spread(near_b, along_x)
+    sens_a, sens_b, ga = fixed((sens_a, sens_b, ga))
+    ta, tb = spread(sens_a, along_row), spread(sens_b, along_x)
     fu, fut, fw, su, sut, sw = early(first_panel, first_inverse, second_panel, second_inverse)
-    first_cross, first_diag, second_cross, second_diag, products = late(
-        me, first_index, second_positions, row_order, ga, gb, fu, fut, fw, su, sut, sw
+    first_cross, first_diag, second_cross, second_diag, cov = late(
+        me, first_index, second_positions, ga, gb, fu, fut, fw, su, sut, sw
     )
+    products = final(me, row_order, ta, tb, cov)
     tile_products = lax.all_to_all(
         products, ("row", "col"), split_axis=0, concat_axis=0, tiled=True
     )

time: 126 us -> 126 us (level); the launches traced: 124 us -> 125 us
  blocking collectives: 39 us -> 33.9 us
  waiting for transfers between devices: 29.8 us -> 24.7 us
  starting transfers between devices: 25.5 us -> 29.8 us
  local copies, waits for them, and re-layouts: 4.36 us -> 8.64 us
  Pallas kernels: 24.4 us -> 27.6 us
    all_to_all x1, blocking collectives: 39 us -> 33.9 us  [local(): lax.all_to_all(products, ('row', 'col'), split_axis=0, concat_axis=0, til...]
    unnamed x16 -> x18, local copies, waits for them, and re-layouts: 3.27 us -> 7.56 us
    pallas_call x1 -> x3, Pallas kernels: 19 us -> 22.3 us  [the longest x1 12.4 us: late(): pl.pallas_call(late_kernel, grid=(steps,), out_shape=(jax.ShapeDtypeStruc...]
    ppermute x6 -> x9, starting transfers between devices: 9.92 us -> 13.1 us  [along_row(): return lax.ppermute(v, 'row', [(r, (r + k) % 4) for r in range(4)])]
    ppermute x6 -> x9, waiting for transfers between devices: 19.5 us -> 16.7 us  [along_row(): return lax.ppermute(v, 'row', [(r, (r + k) % 4) for r in range(4)])]
    ppermute x6 -> x9, waiting for transfers between devices: 3.69 us -> 1.24 us  [along_x(): lax.ppermute(v, 'col', [(z * 4 + x, z * 4 + (x + k) % 4) for z in range(2...]
    ppermute x6 -> x9, starting transfers between devices: 9.28 us -> 10.4 us  [along_x(): lax.ppermute(v, 'col', [(z * 4 + x, z * 4 + (x + k) % 4) for z in range(2...]
  transfers between devices with their start and end apart: 13 -> 19, of which waited for: 9 -> 6; matrix products, arithmetic and copies ran while one was open for 1% -> 1% of each run, Pallas kernels for 3% -> 13%
where the time goes in v4:
time: 126 us; the launch traced here: 125 us
  blocking collectives  33.9 us (27%)
  starting transfers between devices  29.8 us (24%)
  Pallas kernels  27.6 us (22%)
  waiting for transfers between devices  24.7 us (20%)
  local copies, waits for them, and re-layouts  8.64 us (7%)
    all_to_all x1, blocking collectives, local(): lax.all_to_all(products, ('row', 'col'), split_axis=0, concat_axis=0, til...  33.9 us
    ppermute x9, waiting for transfers between devices, along_row(): return lax.ppermute(v, 'row', [(r, (r + k) % 4) for r in range(4)])  16.7 us
    ppermute x9, starting transfers between devices, along_row(): return lax.ppermute(v, 'row', [(r, (r + k) % 4) for r in range(4)])  13.1 us
    pallas_call x1, Pallas kernels, late(): pl.pallas_call(late_kernel, grid=(steps,), out_shape=(jax.ShapeDtypeStruc...  12.4 us
    ppermute x9, starting transfers between devices, along_x(): lax.ppermute(v, 'col', [(z * 4 + x, z * 4 + (x + k) % 4) for z in range(2...  10.4 us
    pallas_call x1, Pallas kernels, final(): pl.pallas_call(final_kernel, out_shape=jax.ShapeDtypeStruct((n // 2, B),...  8.91 us
    unnamed x18, local copies, waits for them, and re-layouts  7.56 us
    ppermute x1, waiting for transfers between devices, local(): other = lax.ppermute(mine, 'col', [(c, (c + 4) % 8) for c in range(8)])  6.7 us
  transfers between devices with their start and end apart: 19, of which 6 were waited for; matrix products, arithmetic and copies ran while one was open for 1% of the time, Pallas kernels for 13%

profile of v4, /device:TPU:34, one launch (start us, length us, event | category | flops | bytes accessed | tf_op | source)
XLA Modules:
  0.0 125.4 jit_solution(9154352226331728195)
XLA Ops:
  0.6 1.6 %pack.1 = bf16[2,320,128]{2,1,0:T(8,128)(2,1)} custom-call(s32[1]{0:T(128)} %bitcast.pos, bf16[48,1536]{1,0:T(8,128)(2,1)} %x_ref.1, bf16[1,256,128]{2,1,0:T(8,128)(2,1)} %s_ref.1), custom_call_target="tpu_custom_call" | custom-call | tf_op jit(solution)/shard_map/pack/pallas_call | solution.py:49
  2.2 6.3 %collective-permute-start = (bf16[2,320,128]{2,1,0:T(8,128)(2,1)}, bf16[2,320,128]{2,1,0:T(8,128)(2,1)S(1)}, u32[]{:S(2)}, u32[]{:S(2)}) collective-permute-start(bf16[2,320,128]{2,1,0:T(8,128)(2,1)} %pack.1), channel_id=1, source_target_pairs={{0,4},{1,5},{2,6},{3,7},{4,0},{5,1},{6,2},{7,3},{8,12},{9,13},{10,... | collective-permute-start | bytes 491528 | tf_op jit(solution)/shard_map/ppermute | solution.py:371
  8.5 1.0 fusion
  9.5 6.7 %collective-permute-done = bf16[2,320,128]{2,1,0:T(8,128)(2,1)S(1)} collective-permute-done((bf16[2,320,128]{2,1,0:T(8,128)(2,1)}, bf16[2,320,128]{2,1,0:T(8,128)(2,1)S(1)}, u32[]{:S(2)}, u32[]{:S(2)}) %collective-permute-start) | collective-permute-done | bytes 163872 | tf_op jit(solution)/shard_map/ppermute | solution.py:371
  16.3 1.6 %collective-permute-start.1 = (bf16[2,320,128]{2,1,0:T(8,128)(2,1)S(1)}, bf16[2,320,128]{2,1,0:T(8,128)(2,1)S(1)}, u32[]{:S(2)}, u32[]{:S(2)}) collective-permute-start(bf16[2,320,128]{2,1,0:T(8,128)(2,1)S(1)} %get-tuple-element.38.refs_0_), channel_id=1, source_target_pairs={{0,1},{1,2},{2,3},{3,0},{4,5},{5,6},{6,7},{7,4},{8,9},{9,10},{10,1... | collective-permute-start | bytes 491528 | tf_op jit(solution)/shard_map/ppermute | solution.py:344
  17.8 0.5 collective-permute-start.2
  18.4 2.1 %collective-permute-start.3 = (bf16[2,320,128]{2,1,0:T(8,128)(2,1)S(1)}, bf16[2,320,128]{2,1,0:T(8,128)(2,1)S(1)}, u32[]{:S(2)}, u32[]{:S(2)}) collective-permute-start(bf16[2,320,128]{2,1,0:T(8,128)(2,1)S(1)} %get-tuple-element.38.refs_0_), channel_id=1, source_target_pairs={{0,2},{1,3},{2,0},{3,1},{4,6},{5,7},{6,4},{7,5},{8,10},{9,11},{10,... | collective-permute-start | bytes 491528 | tf_op jit(solution)/shard_map/ppermute | solution.py:344
  20.5 1.6 %collective-permute-start.4 = (bf16[2,320,128]{2,1,0:T(8,128)(2,1)S(1)}, bf16[2,320,128]{2,1,0:T(8,128)(2,1)S(1)}, u32[]{:S(2)}, u32[]{:S(2)}) collective-permute-start(bf16[2,320,128]{2,1,0:T(8,128)(2,1)S(1)} %get-tuple-element.42.refs_4_), channel_id=1, source_target_pairs={{0,8},{8,16},{16,24},{24,0},{1,9},{9,17},{17,25},{25,1},{2,10},{10... | collective-permute-start | bytes 491528 | tf_op jit(solution)/shard_map/ppermute | solution.py:350
  22.1 1.7 %collective-permute-start.5 = (bf16[2,320,128]{2,1,0:T(8,128)(2,1)S(1)}, bf16[2,320,128]{2,1,0:T(8,128)(2,1)S(1)}, u32[]{:S(2)}, u32[]{:S(2)}) collective-permute-start(bf16[2,320,128]{2,1,0:T(8,128)(2,1)S(1)} %get-tuple-element.42.refs_4_), channel_id=1, source_target_pairs={{0,24},{8,0},{16,8},{24,16},{1,25},{9,1},{17,9},{25,17},{2,26},{10... | collective-permute-start | bytes 491528 | tf_op jit(solution)/shard_map/ppermute | solution.py:350
  23.7 0.0 collective-permute-done.1.refs_1_
  23.7 2.0 %collective-permute-start.6 = (bf16[2,320,128]{2,1,0:T(8,128)(2,1)S(1)}, bf16[2,320,128]{2,1,0:T(8,128)(2,1)S(1)}, u32[]{:S(2)}, u32[]{:S(2)}) collective-permute-start(bf16[2,320,128]{2,1,0:T(8,128)(2,1)S(1)} %get-tuple-element.42.refs_4_), channel_id=1, source_target_pairs={{0,16},{8,24},{16,0},{24,8},{1,17},{9,25},{17,1},{25,9},{2,18},{10... | collective-permute-start | bytes 491528 | tf_op jit(solution)/shard_map/ppermute | solution.py:350
  25.7 1.2 collective-permute-done.3.refs_3_
  26.9 1.8 %collective-permute-done.4.refs_5_ = bf16[2,320,128]{2,1,0:T(8,128)(2,1)S(1)} collective-permute-done((bf16[2,320,128]{2,1,0:T(8,128)(2,1)S(1)}, bf16[2,320,128]{2,1,0:T(8,128)(2,1)S(1)}, u32[]{:S(2)}, u32[]{:S(2)}) %collective-permute-start.4) | collective-permute-done | bytes 163872 | tf_op jit(solution)/shard_map/ppermute | solution.py:350
  28.8 0.0 collective-permute-done.5.refs_6_
  28.8 2.1 %collective-permute-done.6.refs_7_ = bf16[2,320,128]{2,1,0:T(8,128)(2,1)S(1)} collective-permute-done((bf16[2,320,128]{2,1,0:T(8,128)(2,1)S(1)}, bf16[2,320,128]{2,1,0:T(8,128)(2,1)S(1)}, u32[]{:S(2)}, u32[]{:S(2)}) %collective-permute-start.6) | collective-permute-done | bytes 163872 | tf_op jit(solution)/shard_map/ppermute | solution.py:350
  30.9 1.0 sort_near.1
  31.9 0.0 copy-start.3
  31.9 0.7 copy-done.3
  32.6 1.1 collective-permute-start.7
  33.7 2.1 %collective-permute-start.8 = (bf16[4,2,192,128]{3,2,1,0:T(8,128)(2,1)S(1)}, bf16[4,2,192,128]{3,2,1,0:T(8,128)(2,1)S(1)}, u32[]{:S(2)}, u32[]{:S(2)}) collective-permute-start(bf16[4,2,192,128]{3,2,1,0:T(8,128)(2,1)S(1)} %get-tuple-element.49.a0), channel_id=1, source_target_pairs={{0,24},{8,0},{16,8},{24,16},{1,25},{9,1},{17,9},{25,17},{2,26},{10... | collective-permute-start | bytes 1179656 | tf_op jit(solution)/shard_map/ppermute | solution.py:350
  35.8 0.4 collective-permute-start.9
  36.3 1.2 collective-permute-start.10
  37.5 0.8 collective-permute-start.11
  38.3 11.5 %collective-permute-done.7.a1 = bf16[4,2,192,128]{3,2,1,0:T(8,128)(2,1)S(1)} collective-permute-done((bf16[4,2,192,128]{3,2,1,0:T(8,128)(2,1)S(1)}, bf16[4,2,192,128]{3,2,1,0:T(8,128)(2,1)S(1)}, u32[]{:S(2)}, u32[]{:S(2)}) %collective-permute-start.7) | collective-permute-done | bytes 393248 | tf_op jit(solution)/shard_map/ppermute | solution.py:350
  49.8 0.0 collective-permute-done.8.a2
  49.8 1.3 %collective-permute-done.9.a3 = bf16[4,2,192,128]{3,2,1,0:T(8,128)(2,1)S(1)} collective-permute-done((bf16[4,2,192,128]{3,2,1,0:T(8,128)(2,1)S(1)}, bf16[4,2,192,128]{3,2,1,0:T(8,128)(2,1)S(1)}, u32[]{:S(2)}, u32[]{:S(2)}) %collective-permute-start.9) | collective-permute-done | bytes 393248 | tf_op jit(solution)/shard_map/ppermute | solution.py:350
  51.1 0.4 collective-permute-start.13
  51.5 0.8 copy.15
  52.3 0.1 reshape.21.spos
  52.4 0.0 copy-start
  52.4 2.2 %copy-done = bf16[32,4,128,128]{3,2,1,0:T(8,128)(2,1)S(1)} copy-done((bf16[32,4,128,128]{3,2,1,0:T(8,128)(2,1)S(1)}, bf16[32,4,128,128]{3,2,1,0:T(8,128)(2,1)}, u32[]{:S(2)}) %copy-start) | copy-done | bytes 4194328
  54.6 1.2 copy-done.1
  55.8 0.9 copy-done.2
  56.8 0.8 copy-done.5
  57.5 3.6 %early.1 = (bf16[1024,128]{1,0:T(8,128)(2,1)S(1)}, bf16[128,1024]{1,0:T(8,128)(2,1)S(1)}, f32[128,128]{1,0:T(8,128)S(1)}, bf16[32,512,128]{2,1,0:T(8,128)(2,1)S(...) custom-call(bf16[1,8,128,128]{3,2,1,0:T(8,128)(2,1)S(1)} %copy-done.2, ...), custom_call_target="tpu_custom_call" | custom-call | flops 1258291200 | bytes 20971520 | tf_op jit(solution)/shard_map/early/pallas_call | solution.py:114
  61.1 2.9 %collective-permute-start.14 = (bf16[4,2,128,128]{3,2,1,0:T(8,128)(2,1)S(1)}, bf16[4,2,128,128]{3,2,1,0:T(8,128)(2,1)S(1)}, u32[]{:S(2)}, u32[]{:S(2)}) collective-permute-start(bf16[4,2,128,128]{3,2,1,0:T(8,128)(2,1)S(1)} %get-tuple-element.64.a0), channel_id=1, source_target_pairs={{0,24},{8,0},{16,8},{24,16},{1,25},{9,1},{17,9},{25,17},{2,26},{10... | collective-permute-start | bytes 786440 | tf_op jit(solution)/shard_map/ppermute | solution.py:350
  64.0 0.0 collective-permute-done.10.b1
  64.0 0.9 collective-permute-start.15
  64.9 1.5 %collective-permute-start.16 = (bf16[4,2,128,128]{3,2,1,0:T(8,128)(2,1)S(1)}, bf16[4,2,128,128]{3,2,1,0:T(8,128)(2,1)S(1)}, u32[]{:S(2)}, u32[]{:S(2)}) collective-permute-start(bf16[4,2,128,128]{3,2,1,0:T(8,128)(2,1)S(1)} %copy-done.4), channel_id=1, source_target_pairs={{0,1},{1,2},{2,3},{3,0},{4,5},{5,6},{6,7},{7,4},{8,9},{9,10},{10,1... | collective-permute-start | bytes 786440 | tf_op jit(solution)/shard_map/ppermute | solution.py:344
  66.4 0.0 collective-permute-done.12.b3
  66.4 0.5 collective-permute-start.17
  66.9 0.0 collective-permute-done.13.a1
  66.9 2.1 %collective-permute-start.18 = (bf16[4,2,128,128]{3,2,1,0:T(8,128)(2,1)S(1)}, bf16[4,2,128,128]{3,2,1,0:T(8,128)(2,1)S(1)}, u32[]{:S(2)}, u32[]{:S(2)}) collective-permute-start(bf16[4,2,128,128]{3,2,1,0:T(8,128)(2,1)S(1)} %copy-done.4), channel_id=1, source_target_pairs={{0,2},{1,3},{2,0},{3,1},{4,6},{5,7},{6,4},{7,5},{8,10},{9,11},{10,... | collective-permute-start | bytes 786440 | tf_op jit(solution)/shard_map/ppermute | solution.py:344
  69.1 12.4 %late.1 = (bf16[1,8,128,128]{3,2,1,0:T(8,128)(2,1)}, bf16[1,128,128]{2,1,0:T(8,128)(2,1)}, bf16[32,4,128,128]{3,2,1,0:T(8,128)(2,1)}, bf16[32,128,128]{2,1,0:T(8,128)(2,1)}, f32[8192,128]{1,0:T(8,128)S(1)}) custom-call(s32[1]{0:T(128)} %bitcast.pos, s32[1,8]{1,0:T(1,128)S(1)} %copy-done.7, s32[96]{0:T(128)S(1)} %reshape.21.spos, ...), custom_call_target="tpu_custom_call" | custom-call | flops 3019898880 | bytes 33554432 | tf_op jit(solution)/shard_map/late/pallas_call | solution.py:302
  81.5 0.0 collective-permute-done.14.a2
  81.6 8.9 %final.1 = bf16[4096,128]{1,0:T(8,128)(2,1)S(1)} custom-call(s32[1]{0:T(128)} %bitcast.pos, s32[4096]{0:T(1024)S(1)} %copy-done.6, bf16[4,2,128,128]{3,2,1,0:T(8,128)(2,1)S(1)} %get-tuple-element.64.a0, bf16[4,2,128,128]{3,2,1,0:T(8,128)(2,1)} %collective-permute-done.13.a1, bf16[4,2,128,128]{3,2,1,0:T(8,128)(2,1)S(1)} %collective-permute-done.14.a2, ...), custom_call_target="tpu_custom_call" | custom-call | flops 268435456 | bytes 12582912 | tf_op jit(solution)/shard_map/final/pallas_call | solution.py:274
  90.5 33.9 %all_to_all.12 = bf16[32,128,128]{2,1,0:T(8,128)(2,1)S(1)} all-to-all(bf16[32,128,128]{2,1,0:T(8,128)(2,1)S(1)} %bitcast.3), channel_id=1, replica_groups=mesh['grp'=8,'row'=4,'col'=8] {'row','col'}, dimensions={0} | all-to-all | bytes 2097152 | tf_op jit(solution)/shard_map/all_to_all | solution.py:383
  124.4 1.0 copy.17
  (18 shorter events, 0.1 us)
Async XLA Ops:
  2.2 66.8 %copy-start.7 = (s32[1,8]{1,0:T(1,128)S(1)}, s32[1,8]{1,0:T(1,128)}, u32[]{:S(2)}) copy-start(s32[1,8]{1,0:T(1,128)} %fidx.1) | copy-start | bytes 100
  2.2 14.0 %collective-permute-start = (bf16[2,320,128]{2,1,0:T(8,128)(2,1)}, bf16[2,320,128]{2,1,0:T(8,128)(2,1)S(1)}, u32[]{:S(2)}, u32[]{:S(2)}) collective-permute-start(bf16[2,320,128]{2,1,0:T(8,128)(2,1)} %pack.1), channel_id=1, source_target_pairs={{0,4},{1,5},{2,6},{3,7},{4,0},{5,1},{6,2},{7,3},{8,12},{9,13},{10,... | collective-permute-start | bytes 491528 | tf_op jit(solution)/shard_map/ppermute | solution.py:371
  16.3 7.5 %collective-permute-start.1 = (bf16[2,320,128]{2,1,0:T(8,128)(2,1)S(1)}, bf16[2,320,128]{2,1,0:T(8,128)(2,1)S(1)}, u32[]{:S(2)}, u32[]{:S(2)}) collective-permute-start(bf16[2,320,128]{2,1,0:T(8,128)(2,1)S(1)} %get-tuple-element.38.refs_0_), channel_id=1, source_target_pairs={{0,1},{1,2},{2,3},{3,0},{4,5},{5,6},{6,7},{7,4},{8,9},{9,10},{10,1... | collective-permute-start | bytes 491528 | tf_op jit(solution)/shard_map/ppermute | solution.py:344
  17.8 7.9 %collective-permute-start.2 = (bf16[2,320,128]{2,1,0:T(8,128)(2,1)S(1)}, bf16[2,320,128]{2,1,0:T(8,128)(2,1)S(1)}, u32[]{:S(2)}, u32[]{:S(2)}) collective-permute-start(bf16[2,320,128]{2,1,0:T(8,128)(2,1)S(1)} %get-tuple-element.38.refs_0_), channel_id=1, source_target_pairs={{0,3},{1,0},{2,1},{3,2},{4,7},{5,4},{6,5},{7,6},{8,11},{9,8},{10,9... | collective-permute-start | bytes 491528 | tf_op jit(solution)/shard_map/ppermute | solution.py:344
  18.4 8.6 %collective-permute-start.3 = (bf16[2,320,128]{2,1,0:T(8,128)(2,1)S(1)}, bf16[2,320,128]{2,1,0:T(8,128)(2,1)S(1)}, u32[]{:S(2)}, u32[]{:S(2)}) collective-permute-start(bf16[2,320,128]{2,1,0:T(8,128)(2,1)S(1)} %get-tuple-element.38.refs_0_), channel_id=1, source_target_pairs={{0,2},{1,3},{2,0},{3,1},{4,6},{5,7},{6,4},{7,5},{8,10},{9,11},{10,... | collective-permute-start | bytes 491528 | tf_op jit(solution)/shard_map/ppermute | solution.py:344
  20.5 8.3 %collective-permute-start.4 = (bf16[2,320,128]{2,1,0:T(8,128)(2,1)S(1)}, bf16[2,320,128]{2,1,0:T(8,128)(2,1)S(1)}, u32[]{:S(2)}, u32[]{:S(2)}) collective-permute-start(bf16[2,320,128]{2,1,0:T(8,128)(2,1)S(1)} %get-tuple-element.42.refs_4_), channel_id=1, source_target_pairs={{0,8},{8,16},{16,24},{24,0},{1,9},{9,17},{17,25},{25,1},{2,10},{10... | collective-permute-start | bytes 491528 | tf_op jit(solution)/shard_map/ppermute | solution.py:350
  22.1 6.7 %collective-permute-start.5 = (bf16[2,320,128]{2,1,0:T(8,128)(2,1)S(1)}, bf16[2,320,128]{2,1,0:T(8,128)(2,1)S(1)}, u32[]{:S(2)}, u32[]{:S(2)}) collective-permute-start(bf16[2,320,128]{2,1,0:T(8,128)(2,1)S(1)} %get-tuple-element.42.refs_4_), channel_id=1, source_target_pairs={{0,24},{8,0},{16,8},{24,16},{1,25},{9,1},{17,9},{25,17},{2,26},{10... | collective-permute-start | bytes 491528 | tf_op jit(solution)/shard_map/ppermute | solution.py:350
  23.7 7.2 %collective-permute-start.6 = (bf16[2,320,128]{2,1,0:T(8,128)(2,1)S(1)}, bf16[2,320,128]{2,1,0:T(8,128)(2,1)S(1)}, u32[]{:S(2)}, u32[]{:S(2)}) collective-permute-start(bf16[2,320,128]{2,1,0:T(8,128)(2,1)S(1)} %get-tuple-element.42.refs_4_), channel_id=1, source_target_pairs={{0,16},{8,24},{16,0},{24,8},{1,17},{9,25},{17,1},{25,9},{2,18},{10... | collective-permute-start | bytes 491528 | tf_op jit(solution)/shard_map/ppermute | solution.py:350
  31.9 0.7 copy-start.3
  32.6 17.2 %collective-permute-start.7 = (bf16[4,2,192,128]{3,2,1,0:T(8,128)(2,1)S(1)}, bf16[4,2,192,128]{3,2,1,0:T(8,128)(2,1)S(1)}, u32[]{:S(2)}, u32[]{:S(2)}) collective-permute-start(bf16[4,2,192,128]{3,2,1,0:T(8,128)(2,1)S(1)} %get-tuple-element.49.a0), channel_id=1, source_target_pairs={{0,8},{8,16},{16,24},{24,0},{1,9},{9,17},{17,25},{25,1},{2,10},{10... | collective-permute-start | bytes 1179656 | tf_op jit(solution)/shard_map/ppermute | solution.py:350
  33.7 16.1 %collective-permute-start.8 = (bf16[4,2,192,128]{3,2,1,0:T(8,128)(2,1)S(1)}, bf16[4,2,192,128]{3,2,1,0:T(8,128)(2,1)S(1)}, u32[]{:S(2)}, u32[]{:S(2)}) collective-permute-start(bf16[4,2,192,128]{3,2,1,0:T(8,128)(2,1)S(1)} %get-tuple-element.49.a0), channel_id=1, source_target_pairs={{0,24},{8,0},{16,8},{24,16},{1,25},{9,1},{17,9},{25,17},{2,26},{10... | collective-permute-start | bytes 1179656 | tf_op jit(solution)/shard_map/ppermute | solution.py:350
  35.8 15.2 %collective-permute-start.9 = (bf16[4,2,192,128]{3,2,1,0:T(8,128)(2,1)S(1)}, bf16[4,2,192,128]{3,2,1,0:T(8,128)(2,1)S(1)}, u32[]{:S(2)}, u32[]{:S(2)}) collective-permute-start(bf16[4,2,192,128]{3,2,1,0:T(8,128)(2,1)S(1)} %get-tuple-element.49.a0), channel_id=1, source_target_pairs={{0,16},{8,24},{16,0},{24,8},{1,17},{9,25},{17,1},{25,9},{2,18},{10... | collective-permute-start | bytes 1179656 | tf_op jit(solution)/shard_map/ppermute | solution.py:350
  36.3 27.8 %collective-permute-start.10 = (bf16[4,2,192,128]{3,2,1,0:T(8,128)(2,1)S(1)}, bf16[4,2,192,128]{3,2,1,0:T(8,128)(2,1)S(1)}, u32[]{:S(2)}, u32[]{:S(2)}) collective-permute-start(bf16[4,2,192,128]{3,2,1,0:T(8,128)(2,1)S(1)} %get-tuple-element.53.b0), channel_id=1, source_target_pairs={{0,1},{1,2},{2,3},{3,0},{4,5},{5,6},{6,7},{7,4},{8,9},{9,10},{10,1... | collective-permute-start | bytes 1179656 | tf_op jit(solution)/shard_map/ppermute | solution.py:344
  37.5 27.4 %collective-permute-start.11 = (bf16[4,2,192,128]{3,2,1,0:T(8,128)(2,1)S(1)}, bf16[4,2,192,128]{3,2,1,0:T(8,128)(2,1)S(1)}, u32[]{:S(2)}, u32[]{:S(2)}) collective-permute-start(bf16[4,2,192,128]{3,2,1,0:T(8,128)(2,1)S(1)} %get-tuple-element.53.b0), channel_id=1, source_target_pairs={{0,3},{1,0},{2,1},{3,2},{4,7},{5,4},{6,5},{7,6},{8,11},{9,8},{10,9... | collective-permute-start | bytes 1179656 | tf_op jit(solution)/shard_map/ppermute | solution.py:344
  49.8 16.6 %collective-permute-start.12 = (bf16[4,2,192,128]{3,2,1,0:T(8,128)(2,1)S(1)}, bf16[4,2,192,128]{3,2,1,0:T(8,128)(2,1)S(1)}, u32[]{:S(2)}, u32[]{:S(2)}) collective-permute-start(bf16[4,2,192,128]{3,2,1,0:T(8,128)(2,1)S(1)} %get-tuple-element.53.b0), channel_id=1, source_target_pairs={{0,2},{1,3},{2,0},{3,1},{4,6},{5,7},{6,4},{7,5},{8,10},{9,11},{10,... | collective-permute-start | bytes 1179656 | tf_op jit(solution)/shard_map/ppermute | solution.py:344
  51.1 15.9 %collective-permute-start.13 = (bf16[4,2,128,128]{3,2,1,0:T(8,128)(2,1)S(1)}, bf16[4,2,128,128]{3,2,1,0:T(8,128)(2,1)}, u32[]{:S(2)}, u32[]{:S(2)}) collective-permute-start(bf16[4,2,128,128]{3,2,1,0:T(8,128)(2,1)S(1)} %get-tuple-element.64.a0), channel_id=1, source_target_pairs={{0,8},{8,16},{16,24},{24,0},{1,9},{9,17},{17,25},{25,1},{2,10},{10... | collective-permute-start | bytes 786440 | tf_op jit(solution)/shard_map/ppermute | solution.py:350
  52.4 2.2 %copy-start = (bf16[32,4,128,128]{3,2,1,0:T(8,128)(2,1)S(1)}, bf16[32,4,128,128]{3,2,1,0:T(8,128)(2,1)}, u32[]{:S(2)}) copy-start(bf16[32,4,128,128]{3,2,1,0:T(8,128)(2,1)} %sp.1) | copy-start | bytes 12582916
  54.6 1.2 copy-start.1
  55.8 0.9 copy-start.2
  56.8 0.8 copy-start.5
  57.5 7.4 %copy-start.4 = (bf16[4,2,128,128]{3,2,1,0:T(8,128)(2,1)S(1)}, bf16[4,2,128,128]{3,2,1,0:T(8,128)(2,1)}, u32[]{:S(2)}) copy-start(bf16[4,2,128,128]{3,2,1,0:T(8,128)(2,1)} %copy-done.3) | copy-start | bytes 786436
  61.1 20.4 %collective-permute-start.14 = (bf16[4,2,128,128]{3,2,1,0:T(8,128)(2,1)S(1)}, bf16[4,2,128,128]{3,2,1,0:T(8,128)(2,1)S(1)}, u32[]{:S(2)}, u32[]{:S(2)}) collective-permute-start(bf16[4,2,128,128]{3,2,1,0:T(8,128)(2,1)S(1)} %get-tuple-element.64.a0), channel_id=1, source_target_pairs={{0,24},{8,0},{16,8},{24,16},{1,25},{9,1},{17,9},{25,17},{2,26},{10... | collective-permute-start | bytes 786440 | tf_op jit(solution)/shard_map/ppermute | solution.py:350
  64.0 17.5 %collective-permute-start.15 = (bf16[4,2,128,128]{3,2,1,0:T(8,128)(2,1)S(1)}, bf16[4,2,128,128]{3,2,1,0:T(8,128)(2,1)S(1)}, u32[]{:S(2)}, u32[]{:S(2)}) collective-permute-start(bf16[4,2,128,128]{3,2,1,0:T(8,128)(2,1)S(1)} %get-tuple-element.64.a0), channel_id=1, source_target_pairs={{0,16},{8,24},{16,0},{24,8},{1,17},{9,25},{17,1},{25,9},{2,18},{10... | collective-permute-start | bytes 786440 | tf_op jit(solution)/shard_map/ppermute | solution.py:350
  64.9 16.6 %collective-permute-start.16 = (bf16[4,2,128,128]{3,2,1,0:T(8,128)(2,1)S(1)}, bf16[4,2,128,128]{3,2,1,0:T(8,128)(2,1)S(1)}, u32[]{:S(2)}, u32[]{:S(2)}) collective-permute-start(bf16[4,2,128,128]{3,2,1,0:T(8,128)(2,1)S(1)} %copy-done.4), channel_id=1, source_target_pairs={{0,1},{1,2},{2,3},{3,0},{4,5},{5,6},{6,7},{7,4},{8,9},{9,10},{10,1... | collective-permute-start | bytes 786440 | tf_op jit(solution)/shard_map/ppermute | solution.py:344
  66.4 15.2 %collective-permute-start.17 = (bf16[4,2,128,128]{3,2,1,0:T(8,128)(2,1)S(1)}, bf16[4,2,128,128]{3,2,1,0:T(8,128)(2,1)S(1)}, u32[]{:S(2)}, u32[]{:S(2)}) collective-permute-start(bf16[4,2,128,128]{3,2,1,0:T(8,128)(2,1)S(1)} %copy-done.4), channel_id=1, source_target_pairs={{0,3},{1,0},{2,1},{3,2},{4,7},{5,4},{6,5},{7,6},{8,11},{9,8},{10,9... | collective-permute-start | bytes 786440 | tf_op jit(solution)/shard_map/ppermute | solution.py:344
  66.9 14.6 %collective-permute-start.18 = (bf16[4,2,128,128]{3,2,1,0:T(8,128)(2,1)S(1)}, bf16[4,2,128,128]{3,2,1,0:T(8,128)(2,1)S(1)}, u32[]{:S(2)}, u32[]{:S(2)}) collective-permute-start(bf16[4,2,128,128]{3,2,1,0:T(8,128)(2,1)S(1)} %copy-done.4), channel_id=1, source_target_pairs={{0,2},{1,3},{2,0},{3,1},{4,6},{5,7},{6,4},{7,5},{8,10},{9,11},{10,... | collective-permute-start | bytes 786440 | tf_op jit(solution)/shard_map/ppermute | solution.py:344
  69.1 12.5 %copy-start.6 = (s32[4096]{0:T(1024)S(1)}, s32[4096]{0:T(1024)}, u32[]{:S(2)}) copy-start(s32[4096]{0:T(1024)} %order.1) | copy-start | bytes 49156

commit v5 on v4

--- a/solution.py
+++ b/solution.py
@@ -139,7 +139,7 @@
         cost_estimate=pl.CostEstimate(
             flops=300 * 2 * B**3, bytes_accessed=20 * 2**20, transcendentals=0
         ),
-        compiler_params=pltpu.CompilerParams(vmem_limit_bytes=12 * 2**20),
+        compiler_params=pltpu.CompilerParams(vmem_limit_bytes=58 * 2**20),
         name="early",
     )(fp, fi, sp, si)
 
@@ -286,7 +286,7 @@
         cost_estimate=pl.CostEstimate(
             flops=64 * 2 * B**3, bytes_accessed=12 * 2**20, transcendentals=0
         ),
-        compiler_params=pltpu.CompilerParams(vmem_limit_bytes=12 * 2**20),
+        compiler_params=pltpu.CompilerParams(vmem_limit_bytes=58 * 2**20),
         name="final",
     )(me.reshape(1), order, *ta, *tb, cov)
 
@@ -335,7 +335,7 @@
         cost_estimate=pl.CostEstimate(
             flops=720 * 2 * B**3, bytes_accessed=32 * 2**20, transcendentals=0
         ),
-        compiler_params=pltpu.CompilerParams(vmem_limit_bytes=26 * 2**20),
+        compiler_params=pltpu.CompilerParams(vmem_limit_bytes=56 * 2**20),
         name="late",
     )(me.reshape(1), fidx, spos.reshape(-1), *ga, *gb, fu, fut, fw, su, sut, sw)
 
@@ -369,15 +369,17 @@
     fixed = lax.optimization_barrier
     mine = pack(top_covariance, sensitivity, me)
     other = lax.ppermute(mine, "col", [(c, (c + 4) % 8) for c in range(8)])
+    other, *ready = fixed(
+        (other, *early(first_panel, first_inverse, second_panel, second_inverse))
+    )
     half_a, half_b = fixed((jnp.stack([mine[0], other[0]]), jnp.stack([mine[1], other[1]])))
     near_a, near_b = fixed((spread(half_a, along_x), spread(half_b, along_row)))
     near_a, near_b, sens_a, sens_b = sort_near(near_a, near_b)
     ga, gb = spread(near_a, along_row), spread(near_b, along_x)
     sens_a, sens_b, ga = fixed((sens_a, sens_b, ga))
     ta, tb = spread(sens_a, along_row), spread(sens_b, along_x)
-    fu, fut, fw, su, sut, sw = early(first_panel, first_inverse, second_panel, second_inverse)
     first_cross, first_diag, second_cross, second_diag, cov = late(
-        me, first_index, second_positions, ga, gb, fu, fut, fw, su, sut, sw
+        me, first_index, second_positions, ga, gb, *ready
     )
     products = final(me, row_order, ta, tb, cov)
     tile_products = lax.all_to_all(

time: 126 us -> 127 us (level)
  Pallas kernels: 27.6 us -> 37.1 us
  waiting for transfers between devices: 24.7 us -> 20.4 us
  local copies, waits for them, and re-layouts: 8.64 us -> 4.47 us
  starting transfers between devices: 29.8 us -> 31.5 us
  blocking collectives: 33.9 us -> 32.4 us
    ppermute x1, waiting for transfers between devices: 6.7 us -> 0.01 us  [local(): other = lax.ppermute(mine, 'col', [(c, (c + 4) % 8) for c in range(8)])]
    pallas_call x1, Pallas kernels: 3.63 us -> 8.48 us  [early(): pl.pallas_call(early_kernel, grid=(n // KIDS,), out_shape=(jax.ShapeDtype...]
    unnamed x18 -> x32, local copies, waits for them, and re-layouts: 7.56 us -> 2.8 us
    pallas_call x1, Pallas kernels: 8.91 us -> 11.5 us  [final(): pl.pallas_call(final_kernel, out_shape=jax.ShapeDtypeStruct((n // 2, B),...]
    pallas_call x1, Pallas kernels: 12.4 us -> 14.5 us  [late(): pl.pallas_call(late_kernel, grid=(steps,), out_shape=(jax.ShapeDtypeStruc...]
    ppermute x9, waiting for transfers between devices: 16.7 us -> 18.8 us  [along_row(): return lax.ppermute(v, 'row', [(r, (r + k) % 4) for r in range(4)])]
    all_to_all x1, blocking collectives: 33.9 us -> 32.4 us  [local(): lax.all_to_all(products, ('row', 'col'), split_axis=0, concat_axis=0, til...]
    ppermute x9, starting transfers between devices: 10.4 us -> 11.8 us  [along_x(): lax.ppermute(v, 'col', [(z * 4 + x, z * 4 + (x + k) % 4) for z in range(2...]
  transfers between devices with their start and end apart: 19 -> 19, of which waited for: 6 -> 8; matrix products, arithmetic and copies ran while one was open for 1% -> 2% of each run, Pallas kernels for 13% -> 18%
where the time goes in v5:
time: 127 us
  Pallas kernels  37.1 us (29%)
  blocking collectives  32.4 us (26%)
  starting transfers between devices  31.5 us (25%)
  waiting for transfers between devices  20.4 us (16%)
  local copies, waits for them, and re-layouts  4.47 us (4%)
    all_to_all x1, blocking collectives, local(): lax.all_to_all(products, ('row', 'col'), split_axis=0, concat_axis=0, til...  32.4 us
    ppermute x9, waiting for transfers between devices, along_row(): return lax.ppermute(v, 'row', [(r, (r + k) % 4) for r in range(4)])  18.8 us
    pallas_call x1, Pallas kernels, late(): pl.pallas_call(late_kernel, grid=(steps,), out_shape=(jax.ShapeDtypeStruc...  14.5 us
    ppermute x9, starting transfers between devices, along_row(): return lax.ppermute(v, 'row', [(r, (r + k) % 4) for r in range(4)])  13.4 us
    ppermute x9, starting transfers between devices, along_x(): lax.ppermute(v, 'col', [(z * 4 + x, z * 4 + (x + k) % 4) for z in range(2...  11.8 us
    pallas_call x1, Pallas kernels, final(): pl.pallas_call(final_kernel, out_shape=jax.ShapeDtypeStruct((n // 2, B),...  11.5 us
    pallas_call x1, Pallas kernels, early(): pl.pallas_call(early_kernel, grid=(n // KIDS,), out_shape=(jax.ShapeDtype...  8.48 us
    ppermute x1, starting transfers between devices, local(): other = lax.ppermute(mine, 'col', [(c, (c + 4) % 8) for c in range(8)])  6.29 us
  transfers between devices with their start and end apart: 19, of which 8 were waited for; matrix products, arithmetic and copies ran while one was open for 2% of the time, Pallas kernels for 18%

profile of v5, /device:TPU:34, one launch (start us, length us, event | category | flops | bytes accessed | tf_op | source)
XLA Modules:
  0.0 126.8 jit_solution(6109313494232564182)
XLA Ops:
  0.6 1.6 %pack.1 = bf16[2,320,128]{2,1,0:T(8,128)(2,1)} custom-call(s32[1]{0:T(128)} %bitcast.pos, bf16[48,1536]{1,0:T(8,128)(2,1)} %x_ref.1, bf16[1,256,128]{2,1,0:T(8,128)(2,1)} %s_ref.1), custom_call_target="tpu_custom_call" | custom-call | tf_op jit(solution)/shard_map/pack/pallas_call | solution.py:49
  2.2 6.3 %collective-permute-start = (bf16[2,320,128]{2,1,0:T(8,128)(2,1)}, bf16[2,320,128]{2,1,0:T(8,128)(2,1)S(1)}, u32[]{:S(2)}, u32[]{:S(2)}) collective-permute-start(bf16[2,320,128]{2,1,0:T(8,128)(2,1)} %pack.1), channel_id=1, source_target_pairs={{0,4},{1,5},{2,6},{3,7},{4,0},{5,1},{6,2},{7,3},{8,12},{9,13},{10,... | collective-permute-start | bytes 491528 | tf_op jit(solution)/shard_map/ppermute | solution.py:371
  8.5 1.0 fusion
  9.5 8.5 %early.1 = (bf16[1024,128]{1,0:T(8,128)(2,1)}, bf16[128,1024]{1,0:T(8,128)(2,1)}, f32[128,128]{1,0:T(8,128)}, bf16[32,512,128]{2,1,0:T(8,128)(2,1)}, bf16[32,128...) custom-call(bf16[1,8,128,128]{3,2,1,0:T(8,128)(2,1)} %fp.1, bf16[1,128,128]{2,1,0:T(8,128)(2,1)} %fi.1, ...), custom_call_target="tpu_custom_call" | custom-call | flops 1258291200 | bytes 20971520 | tf_op jit(solution)/shard_map/early/pallas_call | solution.py:114
  18.0 0.0 collective-permute-done
  18.1 1.6 %collective-permute-start.1 = (bf16[2,320,128]{2,1,0:T(8,128)(2,1)S(1)}, bf16[2,320,128]{2,1,0:T(8,128)(2,1)S(1)}, u32[]{:S(2)}, u32[]{:S(2)}) collective-permute-start(bf16[2,320,128]{2,1,0:T(8,128)(2,1)S(1)} %get-tuple-element.52.refs_0_), channel_id=1, source_target_pairs={{0,1},{1,2},{2,3},{3,0},{4,5},{5,6},{6,7},{7,4},{8,9},{9,10},{10,1... | collective-permute-start | bytes 491528 | tf_op jit(solution)/shard_map/ppermute | solution.py:344
  19.6 0.5 collective-permute-start.2
  20.2 2.1 %collective-permute-start.3 = (bf16[2,320,128]{2,1,0:T(8,128)(2,1)S(1)}, bf16[2,320,128]{2,1,0:T(8,128)(2,1)S(1)}, u32[]{:S(2)}, u32[]{:S(2)}) collective-permute-start(bf16[2,320,128]{2,1,0:T(8,128)(2,1)S(1)} %get-tuple-element.52.refs_0_), channel_id=1, source_target_pairs={{0,2},{1,3},{2,0},{3,1},{4,6},{5,7},{6,4},{7,5},{8,10},{9,11},{10,... | collective-permute-start | bytes 491528 | tf_op jit(solution)/shard_map/ppermute | solution.py:344
  22.3 1.6 %collective-permute-start.4 = (bf16[2,320,128]{2,1,0:T(8,128)(2,1)S(1)}, bf16[2,320,128]{2,1,0:T(8,128)(2,1)S(1)}, u32[]{:S(2)}, u32[]{:S(2)}) collective-permute-start(bf16[2,320,128]{2,1,0:T(8,128)(2,1)S(1)} %get-tuple-element.56.refs_4_), channel_id=1, source_target_pairs={{0,8},{8,16},{16,24},{24,0},{1,9},{9,17},{17,25},{25,1},{2,10},{10... | collective-permute-start | bytes 491528 | tf_op jit(solution)/shard_map/ppermute | solution.py:350
  23.9 1.7 %collective-permute-start.5 = (bf16[2,320,128]{2,1,0:T(8,128)(2,1)S(1)}, bf16[2,320,128]{2,1,0:T(8,128)(2,1)S(1)}, u32[]{:S(2)}, u32[]{:S(2)}) collective-permute-start(bf16[2,320,128]{2,1,0:T(8,128)(2,1)S(1)} %get-tuple-element.56.refs_4_), channel_id=1, source_target_pairs={{0,24},{8,0},{16,8},{24,16},{1,25},{9,1},{17,9},{25,17},{2,26},{10... | collective-permute-start | bytes 491528 | tf_op jit(solution)/shard_map/ppermute | solution.py:350
  25.5 0.0 collective-permute-done.1.refs_1_
  25.5 2.0 %collective-permute-start.6 = (bf16[2,320,128]{2,1,0:T(8,128)(2,1)S(1)}, bf16[2,320,128]{2,1,0:T(8,128)(2,1)S(1)}, u32[]{:S(2)}, u32[]{:S(2)}) collective-permute-start(bf16[2,320,128]{2,1,0:T(8,128)(2,1)S(1)} %get-tuple-element.56.refs_4_), channel_id=1, source_target_pairs={{0,16},{8,24},{16,0},{24,8},{1,17},{9,25},{17,1},{25,9},{2,18},{10... | collective-permute-start | bytes 491528 | tf_op jit(solution)/shard_map/ppermute | solution.py:350
  27.5 1.6 %collective-permute-done.3.refs_3_ = bf16[2,320,128]{2,1,0:T(8,128)(2,1)S(1)} collective-permute-done((bf16[2,320,128]{2,1,0:T(8,128)(2,1)S(1)}, bf16[2,320,128]{2,1,0:T(8,128)(2,1)S(1)}, u32[]{:S(2)}, u32[]{:S(2)}) %collective-permute-start.3) | collective-permute-done | bytes 163872 | tf_op jit(solution)/shard_map/ppermute | solution.py:344
  29.2 1.0 collective-permute-done.4.refs_5_
  30.2 0.2 collective-permute-done.5.refs_6_
  30.4 2.7 %collective-permute-done.6.refs_7_ = bf16[2,320,128]{2,1,0:T(8,128)(2,1)S(1)} collective-permute-done((bf16[2,320,128]{2,1,0:T(8,128)(2,1)S(1)}, bf16[2,320,128]{2,1,0:T(8,128)(2,1)S(1)}, u32[]{:S(2)}, u32[]{:S(2)}) %collective-permute-start.6) | collective-permute-done | bytes 163872 | tf_op jit(solution)/shard_map/ppermute | solution.py:350
  33.1 1.0 sort_near.1
  34.1 0.0 copy-start
  34.2 1.2 collective-permute-start.7
  35.3 2.1 %collective-permute-start.8 = (bf16[4,2,192,128]{3,2,1,0:T(8,128)(2,1)S(1)}, bf16[4,2,192,128]{3,2,1,0:T(8,128)(2,1)S(1)}, u32[]{:S(2)}, u32[]{:S(2)}) collective-permute-start(bf16[4,2,192,128]{3,2,1,0:T(8,128)(2,1)S(1)} %get-tuple-element.63.a0), channel_id=1, source_target_pairs={{0,24},{8,0},{16,8},{24,16},{1,25},{9,1},{17,9},{25,17},{2,26},{10... | collective-permute-start | bytes 1179656 | tf_op jit(solution)/shard_map/ppermute | solution.py:350
  37.5 0.1 collective-permute-start.9
  37.6 1.4 %collective-permute-start.10 = (bf16[4,2,192,128]{3,2,1,0:T(8,128)(2,1)S(1)}, bf16[4,2,192,128]{3,2,1,0:T(8,128)(2,1)S(1)}, u32[]{:S(2)}, u32[]{:S(2)}) collective-permute-start(bf16[4,2,192,128]{3,2,1,0:T(8,128)(2,1)S(1)} %get-tuple-element.67.b0), channel_id=1, source_target_pairs={{0,1},{1,2},{2,3},{3,0},{4,5},{5,6},{6,7},{7,4},{8,9},{9,10},{10,1... | collective-permute-start | bytes 1179656 | tf_op jit(solution)/shard_map/ppermute | solution.py:344
  39.0 0.6 collective-permute-start.11
  39.6 8.1 %collective-permute-done.7.a1 = bf16[4,2,192,128]{3,2,1,0:T(8,128)(2,1)S(1)} collective-permute-done((bf16[4,2,192,128]{3,2,1,0:T(8,128)(2,1)S(1)}, bf16[4,2,192,128]{3,2,1,0:T(8,128)(2,1)S(1)}, u32[]{:S(2)}, u32[]{:S(2)}) %collective-permute-start.7) | collective-permute-done | bytes 393248 | tf_op jit(solution)/shard_map/ppermute | solution.py:350
  47.7 0.2 collective-permute-start.12
  47.9 4.0 %collective-permute-done.8.a2 = bf16[4,2,192,128]{3,2,1,0:T(8,128)(2,1)S(1)} collective-permute-done((bf16[4,2,192,128]{3,2,1,0:T(8,128)(2,1)S(1)}, bf16[4,2,192,128]{3,2,1,0:T(8,128)(2,1)S(1)}, u32[]{:S(2)}, u32[]{:S(2)}) %collective-permute-start.8) | collective-permute-done | bytes 393248 | tf_op jit(solution)/shard_map/ppermute | solution.py:350
  51.9 0.7 collective-permute-done.9.a3
  52.6 1.1 collective-permute-start.13
  53.6 0.8 copy.15
  54.4 0.7 reshape.21.spos
  55.1 2.2 %collective-permute-start.14 = (bf16[4,2,128,128]{3,2,1,0:T(8,128)(2,1)S(1)}, bf16[4,2,128,128]{3,2,1,0:T(8,128)(2,1)S(1)}, u32[]{:S(2)}, u32[]{:S(2)}) collective-permute-start(bf16[4,2,128,128]{3,2,1,0:T(8,128)(2,1)S(1)} %get-tuple-element.78.a0), channel_id=1, source_target_pairs={{0,24},{8,0},{16,8},{24,16},{1,25},{9,1},{17,9},{25,17},{2,26},{10... | collective-permute-start | bytes 786440 | tf_op jit(solution)/shard_map/ppermute | solution.py:350
  57.3 1.5 %collective-permute-start.15 = (bf16[4,2,128,128]{3,2,1,0:T(8,128)(2,1)S(1)}, bf16[4,2,128,128]{3,2,1,0:T(8,128)(2,1)S(1)}, u32[]{:S(2)}, u32[]{:S(2)}) collective-permute-start(bf16[4,2,128,128]{3,2,1,0:T(8,128)(2,1)S(1)} %get-tuple-element.78.a0), channel_id=1, source_target_pairs={{0,16},{8,24},{16,0},{24,8},{1,17},{9,25},{17,1},{25,9},{2,18},{10... | collective-permute-start | bytes 786440 | tf_op jit(solution)/shard_map/ppermute | solution.py:350
  58.8 0.0 collective-permute-done.11.b2
  58.8 1.1 collective-permute-start.16
  59.9 0.0 collective-permute-done.12.b3
  59.9 0.9 collective-permute-start.17
  60.8 2.1 %collective-permute-done.13.a1 = bf16[4,2,128,128]{3,2,1,0:T(8,128)(2,1)S(1)} collective-permute-done((bf16[4,2,128,128]{3,2,1,0:T(8,128)(2,1)S(1)}, bf16[4,2,128,128]{3,2,1,0:T(8,128)(2,1)S(1)}, u32[]{:S(2)}, u32[]{:S(2)}) %collective-permute-start.13) | collective-permute-done | bytes 262176 | tf_op jit(solution)/shard_map/ppermute | solution.py:350
  62.9 3.3 %collective-permute-start.18 = (bf16[4,2,128,128]{3,2,1,0:T(8,128)(2,1)S(1)}, bf16[4,2,128,128]{3,2,1,0:T(8,128)(2,1)S(1)}, u32[]{:S(2)}, u32[]{:S(2)}) collective-permute-start(bf16[4,2,128,128]{3,2,1,0:T(8,128)(2,1)S(1)} %get-tuple-element.79.b0), channel_id=1, source_target_pairs={{0,2},{1,3},{2,0},{3,1},{4,6},{5,7},{6,4},{7,5},{8,10},{9,11},{10,... | collective-permute-start | bytes 786440 | tf_op jit(solution)/shard_map/ppermute | solution.py:344
  66.2 14.5 %late.1 = (bf16[1,8,128,128]{3,2,1,0:T(8,128)(2,1)}, bf16[1,128,128]{2,1,0:T(8,128)(2,1)}, bf16[32,4,128,128]{3,2,1,0:T(8,128)(2,1)}, bf16[32,128,128]{2,1,0:T(8,128)(2,1)}, f32[8192,128]{1,0:T(8,128)}) custom-call(s32[1]{0:T(128)} %bitcast.pos, s32[1,8]{1,0:T(1,128)} %fidx.1, s32[96]{0:T(128)} %reshape.21.spos, bf16[4,2,192,128]{3,2,1,0:T(8,128)(2,1)} %copy-done, ...), custom_call_target="tpu_custom_call" | custom-call | flops 3019898880 | bytes 33554432 | tf_op jit(solution)/shard_map/late/pallas_call | solution.py:302
  80.8 0.0 collective-permute-done.15.a3
  80.9 0.6 copy-done.10
  81.5 0.1 copy-done.11
  81.6 0.1 copy-done.12
  81.7 0.1 copy-done.13
  81.8 0.1 copy-done.14
  81.9 11.5 %final.1 = bf16[4096,128]{1,0:T(8,128)(2,1)} custom-call(s32[1]{0:T(128)} %bitcast.pos, s32[4096]{0:T(1024)} %order.1, bf16[4,2,128,128]{3,2,1,0:T(8,128)(2,1)} %copy-done.2, bf16[4,2,128,128]{3,2,1,0:T(8,128)(2,1)} %copy-done.9, bf16[4,2,128,128]{3,2,1,0:T(8,128)(2,1)} %copy-done.10, bf16[4,2,128,128]{3,2,1,0:T(8,128)(2,1)} %copy-done.11, ...), custom_call_target="tpu_custom_call" | custom-call | flops 268435456 | bytes 12582912 | tf_op jit(solution)/shard_map/final/pallas_call | solution.py:274
  93.4 32.4 %all_to_all.12 = bf16[32,128,128]{2,1,0:T(8,128)(2,1)S(1)} all-to-all(bf16[32,128,128]{2,1,0:T(8,128)(2,1)} %bitcast.4), channel_id=1, replica_groups=mesh['grp'=8,'row'=4,'col'=8] {'row','col'}, dimensions={0} | all-to-all | bytes 2097152 | tf_op jit(solution)/shard_map/all_to_all | solution.py:385
  125.8 1.0 copy.17
  (32 shorter events, 0.1 us)
Async XLA Ops:
  2.2 15.7 %collective-permute-start = (bf16[2,320,128]{2,1,0:T(8,128)(2,1)}, bf16[2,320,128]{2,1,0:T(8,128)(2,1)S(1)}, u32[]{:S(2)}, u32[]{:S(2)}) collective-permute-start(bf16[2,320,128]{2,1,0:T(8,128)(2,1)} %pack.1), channel_id=1, source_target_pairs={{0,4},{1,5},{2,6},{3,7},{4,0},{5,1},{6,2},{7,3},{8,12},{9,13},{10,... | collective-permute-start | bytes 491528 | tf_op jit(solution)/shard_map/ppermute | solution.py:371
  18.1 7.5 %collective-permute-start.1 = (bf16[2,320,128]{2,1,0:T(8,128)(2,1)S(1)}, bf16[2,320,128]{2,1,0:T(8,128)(2,1)S(1)}, u32[]{:S(2)}, u32[]{:S(2)}) collective-permute-start(bf16[2,320,128]{2,1,0:T(8,128)(2,1)S(1)} %get-tuple-element.52.refs_0_), channel_id=1, source_target_pairs={{0,1},{1,2},{2,3},{3,0},{4,5},{5,6},{6,7},{7,4},{8,9},{9,10},{10,1... | collective-permute-start | bytes 491528 | tf_op jit(solution)/shard_map/ppermute | solution.py:344
  19.6 7.9 %collective-permute-start.2 = (bf16[2,320,128]{2,1,0:T(8,128)(2,1)S(1)}, bf16[2,320,128]{2,1,0:T(8,128)(2,1)S(1)}, u32[]{:S(2)}, u32[]{:S(2)}) collective-permute-start(bf16[2,320,128]{2,1,0:T(8,128)(2,1)S(1)} %get-tuple-element.52.refs_0_), channel_id=1, source_target_pairs={{0,3},{1,0},{2,1},{3,2},{4,7},{5,4},{6,5},{7,6},{8,11},{9,8},{10,9... | collective-permute-start | bytes 491528 | tf_op jit(solution)/shard_map/ppermute | solution.py:344
  20.2 9.0 %collective-permute-start.3 = (bf16[2,320,128]{2,1,0:T(8,128)(2,1)S(1)}, bf16[2,320,128]{2,1,0:T(8,128)(2,1)S(1)}, u32[]{:S(2)}, u32[]{:S(2)}) collective-permute-start(bf16[2,320,128]{2,1,0:T(8,128)(2,1)S(1)} %get-tuple-element.52.refs_0_), channel_id=1, source_target_pairs={{0,2},{1,3},{2,0},{3,1},{4,6},{5,7},{6,4},{7,5},{8,10},{9,11},{10,... | collective-permute-start | bytes 491528 | tf_op jit(solution)/shard_map/ppermute | solution.py:344
  22.3 7.9 %collective-permute-start.4 = (bf16[2,320,128]{2,1,0:T(8,128)(2,1)S(1)}, bf16[2,320,128]{2,1,0:T(8,128)(2,1)S(1)}, u32[]{:S(2)}, u32[]{:S(2)}) collective-permute-start(bf16[2,320,128]{2,1,0:T(8,128)(2,1)S(1)} %get-tuple-element.56.refs_4_), channel_id=1, source_target_pairs={{0,8},{8,16},{16,24},{24,0},{1,9},{9,17},{17,25},{25,1},{2,10},{10... | collective-permute-start | bytes 491528 | tf_op jit(solution)/shard_map/ppermute | solution.py:350
  23.9 6.6 %collective-permute-start.5 = (bf16[2,320,128]{2,1,0:T(8,128)(2,1)S(1)}, bf16[2,320,128]{2,1,0:T(8,128)(2,1)S(1)}, u32[]{:S(2)}, u32[]{:S(2)}) collective-permute-start(bf16[2,320,128]{2,1,0:T(8,128)(2,1)S(1)} %get-tuple-element.56.refs_4_), channel_id=1, source_target_pairs={{0,24},{8,0},{16,8},{24,16},{1,25},{9,1},{17,9},{25,17},{2,26},{10... | collective-permute-start | bytes 491528 | tf_op jit(solution)/shard_map/ppermute | solution.py:350
  25.5 7.6 %collective-permute-start.6 = (bf16[2,320,128]{2,1,0:T(8,128)(2,1)S(1)}, bf16[2,320,128]{2,1,0:T(8,128)(2,1)S(1)}, u32[]{:S(2)}, u32[]{:S(2)}) collective-permute-start(bf16[2,320,128]{2,1,0:T(8,128)(2,1)S(1)} %get-tuple-element.56.refs_4_), channel_id=1, source_target_pairs={{0,16},{8,24},{16,0},{24,8},{1,17},{9,25},{17,1},{25,9},{2,18},{10... | collective-permute-start | bytes 491528 | tf_op jit(solution)/shard_map/ppermute | solution.py:350
  34.1 32.1 %copy-start = (bf16[4,2,192,128]{3,2,1,0:T(8,128)(2,1)}, bf16[4,2,192,128]{3,2,1,0:T(8,128)(2,1)S(1)}, u32[]{:S(2)}) copy-start(bf16[4,2,192,128]{3,2,1,0:T(8,128)(2,1)S(1)} %get-tuple-element.63.a0) | copy-start | bytes 1179652
  34.1 32.1 %copy-start.1 = (bf16[4,2,192,128]{3,2,1,0:T(8,128)(2,1)}, bf16[4,2,192,128]{3,2,1,0:T(8,128)(2,1)S(1)}, u32[]{:S(2)}) copy-start(bf16[4,2,192,128]{3,2,1,0:T(8,128)(2,1)S(1)} %get-tuple-element.67.b0) | copy-start | bytes 1179652
  34.1 46.6 %copy-start.2 = (bf16[4,2,128,128]{3,2,1,0:T(8,128)(2,1)}, bf16[4,2,128,128]{3,2,1,0:T(8,128)(2,1)S(1)}, u32[]{:S(2)}) copy-start(bf16[4,2,128,128]{3,2,1,0:T(8,128)(2,1)S(1)} %get-tuple-element.78.a0) | copy-start | bytes 786436
  34.1 46.6 %copy-start.3 = (bf16[4,2,128,128]{3,2,1,0:T(8,128)(2,1)}, bf16[4,2,128,128]{3,2,1,0:T(8,128)(2,1)S(1)}, u32[]{:S(2)}) copy-start(bf16[4,2,128,128]{3,2,1,0:T(8,128)(2,1)S(1)} %get-tuple-element.79.b0) | copy-start | bytes 786436
  34.2 13.6 %collective-permute-start.7 = (bf16[4,2,192,128]{3,2,1,0:T(8,128)(2,1)S(1)}, bf16[4,2,192,128]{3,2,1,0:T(8,128)(2,1)S(1)}, u32[]{:S(2)}, u32[]{:S(2)}) collective-permute-start(bf16[4,2,192,128]{3,2,1,0:T(8,128)(2,1)S(1)} %get-tuple-element.63.a0), channel_id=1, source_target_pairs={{0,8},{8,16},{16,24},{24,0},{1,9},{9,17},{17,25},{25,1},{2,10},{10... | collective-permute-start | bytes 1179656 | tf_op jit(solution)/shard_map/ppermute | solution.py:350
  35.3 16.5 %collective-permute-start.8 = (bf16[4,2,192,128]{3,2,1,0:T(8,128)(2,1)S(1)}, bf16[4,2,192,128]{3,2,1,0:T(8,128)(2,1)S(1)}, u32[]{:S(2)}, u32[]{:S(2)}) collective-permute-start(bf16[4,2,192,128]{3,2,1,0:T(8,128)(2,1)S(1)} %get-tuple-element.63.a0), channel_id=1, source_target_pairs={{0,24},{8,0},{16,8},{24,16},{1,25},{9,1},{17,9},{25,17},{2,26},{10... | collective-permute-start | bytes 1179656 | tf_op jit(solution)/shard_map/ppermute | solution.py:350
  37.5 15.1 %collective-permute-start.9 = (bf16[4,2,192,128]{3,2,1,0:T(8,128)(2,1)S(1)}, bf16[4,2,192,128]{3,2,1,0:T(8,128)(2,1)S(1)}, u32[]{:S(2)}, u32[]{:S(2)}) collective-permute-start(bf16[4,2,192,128]{3,2,1,0:T(8,128)(2,1)S(1)} %get-tuple-element.63.a0), channel_id=1, source_target_pairs={{0,16},{8,24},{16,0},{24,8},{1,17},{9,25},{17,1},{25,9},{2,18},{10... | collective-permute-start | bytes 1179656 | tf_op jit(solution)/shard_map/ppermute | solution.py:350
  37.6 19.7 %collective-permute-start.10 = (bf16[4,2,192,128]{3,2,1,0:T(8,128)(2,1)S(1)}, bf16[4,2,192,128]{3,2,1,0:T(8,128)(2,1)S(1)}, u32[]{:S(2)}, u32[]{:S(2)}) collective-permute-start(bf16[4,2,192,128]{3,2,1,0:T(8,128)(2,1)S(1)} %get-tuple-element.67.b0), channel_id=1, source_target_pairs={{0,1},{1,2},{2,3},{3,0},{4,5},{5,6},{6,7},{7,4},{8,9},{9,10},{10,1... | collective-permute-start | bytes 1179656 | tf_op jit(solution)/shard_map/ppermute | solution.py:344
  39.0 19.8 %collective-permute-start.11 = (bf16[4,2,192,128]{3,2,1,0:T(8,128)(2,1)S(1)}, bf16[4,2,192,128]{3,2,1,0:T(8,128)(2,1)S(1)}, u32[]{:S(2)}, u32[]{:S(2)}) collective-permute-start(bf16[4,2,192,128]{3,2,1,0:T(8,128)(2,1)S(1)} %get-tuple-element.67.b0), channel_id=1, source_target_pairs={{0,3},{1,0},{2,1},{3,2},{4,7},{5,4},{6,5},{7,6},{8,11},{9,8},{10,9... | collective-permute-start | bytes 1179656 | tf_op jit(solution)/shard_map/ppermute | solution.py:344
  47.7 18.5 %copy-start.4 = (bf16[4,2,192,128]{3,2,1,0:T(8,128)(2,1)}, bf16[4,2,192,128]{3,2,1,0:T(8,128)(2,1)S(1)}, u32[]{:S(2)}) copy-start(bf16[4,2,192,128]{3,2,1,0:T(8,128)(2,1)S(1)} %collective-permute-done.7.a1) | copy-start | bytes 1179652
  47.7 12.2 %collective-permute-start.12 = (bf16[4,2,192,128]{3,2,1,0:T(8,128)(2,1)S(1)}, bf16[4,2,192,128]{3,2,1,0:T(8,128)(2,1)}, u32[]{:S(2)}, u32[]{:S(2)}) collective-permute-start(bf16[4,2,192,128]{3,2,1,0:T(8,128)(2,1)S(1)} %get-tuple-element.67.b0), channel_id=1, source_target_pairs={{0,2},{1,3},{2,0},{3,1},{4,6},{5,7},{6,4},{7,5},{8,10},{9,11},{10,... | collective-permute-start | bytes 1179656 | tf_op jit(solution)/shard_map/ppermute | solution.py:344
  51.9 14.3 %copy-start.5 = (bf16[4,2,192,128]{3,2,1,0:T(8,128)(2,1)}, bf16[4,2,192,128]{3,2,1,0:T(8,128)(2,1)S(1)}, u32[]{:S(2)}) copy-start(bf16[4,2,192,128]{3,2,1,0:T(8,128)(2,1)S(1)} %collective-permute-done.8.a2) | copy-start | bytes 1179652
  52.6 13.6 %copy-start.6 = (bf16[4,2,192,128]{3,2,1,0:T(8,128)(2,1)}, bf16[4,2,192,128]{3,2,1,0:T(8,128)(2,1)S(1)}, u32[]{:S(2)}) copy-start(bf16[4,2,192,128]{3,2,1,0:T(8,128)(2,1)S(1)} %collective-permute-done.9.a3) | copy-start | bytes 1179652
  52.6 10.3 %collective-permute-start.13 = (bf16[4,2,128,128]{3,2,1,0:T(8,128)(2,1)S(1)}, bf16[4,2,128,128]{3,2,1,0:T(8,128)(2,1)S(1)}, u32[]{:S(2)}, u32[]{:S(2)}) collective-permute-start(bf16[4,2,128,128]{3,2,1,0:T(8,128)(2,1)S(1)} %get-tuple-element.78.a0), channel_id=1, source_target_pairs={{0,8},{8,16},{16,24},{24,0},{1,9},{9,17},{17,25},{25,1},{2,10},{10... | collective-permute-start | bytes 786440 | tf_op jit(solution)/shard_map/ppermute | solution.py:350
  55.1 25.7 %collective-permute-start.14 = (bf16[4,2,128,128]{3,2,1,0:T(8,128)(2,1)S(1)}, bf16[4,2,128,128]{3,2,1,0:T(8,128)(2,1)S(1)}, u32[]{:S(2)}, u32[]{:S(2)}) collective-permute-start(bf16[4,2,128,128]{3,2,1,0:T(8,128)(2,1)S(1)} %get-tuple-element.78.a0), channel_id=1, source_target_pairs={{0,24},{8,0},{16,8},{24,16},{1,25},{9,1},{17,9},{25,17},{2,26},{10... | collective-permute-start | bytes 786440 | tf_op jit(solution)/shard_map/ppermute | solution.py:350
  57.3 9.0 %copy-start.7 = (bf16[4,2,192,128]{3,2,1,0:T(8,128)(2,1)}, bf16[4,2,192,128]{3,2,1,0:T(8,128)(2,1)S(1)}, u32[]{:S(2)}) copy-start(bf16[4,2,192,128]{3,2,1,0:T(8,128)(2,1)S(1)} %collective-permute-done.10.b1) | copy-start | bytes 1179652
  57.3 23.6 %collective-permute-start.15 = (bf16[4,2,128,128]{3,2,1,0:T(8,128)(2,1)S(1)}, bf16[4,2,128,128]{3,2,1,0:T(8,128)(2,1)S(1)}, u32[]{:S(2)}, u32[]{:S(2)}) collective-permute-start(bf16[4,2,128,128]{3,2,1,0:T(8,128)(2,1)S(1)} %get-tuple-element.78.a0), channel_id=1, source_target_pairs={{0,16},{8,24},{16,0},{24,8},{1,17},{9,25},{17,1},{25,9},{2,18},{10... | collective-permute-start | bytes 786440 | tf_op jit(solution)/shard_map/ppermute | solution.py:350
  58.8 7.4 %copy-start.8 = (bf16[4,2,192,128]{3,2,1,0:T(8,128)(2,1)}, bf16[4,2,192,128]{3,2,1,0:T(8,128)(2,1)S(1)}, u32[]{:S(2)}) copy-start(bf16[4,2,192,128]{3,2,1,0:T(8,128)(2,1)S(1)} %collective-permute-done.11.b2) | copy-start | bytes 1179652
  58.8 22.1 %collective-permute-start.16 = (bf16[4,2,128,128]{3,2,1,0:T(8,128)(2,1)S(1)}, bf16[4,2,128,128]{3,2,1,0:T(8,128)(2,1)S(1)}, u32[]{:S(2)}, u32[]{:S(2)}) collective-permute-start(bf16[4,2,128,128]{3,2,1,0:T(8,128)(2,1)S(1)} %get-tuple-element.79.b0), channel_id=1, source_target_pairs={{0,1},{1,2},{2,3},{3,0},{4,5},{5,6},{6,7},{7,4},{8,9},{9,10},{10,1... | collective-permute-start | bytes 786440 | tf_op jit(solution)/shard_map/ppermute | solution.py:344
  59.9 21.0 %collective-permute-start.17 = (bf16[4,2,128,128]{3,2,1,0:T(8,128)(2,1)S(1)}, bf16[4,2,128,128]{3,2,1,0:T(8,128)(2,1)S(1)}, u32[]{:S(2)}, u32[]{:S(2)}) collective-permute-start(bf16[4,2,128,128]{3,2,1,0:T(8,128)(2,1)S(1)} %get-tuple-element.79.b0), channel_id=1, source_target_pairs={{0,3},{1,0},{2,1},{3,2},{4,7},{5,4},{6,5},{7,6},{8,11},{9,8},{10,9... | collective-permute-start | bytes 786440 | tf_op jit(solution)/shard_map/ppermute | solution.py:344
  62.9 17.9 %copy-start.9 = (bf16[4,2,128,128]{3,2,1,0:T(8,128)(2,1)}, bf16[4,2,128,128]{3,2,1,0:T(8,128)(2,1)S(1)}, u32[]{:S(2)}) copy-start(bf16[4,2,128,128]{3,2,1,0:T(8,128)(2,1)S(1)} %collective-permute-done.13.a1) | copy-start | bytes 786436
  62.9 18.0 %collective-permute-start.18 = (bf16[4,2,128,128]{3,2,1,0:T(8,128)(2,1)S(1)}, bf16[4,2,128,128]{3,2,1,0:T(8,128)(2,1)S(1)}, u32[]{:S(2)}, u32[]{:S(2)}) collective-permute-start(bf16[4,2,128,128]{3,2,1,0:T(8,128)(2,1)S(1)} %get-tuple-element.79.b0), channel_id=1, source_target_pairs={{0,2},{1,3},{2,0},{3,1},{4,6},{5,7},{6,4},{7,5},{8,10},{9,11},{10,... | collective-permute-start | bytes 786440 | tf_op jit(solution)/shard_map/ppermute | solution.py:344
  80.8 0.7 copy-start.10
  80.8 0.8 copy-start.11
  80.9 0.9 copy-start.12
  80.9 1.0 copy-start.13
  80.9 1.0 copy-start.14

commit v6 on v5

--- a/solution.py
+++ b/solution.py
@@ -60,7 +60,7 @@
 
 
 def sort_near_kernel(*refs):
-    parts, outs, sems = refs[:8], refs[8:12], refs[12]
+    parts, outs, sems = refs[:8], refs[8:13], refs[13]
     copies = []
     for n, ref in enumerate(parts):
         half, t = n // 4, n % 4
@@ -68,6 +68,8 @@
             pltpu.make_async_copy(ref.at[:, pl.ds(0, PART)], outs[half].at[t], sems.at[n]),
             pltpu.make_async_copy(ref.at[:, pl.ds(PART, B)], outs[2 + half].at[t], sems.at[8 + n]),
         ]
+        if half == 0:
+            copies.append(pltpu.make_async_copy(ref, outs[4].at[t], sems.at[16 + t]))
     for copy in copies:
         copy.start()
     for copy in copies:
@@ -78,10 +80,10 @@
     any_ = pl.BlockSpec(memory_space=pl.ANY)
     return pl.pallas_call(
         sort_near_kernel,
-        out_shape=[jax.ShapeDtypeStruct((4, 2, n, B), BF) for n in (PART, PART, B, B)],
+        out_shape=[jax.ShapeDtypeStruct((4, 2, n, B), BF) for n in (PART, PART, B, B, SENT)],
         in_specs=[any_] * 8,
-        out_specs=[any_] * 4,
-        scratch_shapes=[pltpu.SemaphoreType.DMA((16,))],
+        out_specs=[any_] * 5,
+        scratch_shapes=[pltpu.SemaphoreType.DMA((20,))],
         compiler_params=pltpu.CompilerParams(vmem_limit_bytes=2**20),
         name="sort_near",
     )(*near_a, *near_b)
@@ -157,7 +159,9 @@
         me = pos[0]
         row, zh, x = me // 8, (me // 4) % 2, me % 4
         copies = [
-            pltpu.make_async_copy(ref, landed.at[n], sems.at[n])
+            pltpu.make_async_copy(
+                ref.at[:, :, pl.ds(0, PART)] if n == 3 else ref, landed.at[n], sems.at[n]
+            )
             for n, ref in enumerate((a0, a1, a2, a3, b0, b1, b2, b3))
         ]
         for copy in copies:
@@ -228,7 +232,9 @@
     whole = pltpu.make_async_copy(cov_in, cov, sems.at[8])
     whole.start()
     copies = [
-        pltpu.make_async_copy(ref, landed.at[n], sems.at[n])
+        pltpu.make_async_copy(
+            ref.at[:, :, pl.ds(PART, B)] if n == 3 else ref, landed.at[n], sems.at[n]
+        )
         for n, ref in enumerate((a0, a1, a2, a3, b0, b1, b2, b3))
     ]
     for copy in copies:
@@ -374,10 +380,12 @@
     )
     half_a, half_b = fixed((jnp.stack([mine[0], other[0]]), jnp.stack([mine[1], other[1]])))
     near_a, near_b = fixed((spread(half_a, along_x), spread(half_b, along_row)))
-    near_a, near_b, sens_a, sens_b = sort_near(near_a, near_b)
-    ga, gb = spread(near_a, along_row), spread(near_b, along_x)
+    near_a, near_b, sens_a, sens_b, both_a = sort_near(near_a, near_b)
+    ga = [near_a, along_row(near_a, 1), along_row(near_a, -1), along_row(both_a, 2)]
+    gb = spread(near_b, along_x)
     sens_a, sens_b, ga = fixed((sens_a, sens_b, ga))
-    ta, tb = spread(sens_a, along_row), spread(sens_b, along_x)
+    ta = [sens_a, along_row(sens_a, 1), along_row(sens_a, -1), ga[3]]
+    tb = spread(sens_b, along_x)
     first_cross, first_diag, second_cross, second_diag, cov = late(
         me, first_index, second_positions, ga, gb, *ready
     )

time: 127 us -> 134 us (1.055)
  the two profiles are of different devices: /device:TPU:34 before, /device:TPU:66 now
where the time goes in v6:
time: 134 us; the launch traced here: 133 us
  Pallas kernels  38 us (28%)
  blocking collectives  36.9 us (28%)
  starting transfers between devices  29.8 us (22%)
  waiting for transfers between devices  24.1 us (18%)
  local copies, waits for them, and re-layouts  3.74 us (3%)
    all_to_all x1, blocking collectives, local(): lax.all_to_all(products, ('row', 'col'), split_axis=0, concat_axis=0, til...  36.9 us
    ppermute x8, waiting for transfers between devices, along_row(): return lax.ppermute(v, 'row', [(r, (r + k) % 4) for r in range(4)])  23.4 us
    pallas_call x1, Pallas kernels, late(): pl.pallas_call(late_kernel, grid=(steps,), out_shape=(jax.ShapeDtypeStruc...  14.5 us
    ppermute x9, starting transfers between devices, along_x(): lax.ppermute(v, 'col', [(z * 4 + x, z * 4 + (x + k) % 4) for z in range(2...  13 us
    pallas_call x1, Pallas kernels, final(): pl.pallas_call(final_kernel, out_shape=jax.ShapeDtypeStruct((n // 2, B),...  11.5 us
    ppermute x8, starting transfers between devices, along_row(): return lax.ppermute(v, 'row', [(r, (r + k) % 4) for r in range(4)])  11.4 us
    pallas_call x1, Pallas kernels, early(): pl.pallas_call(early_kernel, grid=(n // KIDS,), out_shape=(jax.ShapeDtype...  8.51 us
    ppermute x1, starting transfers between devices, local(): other = lax.ppermute(mine, 'col', [(c, (c + 4) % 8) for c in range(8)])  5.39 us
  transfers between devices with their start and end apart: 18, of which 7 were waited for; matrix products, arithmetic and copies ran while one was open for 1% of the time, Pallas kernels for 17%

profile of v6, /device:TPU:66, one launch (start us, length us, event | category | flops | bytes accessed | tf_op | source)
XLA Modules:
  0.0 133.4 jit_solution(3032142398135482357)
XLA Ops:
  0.6 1.6 %pack.1 = bf16[2,320,128]{2,1,0:T(8,128)(2,1)} custom-call(s32[1]{0:T(128)} %bitcast.pos, bf16[48,1536]{1,0:T(8,128)(2,1)} %x_ref.1, bf16[1,256,128]{2,1,0:T(8,128)(2,1)} %s_ref.1), custom_call_target="tpu_custom_call" | custom-call | tf_op jit(solution)/shard_map/pack/pallas_call | solution.py:49
  2.3 5.4 %collective-permute-start = (bf16[2,320,128]{2,1,0:T(8,128)(2,1)}, bf16[2,320,128]{2,1,0:T(8,128)(2,1)S(1)}, u32[]{:S(2)}, u32[]{:S(2)}) collective-permute-start(bf16[2,320,128]{2,1,0:T(8,128)(2,1)} %pack.1), channel_id=1, source_target_pairs={{0,4},{1,5},{2,6},{3,7},{4,0},{5,1},{6,2},{7,3},{8,12},{9,13},{10,... | collective-permute-start | bytes 491528 | tf_op jit(solution)/shard_map/ppermute | solution.py:377
  7.7 1.0 fusion
  8.6 8.5 %early.1 = (bf16[1024,128]{1,0:T(8,128)(2,1)}, bf16[128,1024]{1,0:T(8,128)(2,1)}, f32[128,128]{1,0:T(8,128)}, bf16[32,512,128]{2,1,0:T(8,128)(2,1)}, bf16[32,128...) custom-call(bf16[1,8,128,128]{3,2,1,0:T(8,128)(2,1)} %fp.1, bf16[1,128,128]{2,1,0:T(8,128)(2,1)} %fi.1, ...), custom_call_target="tpu_custom_call" | custom-call | flops 1258291200 | bytes 20971520 | tf_op jit(solution)/shard_map/early/pallas_call | solution.py:116
  17.1 0.0 collective-permute-done
  17.2 2.2 %collective-permute-start.3 = (bf16[2,320,128]{2,1,0:T(8,128)(2,1)S(1)}, bf16[2,320,128]{2,1,0:T(8,128)(2,1)S(1)}, u32[]{:S(2)}, u32[]{:S(2)}) collective-permute-start(bf16[2,320,128]{2,1,0:T(8,128)(2,1)S(1)} %get-tuple-element.53.refs_0_), channel_id=1, source_target_pairs={{0,2},{1,3},{2,0},{3,1},{4,6},{5,7},{6,4},{7,5},{8,10},{9,11},{10,... | collective-permute-start | bytes 491528 | tf_op jit(solution)/shard_map/ppermute | solution.py:350
  19.4 1.4 %collective-permute-start.2 = (bf16[2,320,128]{2,1,0:T(8,128)(2,1)S(1)}, bf16[2,320,128]{2,1,0:T(8,128)(2,1)S(1)}, u32[]{:S(2)}, u32[]{:S(2)}) collective-permute-start(bf16[2,320,128]{2,1,0:T(8,128)(2,1)S(1)} %get-tuple-element.53.refs_0_), channel_id=1, source_target_pairs={{0,3},{1,0},{2,1},{3,2},{4,7},{5,4},{6,5},{7,6},{8,11},{9,8},{10,9... | collective-permute-start | bytes 491528 | tf_op jit(solution)/shard_map/ppermute | solution.py:350
  20.8 0.6 collective-permute-start.1
  21.4 3.2 %collective-permute-start.6 = (bf16[2,320,128]{2,1,0:T(8,128)(2,1)S(1)}, bf16[2,320,128]{2,1,0:T(8,128)(2,1)S(1)}, u32[]{:S(2)}, u32[]{:S(2)}) collective-permute-start(bf16[2,320,128]{2,1,0:T(8,128)(2,1)S(1)} %get-tuple-element.57.refs_4_), channel_id=1, source_target_pairs={{0,16},{8,24},{16,0},{24,8},{1,17},{9,25},{17,1},{25,9},{2,18},{10... | collective-permute-start | bytes 491528 | tf_op jit(solution)/shard_map/ppermute | solution.py:356
  24.6 1.1 collective-permute-start.5
  25.7 0.3 collective-permute-done.3.refs_3_
  25.9 1.6 %collective-permute-start.4 = (bf16[2,320,128]{2,1,0:T(8,128)(2,1)S(1)}, bf16[2,320,128]{2,1,0:T(8,128)(2,1)S(1)}, u32[]{:S(2)}, u32[]{:S(2)}) collective-permute-start(bf16[2,320,128]{2,1,0:T(8,128)(2,1)S(1)} %get-tuple-element.57.refs_4_), channel_id=1, source_target_pairs={{0,8},{8,16},{16,24},{24,0},{1,9},{9,17},{17,25},{25,1},{2,10},{10... | collective-permute-start | bytes 491528 | tf_op jit(solution)/shard_map/ppermute | solution.py:356
  27.5 0.4 collective-permute-done.2.refs_2_
  28.0 0.0 collective-permute-done.1.refs_1_
  28.0 0.7 collective-permute-done.6.refs_7_
  28.7 2.9 %collective-permute-done.5.refs_6_ = bf16[2,320,128]{2,1,0:T(8,128)(2,1)S(1)} collective-permute-done((bf16[2,320,128]{2,1,0:T(8,128)(2,1)S(1)}, bf16[2,320,128]{2,1,0:T(8,128)(2,1)S(1)}, u32[]{:S(2)}, u32[]{:S(2)}) %collective-permute-start.5) | collective-permute-done | bytes 163872 | tf_op jit(solution)/shard_map/ppermute | solution.py:356
  31.6 0.9 collective-permute-done.4.refs_5_
  32.5 1.9 %sort_near.1 = (bf16[4,2,192,128]{3,2,1,0:T(8,128)(2,1)S(1)}, bf16[4,2,192,128]{3,2,1,0:T(8,128)(2,1)S(1)}, bf16[4,2,128,128]{3,2,1,0:T(8,128)(2,1)S(1)}, bf16[4...) custom-call(bf16[2,320,128]{2,1,0:T(8,128)(2,1)S(1)} %get-tuple-element.53.refs_0_, ...), custom_call_target="tpu_custom_call" | custom-call | tf_op jit(solution)/shard_map/sort_near/pallas_call | solution.py:81
  34.4 0.0 copy-start
  34.4 1.9 %collective-permute-start.8 = (bf16[4,2,192,128]{3,2,1,0:T(8,128)(2,1)S(1)}, bf16[4,2,192,128]{3,2,1,0:T(8,128)(2,1)S(1)}, u32[]{:S(2)}, u32[]{:S(2)}) collective-permute-start(bf16[4,2,192,128]{3,2,1,0:T(8,128)(2,1)S(1)} %get-tuple-element.65.a0), channel_id=1, source_target_pairs={{0,24},{8,0},{16,8},{24,16},{1,25},{9,1},{17,9},{25,17},{2,26},{10... | collective-permute-start | bytes 1179656 | tf_op jit(solution)/shard_map/ppermute | solution.py:356
  36.3 0.7 collective-permute-start.9
  37.0 0.9 collective-permute-start.7
  37.9 2.6 %collective-permute-start.12 = (bf16[4,2,192,128]{3,2,1,0:T(8,128)(2,1)S(1)}, bf16[4,2,192,128]{3,2,1,0:T(8,128)(2,1)}, u32[]{:S(2)}, u32[]{:S(2)}) collective-permute-start(bf16[4,2,192,128]{3,2,1,0:T(8,128)(2,1)S(1)} %get-tuple-element.69.b0), channel_id=1, source_target_pairs={{0,2},{1,3},{2,0},{3,1},{4,6},{5,7},{6,4},{7,5},{8,10},{9,11},{10,... | collective-permute-start | bytes 1179656 | tf_op jit(solution)/shard_map/ppermute | solution.py:350
  40.5 0.9 collective-permute-start.11
  41.4 16.5 %collective-permute-done.8.a2 = bf16[4,2,192,128]{3,2,1,0:T(8,128)(2,1)S(1)} collective-permute-done((bf16[4,2,192,128]{3,2,1,0:T(8,128)(2,1)S(1)}, bf16[4,2,192,128]{3,2,1,0:T(8,128)(2,1)S(1)}, u32[]{:S(2)}, u32[]{:S(2)}) %collective-permute-start.8) | collective-permute-done | bytes 393248 | tf_op jit(solution)/shard_map/ppermute | solution.py:356
  57.9 0.6 collective-permute-start.10
  58.5 0.1 copy.15
  58.6 0.7 reshape.21.spos
  59.3 2.4 %collective-permute-done.7.a1 = bf16[4,2,192,128]{3,2,1,0:T(8,128)(2,1)S(1)} collective-permute-done((bf16[4,2,192,128]{3,2,1,0:T(8,128)(2,1)S(1)}, bf16[4,2,192,128]{3,2,1,0:T(8,128)(2,1)S(1)}, u32[]{:S(2)}, u32[]{:S(2)}) %collective-permute-start.7) | collective-permute-done | bytes 393248 | tf_op jit(solution)/shard_map/ppermute | solution.py:356
  61.6 0.0 collective-permute-done.9.a3
  61.7 1.4 %collective-permute-start.14 = (bf16[4,2,128,128]{3,2,1,0:T(8,128)(2,1)S(1)}, bf16[4,2,128,128]{3,2,1,0:T(8,128)(2,1)S(1)}, u32[]{:S(2)}, u32[]{:S(2)}) collective-permute-start(bf16[4,2,128,128]{3,2,1,0:T(8,128)(2,1)S(1)} %get-tuple-element.80.a0), channel_id=1, source_target_pairs={{0,24},{8,0},{16,8},{24,16},{1,25},{9,1},{17,9},{25,17},{2,26},{10... | collective-permute-start | bytes 786440 | tf_op jit(solution)/shard_map/ppermute | solution.py:356
  63.1 0.7 collective-permute-start.13
  63.8 0.0 collective-permute-done.12.b3
  63.8 2.6 %collective-permute-start.17 = (bf16[4,2,128,128]{3,2,1,0:T(8,128)(2,1)S(1)}, bf16[4,2,128,128]{3,2,1,0:T(8,128)(2,1)S(1)}, u32[]{:S(2)}, u32[]{:S(2)}) collective-permute-start(bf16[4,2,128,128]{3,2,1,0:T(8,128)(2,1)S(1)} %get-tuple-element.81.b0), channel_id=1, source_target_pairs={{0,2},{1,3},{2,0},{3,1},{4,6},{5,7},{6,4},{7,5},{8,10},{9,11},{10,... | collective-permute-start | bytes 786440 | tf_op jit(solution)/shard_map/ppermute | solution.py:350
  66.4 1.4 %collective-permute-start.16 = (bf16[4,2,128,128]{3,2,1,0:T(8,128)(2,1)S(1)}, bf16[4,2,128,128]{3,2,1,0:T(8,128)(2,1)S(1)}, u32[]{:S(2)}, u32[]{:S(2)}) collective-permute-start(bf16[4,2,128,128]{3,2,1,0:T(8,128)(2,1)S(1)} %get-tuple-element.81.b0), channel_id=1, source_target_pairs={{0,3},{1,0},{2,1},{3,2},{4,7},{5,4},{6,5},{7,6},{8,11},{9,8},{10,9... | collective-permute-start | bytes 786440 | tf_op jit(solution)/shard_map/ppermute | solution.py:350
  67.8 0.0 collective-permute-done.10.b1
  67.8 0.6 collective-permute-start.15
  68.4 14.5 %late.1 = (bf16[1,8,128,128]{3,2,1,0:T(8,128)(2,1)}, bf16[1,128,128]{2,1,0:T(8,128)(2,1)}, bf16[32,4,128,128]{3,2,1,0:T(8,128)(2,1)}, bf16[32,128,128]{2,1,0:T(8,128)(2,1)}, f32[8192,128]{1,0:T(8,128)}) custom-call(s32[1]{0:T(128)} %bitcast.pos, s32[1,8]{1,0:T(1,128)} %fidx.1, s32[96]{0:T(128)} %reshape.21.spos, bf16[4,2,192,128]{3,2,1,0:T(8,128)(2,1)} %copy-done, ...), custom_call_target="tpu_custom_call" | custom-call | flops 3019898880 | bytes 33554432 | tf_op jit(solution)/shard_map/late/pallas_call | solution.py:308
  83.0 0.0 collective-permute-done.13.a1
  83.0 0.0 collective-permute-done.17.b3
  83.1 0.6 copy-done.7
  83.7 0.1 copy-done.8
  83.8 0.1 copy-done.9
  83.9 0.1 copy-done.10
  84.0 0.1 copy-done.11
  84.1 11.5 %final.1 = bf16[4096,128]{1,0:T(8,128)(2,1)} custom-call(s32[1]{0:T(128)} %bitcast.pos, s32[4096]{0:T(1024)} %order.1, bf16[4,2,128,128]{3,2,1,0:T(8,128)(2,1)} %copy-done.2, bf16[4,2,128,128]{3,2,1,0:T(8,128)(2,1)} %copy-done.8, bf16[4,2,128,128]{3,2,1,0:T(8,128)(2,1)} %copy-done.7, bf16[4,2,320,128]{3,2,1,0:T(8,128)(2,1)} %copy-done.4, ...), custom_call_target="tpu_custom_call" | custom-call | flops 268435456 | bytes 12582912 | tf_op jit(solution)/shard_map/final/pallas_call | solution.py:280
  95.5 36.9 %all_to_all.12 = bf16[32,128,128]{2,1,0:T(8,128)(2,1)S(1)} all-to-all(bf16[32,128,128]{2,1,0:T(8,128)(2,1)} %bitcast.4), channel_id=1, replica_groups=mesh['grp'=8,'row'=4,'col'=8] {'row','col'}, dimensions={0} | all-to-all | bytes 2097152 | tf_op jit(solution)/shard_map/all_to_all | solution.py:393
  132.4 1.0 copy.17
  (26 shorter events, 0.1 us)
Async XLA Ops:
  0.6 57.9 %copy-start.12 = (s32[32,3]{0,1:T(4,128)S(1)}, s32[32,3]{0,1:T(4,128)}, u32[]{:S(2)}) copy-start(s32[32,3]{0,1:T(4,128)} %param.15) | copy-start | bytes 1156
  2.3 14.9 %collective-permute-start = (bf16[2,320,128]{2,1,0:T(8,128)(2,1)}, bf16[2,320,128]{2,1,0:T(8,128)(2,1)S(1)}, u32[]{:S(2)}, u32[]{:S(2)}) collective-permute-start(bf16[2,320,128]{2,1,0:T(8,128)(2,1)} %pack.1), channel_id=1, source_target_pairs={{0,4},{1,5},{2,6},{3,7},{4,0},{5,1},{6,2},{7,3},{8,12},{9,13},{10,... | collective-permute-start | bytes 491528 | tf_op jit(solution)/shard_map/ppermute | solution.py:377
  17.2 8.7 %collective-permute-start.3 = (bf16[2,320,128]{2,1,0:T(8,128)(2,1)S(1)}, bf16[2,320,128]{2,1,0:T(8,128)(2,1)S(1)}, u32[]{:S(2)}, u32[]{:S(2)}) collective-permute-start(bf16[2,320,128]{2,1,0:T(8,128)(2,1)S(1)} %get-tuple-element.53.refs_0_), channel_id=1, source_target_pairs={{0,2},{1,3},{2,0},{3,1},{4,6},{5,7},{6,4},{7,5},{8,10},{9,11},{10,... | collective-permute-start | bytes 491528 | tf_op jit(solution)/shard_map/ppermute | solution.py:350
  19.4 8.5 %collective-permute-start.2 = (bf16[2,320,128]{2,1,0:T(8,128)(2,1)S(1)}, bf16[2,320,128]{2,1,0:T(8,128)(2,1)S(1)}, u32[]{:S(2)}, u32[]{:S(2)}) collective-permute-start(bf16[2,320,128]{2,1,0:T(8,128)(2,1)S(1)} %get-tuple-element.53.refs_0_), channel_id=1, source_target_pairs={{0,3},{1,0},{2,1},{3,2},{4,7},{5,4},{6,5},{7,6},{8,11},{9,8},{10,9... | collective-permute-start | bytes 491528 | tf_op jit(solution)/shard_map/ppermute | solution.py:350
  20.8 7.1 %collective-permute-start.1 = (bf16[2,320,128]{2,1,0:T(8,128)(2,1)S(1)}, bf16[2,320,128]{2,1,0:T(8,128)(2,1)S(1)}, u32[]{:S(2)}, u32[]{:S(2)}) collective-permute-start(bf16[2,320,128]{2,1,0:T(8,128)(2,1)S(1)} %get-tuple-element.53.refs_0_), channel_id=1, source_target_pairs={{0,1},{1,2},{2,3},{3,0},{4,5},{5,6},{6,7},{7,4},{8,9},{9,10},{10,1... | collective-permute-start | bytes 491528 | tf_op jit(solution)/shard_map/ppermute | solution.py:350
  21.4 7.3 %collective-permute-start.6 = (bf16[2,320,128]{2,1,0:T(8,128)(2,1)S(1)}, bf16[2,320,128]{2,1,0:T(8,128)(2,1)S(1)}, u32[]{:S(2)}, u32[]{:S(2)}) collective-permute-start(bf16[2,320,128]{2,1,0:T(8,128)(2,1)S(1)} %get-tuple-element.57.refs_4_), channel_id=1, source_target_pairs={{0,16},{8,24},{16,0},{24,8},{1,17},{9,25},{17,1},{25,9},{2,18},{10... | collective-permute-start | bytes 491528 | tf_op jit(solution)/shard_map/ppermute | solution.py:356
  24.6 7.0 %collective-permute-start.5 = (bf16[2,320,128]{2,1,0:T(8,128)(2,1)S(1)}, bf16[2,320,128]{2,1,0:T(8,128)(2,1)S(1)}, u32[]{:S(2)}, u32[]{:S(2)}) collective-permute-start(bf16[2,320,128]{2,1,0:T(8,128)(2,1)S(1)} %get-tuple-element.57.refs_4_), channel_id=1, source_target_pairs={{0,24},{8,0},{16,8},{24,16},{1,25},{9,1},{17,9},{25,17},{2,26},{10... | collective-permute-start | bytes 491528 | tf_op jit(solution)/shard_map/ppermute | solution.py:356
  25.9 6.5 %collective-permute-start.4 = (bf16[2,320,128]{2,1,0:T(8,128)(2,1)S(1)}, bf16[2,320,128]{2,1,0:T(8,128)(2,1)S(1)}, u32[]{:S(2)}, u32[]{:S(2)}) collective-permute-start(bf16[2,320,128]{2,1,0:T(8,128)(2,1)S(1)} %get-tuple-element.57.refs_4_), channel_id=1, source_target_pairs={{0,8},{8,16},{16,24},{24,0},{1,9},{9,17},{17,25},{25,1},{2,10},{10... | collective-permute-start | bytes 491528 | tf_op jit(solution)/shard_map/ppermute | solution.py:356
  34.4 34.1 %copy-start = (bf16[4,2,192,128]{3,2,1,0:T(8,128)(2,1)}, bf16[4,2,192,128]{3,2,1,0:T(8,128)(2,1)S(1)}, u32[]{:S(2)}) copy-start(bf16[4,2,192,128]{3,2,1,0:T(8,128)(2,1)S(1)} %get-tuple-element.65.a0) | copy-start | bytes 1179652
  34.4 34.0 %copy-start.1 = (bf16[4,2,192,128]{3,2,1,0:T(8,128)(2,1)}, bf16[4,2,192,128]{3,2,1,0:T(8,128)(2,1)S(1)}, u32[]{:S(2)}) copy-start(bf16[4,2,192,128]{3,2,1,0:T(8,128)(2,1)S(1)} %get-tuple-element.69.b0) | copy-start | bytes 1179652
  34.4 48.6 %copy-start.2 = (bf16[4,2,128,128]{3,2,1,0:T(8,128)(2,1)}, bf16[4,2,128,128]{3,2,1,0:T(8,128)(2,1)S(1)}, u32[]{:S(2)}) copy-start(bf16[4,2,128,128]{3,2,1,0:T(8,128)(2,1)S(1)} %get-tuple-element.80.a0) | copy-start | bytes 786436
  34.4 48.6 %copy-start.3 = (bf16[4,2,128,128]{3,2,1,0:T(8,128)(2,1)}, bf16[4,2,128,128]{3,2,1,0:T(8,128)(2,1)S(1)}, u32[]{:S(2)}) copy-start(bf16[4,2,128,128]{3,2,1,0:T(8,128)(2,1)S(1)} %get-tuple-element.81.b0) | copy-start | bytes 786436
  34.4 23.5 %collective-permute-start.8 = (bf16[4,2,192,128]{3,2,1,0:T(8,128)(2,1)S(1)}, bf16[4,2,192,128]{3,2,1,0:T(8,128)(2,1)S(1)}, u32[]{:S(2)}, u32[]{:S(2)}) collective-permute-start(bf16[4,2,192,128]{3,2,1,0:T(8,128)(2,1)S(1)} %get-tuple-element.65.a0), channel_id=1, source_target_pairs={{0,24},{8,0},{16,8},{24,16},{1,25},{9,1},{17,9},{25,17},{2,26},{10... | collective-permute-start | bytes 1179656 | tf_op jit(solution)/shard_map/ppermute | solution.py:356
  36.3 25.3 %collective-permute-start.9 = (bf16[4,2,320,128]{3,2,1,0:T(8,128)(2,1)S(1)}, bf16[4,2,320,128]{3,2,1,0:T(8,128)(2,1)S(1)}, u32[]{:S(2)}, u32[]{:S(2)}) collective-permute-start(bf16[4,2,320,128]{3,2,1,0:T(8,128)(2,1)S(1)} %get-tuple-element.64), channel_id=1, source_target_pairs={{0,16},{8,24},{16,0},{24,8},{1,17},{9,25},{17,1},{25,9},{2,18},{10... | collective-permute-start | bytes 1966088 | tf_op jit(solution)/shard_map/ppermute | solution.py:356
  37.0 24.6 %collective-permute-start.7 = (bf16[4,2,192,128]{3,2,1,0:T(8,128)(2,1)S(1)}, bf16[4,2,192,128]{3,2,1,0:T(8,128)(2,1)S(1)}, u32[]{:S(2)}, u32[]{:S(2)}) collective-permute-start(bf16[4,2,192,128]{3,2,1,0:T(8,128)(2,1)S(1)} %get-tuple-element.65.a0), channel_id=1, source_target_pairs={{0,8},{8,16},{16,24},{24,0},{1,9},{9,17},{17,25},{25,1},{2,10},{10... | collective-permute-start | bytes 1179656 | tf_op jit(solution)/shard_map/ppermute | solution.py:356
  37.9 25.9 %collective-permute-start.12 = (bf16[4,2,192,128]{3,2,1,0:T(8,128)(2,1)S(1)}, bf16[4,2,192,128]{3,2,1,0:T(8,128)(2,1)}, u32[]{:S(2)}, u32[]{:S(2)}) collective-permute-start(bf16[4,2,192,128]{3,2,1,0:T(8,128)(2,1)S(1)} %get-tuple-element.69.b0), channel_id=1, source_target_pairs={{0,2},{1,3},{2,0},{3,1},{4,6},{5,7},{6,4},{7,5},{8,10},{9,11},{10,... | collective-permute-start | bytes 1179656 | tf_op jit(solution)/shard_map/ppermute | solution.py:350
  40.5 25.9 %collective-permute-start.11 = (bf16[4,2,192,128]{3,2,1,0:T(8,128)(2,1)S(1)}, bf16[4,2,192,128]{3,2,1,0:T(8,128)(2,1)}, u32[]{:S(2)}, u32[]{:S(2)}) collective-permute-start(bf16[4,2,192,128]{3,2,1,0:T(8,128)(2,1)S(1)} %get-tuple-element.69.b0), channel_id=1, source_target_pairs={{0,3},{1,0},{2,1},{3,2},{4,7},{5,4},{6,5},{7,6},{8,11},{9,8},{10,9... | collective-permute-start | bytes 1179656 | tf_op jit(solution)/shard_map/ppermute | solution.py:350
  57.9 10.5 %copy-start.5 = (bf16[4,2,192,128]{3,2,1,0:T(8,128)(2,1)}, bf16[4,2,192,128]{3,2,1,0:T(8,128)(2,1)S(1)}, u32[]{:S(2)}) copy-start(bf16[4,2,192,128]{3,2,1,0:T(8,128)(2,1)S(1)} %collective-permute-done.8.a2) | copy-start | bytes 1179652
  57.9 9.8 %collective-permute-start.10 = (bf16[4,2,192,128]{3,2,1,0:T(8,128)(2,1)S(1)}, bf16[4,2,192,128]{3,2,1,0:T(8,128)(2,1)}, u32[]{:S(2)}, u32[]{:S(2)}) collective-permute-start(bf16[4,2,192,128]{3,2,1,0:T(8,128)(2,1)S(1)} %get-tuple-element.69.b0), channel_id=1, source_target_pairs={{0,1},{1,2},{2,3},{3,0},{4,5},{5,6},{6,7},{7,4},{8,9},{9,10},{10,1... | collective-permute-start | bytes 1179656 | tf_op jit(solution)/shard_map/ppermute | solution.py:350
  61.6 6.8 %copy-start.6 = (bf16[4,2,192,128]{3,2,1,0:T(8,128)(2,1)}, bf16[4,2,192,128]{3,2,1,0:T(8,128)(2,1)S(1)}, u32[]{:S(2)}) copy-start(bf16[4,2,192,128]{3,2,1,0:T(8,128)(2,1)S(1)} %collective-permute-done.7.a1) | copy-start | bytes 1179652
  61.6 6.8 %copy-start.4 = (bf16[4,2,320,128]{3,2,1,0:T(8,128)(2,1)}, bf16[4,2,320,128]{3,2,1,0:T(8,128)(2,1)S(1)}, u32[]{:S(2)}) copy-start(bf16[4,2,320,128]{3,2,1,0:T(8,128)(2,1)S(1)} %collective-permute-done.9.a3) | copy-start | bytes 1966084
  61.7 21.3 %collective-permute-start.14 = (bf16[4,2,128,128]{3,2,1,0:T(8,128)(2,1)S(1)}, bf16[4,2,128,128]{3,2,1,0:T(8,128)(2,1)S(1)}, u32[]{:S(2)}, u32[]{:S(2)}) collective-permute-start(bf16[4,2,128,128]{3,2,1,0:T(8,128)(2,1)S(1)} %get-tuple-element.80.a0), channel_id=1, source_target_pairs={{0,24},{8,0},{16,8},{24,16},{1,25},{9,1},{17,9},{25,17},{2,26},{10... | collective-permute-start | bytes 786440 | tf_op jit(solution)/shard_map/ppermute | solution.py:356
  63.1 19.9 %collective-permute-start.13 = (bf16[4,2,128,128]{3,2,1,0:T(8,128)(2,1)S(1)}, bf16[4,2,128,128]{3,2,1,0:T(8,128)(2,1)S(1)}, u32[]{:S(2)}, u32[]{:S(2)}) collective-permute-start(bf16[4,2,128,128]{3,2,1,0:T(8,128)(2,1)S(1)} %get-tuple-element.80.a0), channel_id=1, source_target_pairs={{0,8},{8,16},{16,24},{24,0},{1,9},{9,17},{17,25},{25,1},{2,10},{10... | collective-permute-start | bytes 786440 | tf_op jit(solution)/shard_map/ppermute | solution.py:356
  63.8 19.3 %collective-permute-start.17 = (bf16[4,2,128,128]{3,2,1,0:T(8,128)(2,1)S(1)}, bf16[4,2,128,128]{3,2,1,0:T(8,128)(2,1)S(1)}, u32[]{:S(2)}, u32[]{:S(2)}) collective-permute-start(bf16[4,2,128,128]{3,2,1,0:T(8,128)(2,1)S(1)} %get-tuple-element.81.b0), channel_id=1, source_target_pairs={{0,2},{1,3},{2,0},{3,1},{4,6},{5,7},{6,4},{7,5},{8,10},{9,11},{10,... | collective-permute-start | bytes 786440 | tf_op jit(solution)/shard_map/ppermute | solution.py:350
  66.4 16.7 %collective-permute-start.16 = (bf16[4,2,128,128]{3,2,1,0:T(8,128)(2,1)S(1)}, bf16[4,2,128,128]{3,2,1,0:T(8,128)(2,1)S(1)}, u32[]{:S(2)}, u32[]{:S(2)}) collective-permute-start(bf16[4,2,128,128]{3,2,1,0:T(8,128)(2,1)S(1)} %get-tuple-element.81.b0), channel_id=1, source_target_pairs={{0,3},{1,0},{2,1},{3,2},{4,7},{5,4},{6,5},{7,6},{8,11},{9,8},{10,9... | collective-permute-start | bytes 786440 | tf_op jit(solution)/shard_map/ppermute | solution.py:350
  67.8 15.3 %collective-permute-start.15 = (bf16[4,2,128,128]{3,2,1,0:T(8,128)(2,1)S(1)}, bf16[4,2,128,128]{3,2,1,0:T(8,128)(2,1)S(1)}, u32[]{:S(2)}, u32[]{:S(2)}) collective-permute-start(bf16[4,2,128,128]{3,2,1,0:T(8,128)(2,1)S(1)} %get-tuple-element.81.b0), channel_id=1, source_target_pairs={{0,1},{1,2},{2,3},{3,0},{4,5},{5,6},{6,7},{7,4},{8,9},{9,10},{10,1... | collective-permute-start | bytes 786440 | tf_op jit(solution)/shard_map/ppermute | solution.py:350
  83.0 0.7 copy-start.7
  83.0 0.8 copy-start.8
  83.0 0.9 copy-start.9
  83.0 0.9 copy-start.10
  83.1 1.0 copy-start.11

commit v7 on v3

--- a/solution.py
+++ b/solution.py
@@ -60,7 +60,7 @@
     )(me.reshape(1), x, sens)
 
 
-KIDS = 8
+KIDS = 16
 
 
 def early_kernel(fp, fi, sp, si, fu, fut, fw, su, sut, sw):
@@ -112,7 +112,7 @@
         cost_estimate=pl.CostEstimate(
             flops=300 * 2 * B**3, bytes_accessed=20 * 2**20, transcendentals=0
         ),
-        compiler_params=pltpu.CompilerParams(vmem_limit_bytes=12 * 2**20),
+        compiler_params=pltpu.CompilerParams(vmem_limit_bytes=20 * 2**20),
         name="early",
     )(fp, fi, sp, si)
 
@@ -270,7 +270,7 @@
         cost_estimate=pl.CostEstimate(
             flops=720 * 2 * B**3, bytes_accessed=20 * 2**20, transcendentals=0
         ),
-        compiler_params=pltpu.CompilerParams(vmem_limit_bytes=30 * 2**20),
+        compiler_params=pltpu.CompilerParams(vmem_limit_bytes=36 * 2**20),
         name="late",
     )(me.reshape(1), fidx, spos.reshape(-1), order, *ga, *gb, fu, fut, fw, su, sut, sw)
 

time: 126 us -> 126 us (level)
  no operation moved by 1% of the time
where the time goes in v7:
time: 126 us; the launch traced here: 124 us
  blocking collectives  38.9 us (31%)
  waiting for transfers between devices  30.2 us (24%)
  starting transfers between devices  25.5 us (20%)
  Pallas kernels  24.1 us (19%)
  local copies, waits for them, and re-layouts  4.36 us (3%)
    all_to_all x1, blocking collectives, local(): lax.all_to_all(products, ('row', 'col'), split_axis=0, concat_axis=0, til...  38.9 us
    ppermute x6, waiting for transfers between devices, along_row(): return lax.ppermute(v, 'row', [(r, (r + k) % 4) for r in range(4)])  19.8 us
    pallas_call x1, Pallas kernels, late(): pl.pallas_call(functools.partial(late_kernel, steps), grid=(steps + 1,),...  19 us
    ppermute x6, starting transfers between devices, along_row(): return lax.ppermute(v, 'row', [(r, (r + k) % 4) for r in range(4)])  9.92 us
    ppermute x6, starting transfers between devices, along_x(): lax.ppermute(v, 'col', [(z * 4 + x, z * 4 + (x + k) % 4) for z in range(2...  9.28 us
    ppermute x1, waiting for transfers between devices, local(): other = lax.ppermute(mine, 'col', [(c, (c + 4) % 8) for c in range(8)])  6.7 us
    ppermute x1, starting transfers between devices, local(): other = lax.ppermute(mine, 'col', [(c, (c + 4) % 8) for c in range(8)])  6.29 us
    ppermute x6, waiting for transfers between devices, along_x(): lax.ppermute(v, 'col', [(z * 4 + x, z * 4 + (x + k) % 4) for z in range(2...  3.69 us
  transfers between devices with their start and end apart: 13, of which 9 were waited for; matrix products, arithmetic and copies ran while one was open for 1% of the time, Pallas kernels for 3%

profile of v7, /device:TPU:34, one launch (start us, length us, event | category | flops | bytes accessed | tf_op | source)
XLA Modules:
  0.0 124.0 jit_solution(10611499315591548454)
XLA Ops:
  0.6 0.0 copy-start.6
  0.6 0.0 copy-start.1
  0.7 0.0 copy-start.3
  0.7 0.0 copy-start.2
  0.7 1.7 %pack.1 = bf16[2,320,128]{2,1,0:T(8,128)(2,1)} custom-call(s32[1]{0:T(128)} %bitcast.pos, bf16[48,1536]{1,0:T(8,128)(2,1)} %x_ref.1, bf16[1,256,128]{2,1,0:T(8,128)(2,1)} %s_ref.1), custom_call_target="tpu_custom_call" | custom-call | tf_op jit(solution)/shard_map/pack/pallas_call | solution.py:50
  2.4 6.3 %collective-permute-start = (bf16[2,320,128]{2,1,0:T(8,128)(2,1)}, bf16[2,320,128]{2,1,0:T(8,128)(2,1)S(1)}, u32[]{:S(2)}, u32[]{:S(2)}) collective-permute-start(bf16[2,320,128]{2,1,0:T(8,128)(2,1)} %pack.1), channel_id=1, source_target_pairs={{0,4},{1,5},{2,6},{3,7},{4,0},{5,1},{6,2},{7,3},{8,12},{9,13},{10,... | collective-permute-start | bytes 491528 | tf_op jit(solution)/shard_map/ppermute | solution.py:306
  8.7 1.0 fusion
  9.7 6.7 %collective-permute-done = bf16[2,320,128]{2,1,0:T(8,128)(2,1)S(1)} collective-permute-done((bf16[2,320,128]{2,1,0:T(8,128)(2,1)}, bf16[2,320,128]{2,1,0:T(8,128)(2,1)S(1)}, u32[]{:S(2)}, u32[]{:S(2)}) %collective-permute-start) | collective-permute-done | bytes 163872 | tf_op jit(solution)/shard_map/ppermute | solution.py:306
  16.4 0.0 copy-start.4
  16.4 0.0 copy-start.5
  16.4 2.2 %collective-permute-start.3 = (bf16[2,320,128]{2,1,0:T(8,128)(2,1)S(1)}, bf16[2,320,128]{2,1,0:T(8,128)(2,1)S(1)}, u32[]{:S(2)}, u32[]{:S(2)}) collective-permute-start(bf16[2,320,128]{2,1,0:T(8,128)(2,1)S(1)} %get-tuple-element.30), channel_id=1, source_target_pairs={{0,2},{1,3},{2,0},{3,1},{4,6},{5,7},{6,4},{7,5},{8,10},{9,11},{10,... | collective-permute-start | bytes 491528 | tf_op jit(solution)/shard_map/ppermute | solution.py:279
  18.6 1.4 %collective-permute-start.2 = (bf16[2,320,128]{2,1,0:T(8,128)(2,1)S(1)}, bf16[2,320,128]{2,1,0:T(8,128)(2,1)S(1)}, u32[]{:S(2)}, u32[]{:S(2)}) collective-permute-start(bf16[2,320,128]{2,1,0:T(8,128)(2,1)S(1)} %get-tuple-element.30), channel_id=1, source_target_pairs={{0,3},{1,0},{2,1},{3,2},{4,7},{5,4},{6,5},{7,6},{8,11},{9,8},{10,9... | collective-permute-start | bytes 491528 | tf_op jit(solution)/shard_map/ppermute | solution.py:279
  20.1 0.6 collective-permute-start.1
  20.7 3.2 %collective-permute-start.6 = (bf16[2,320,128]{2,1,0:T(8,128)(2,1)S(1)}, bf16[2,320,128]{2,1,0:T(8,128)(2,1)S(1)}, u32[]{:S(2)}, u32[]{:S(2)}) collective-permute-start(bf16[2,320,128]{2,1,0:T(8,128)(2,1)S(1)} %get-tuple-element.34), channel_id=1, source_target_pairs={{0,16},{8,24},{16,0},{24,8},{1,17},{9,25},{17,1},{25,9},{2,18},{10... | collective-permute-start | bytes 491528 | tf_op jit(solution)/shard_map/ppermute | solution.py:285
  23.9 1.1 collective-permute-start.5
  24.9 0.1 collective-permute-done.3
  25.0 1.6 %collective-permute-start.4 = (bf16[2,320,128]{2,1,0:T(8,128)(2,1)S(1)}, bf16[2,320,128]{2,1,0:T(8,128)(2,1)S(1)}, u32[]{:S(2)}, u32[]{:S(2)}) collective-permute-start(bf16[2,320,128]{2,1,0:T(8,128)(2,1)S(1)} %get-tuple-element.34), channel_id=1, source_target_pairs={{0,8},{8,16},{16,24},{24,0},{1,9},{9,17},{17,25},{25,1},{2,10},{10... | collective-permute-start | bytes 491528 | tf_op jit(solution)/shard_map/ppermute | solution.py:285
  26.6 0.2 collective-permute-done.2
  26.8 0.0 collective-permute-done.1
  26.8 1.7 %collective-permute-done.6 = bf16[2,320,128]{2,1,0:T(8,128)(2,1)S(1)} collective-permute-done((bf16[2,320,128]{2,1,0:T(8,128)(2,1)S(1)}, bf16[2,320,128]{2,1,0:T(8,128)(2,1)S(1)}, u32[]{:S(2)}, u32[]{:S(2)}) %collective-permute-start.6) | collective-permute-done | bytes 163872 | tf_op jit(solution)/shard_map/ppermute | solution.py:285
  28.5 1.9 %collective-permute-done.5 = bf16[2,320,128]{2,1,0:T(8,128)(2,1)S(1)} collective-permute-done((bf16[2,320,128]{2,1,0:T(8,128)(2,1)S(1)}, bf16[2,320,128]{2,1,0:T(8,128)(2,1)S(1)}, u32[]{:S(2)}, u32[]{:S(2)}) %collective-permute-start.5) | collective-permute-done | bytes 163872 | tf_op jit(solution)/shard_map/ppermute | solution.py:285
  30.4 1.1 collective-permute-done.4
  31.6 0.1 pad_maximum_fusion.a0
  31.6 0.1 pad_maximum_fusion.1.b0
  31.7 2.1 %collective-permute-start.9 = (bf16[4,2,320,128]{3,2,1,0:T(8,128)(2,1)S(1)}, bf16[4,2,320,128]{3,2,1,0:T(8,128)(2,1)S(1)}, u32[]{:S(2)}, u32[]{:S(2)}) collective-permute-start(bf16[4,2,320,128]{3,2,1,0:T(8,128)(2,1)S(1)} %pad_maximum_fusion.a0), channel_id=1, source_target_pairs={{0,16},{8,24},{16,0},{24,8},{1,17},{9,25},{17,1},{25,9},{2,18},{10... | collective-permute-start | bytes 1966088 | tf_op jit(solution)/shard_map/ppermute | solution.py:285
  33.8 1.1 collective-permute-start.8
  34.9 1.0 collective-permute-start.7
  35.8 2.4 %collective-permute-start.12 = (bf16[4,2,320,128]{3,2,1,0:T(8,128)(2,1)S(1)}, bf16[4,2,320,128]{3,2,1,0:T(8,128)(2,1)}, u32[]{:S(2)}, u32[]{:S(2)}) collective-permute-start(bf16[4,2,320,128]{3,2,1,0:T(8,128)(2,1)S(1)} %pad_maximum_fusion.1.b0), channel_id=1, source_target_pairs={{0,2},{1,3},{2,0},{3,1},{4,6},{5,7},{6,4},{7,5},{8,10},{9,11},{10,... | collective-permute-start | bytes 1966088 | tf_op jit(solution)/shard_map/ppermute | solution.py:279
  38.2 1.2 collective-permute-start.11
  39.4 11.7 %collective-permute-done.9.a3 = bf16[4,2,320,128]{3,2,1,0:T(8,128)(2,1)S(1)} collective-permute-done((bf16[4,2,320,128]{3,2,1,0:T(8,128)(2,1)S(1)}, bf16[4,2,320,128]{3,2,1,0:T(8,128)(2,1)S(1)}, u32[]{:S(2)}, u32[]{:S(2)}) %collective-permute-start.9) | collective-permute-done | bytes 655392 | tf_op jit(solution)/shard_map/ppermute | solution.py:285
  51.0 1.5 %collective-permute-start.10 = (bf16[4,2,320,128]{3,2,1,0:T(8,128)(2,1)S(1)}, bf16[4,2,320,128]{3,2,1,0:T(8,128)(2,1)}, u32[]{:S(2)}, u32[]{:S(2)}) collective-permute-start(bf16[4,2,320,128]{3,2,1,0:T(8,128)(2,1)S(1)} %pad_maximum_fusion.1.b0), channel_id=1, source_target_pairs={{0,1},{1,2},{2,3},{3,0},{4,5},{5,6},{6,7},{7,4},{8,9},{9,10},{10,1... | collective-permute-start | bytes 1966088 | tf_op jit(solution)/shard_map/ppermute | solution.py:279
  52.5 0.1 copy.15
  52.6 0.1 reshape.20.spos
  52.7 0.0 copy-done.1
  52.7 0.0 copy-done.3
  52.8 0.0 copy-done.2
  52.8 0.0 copy-start
  52.8 2.2 %copy-done = bf16[32,4,128,128]{3,2,1,0:T(8,128)(2,1)S(1)} copy-done((bf16[32,4,128,128]{3,2,1,0:T(8,128)(2,1)S(1)}, bf16[32,4,128,128]{3,2,1,0:T(8,128)(2,1)}, u32[]{:S(2)}) %copy-start) | copy-done | bytes 4194328
  55.0 3.3 %early.1 = (bf16[1024,128]{1,0:T(8,128)(2,1)S(1)}, bf16[128,1024]{1,0:T(8,128)(2,1)S(1)}, f32[128,128]{1,0:T(8,128)S(1)}, bf16[32,512,128]{2,1,0:T(8,128)(2,1)S(...) custom-call(bf16[1,8,128,128]{3,2,1,0:T(8,128)(2,1)S(1)} %copy-done.2, ...), custom_call_target="tpu_custom_call" | custom-call | flops 1258291200 | bytes 20971520 | tf_op jit(solution)/shard_map/early/pallas_call | solution.py:87
  58.3 3.4 %collective-permute-done.8.a2 = bf16[4,2,320,128]{3,2,1,0:T(8,128)(2,1)} collective-permute-done((bf16[4,2,320,128]{3,2,1,0:T(8,128)(2,1)S(1)}, bf16[4,2,320,128]{3,2,1,0:T(8,128)(2,1)}, u32[]{:S(2)}, u32[]{:S(2)}) %collective-permute-start.8) | collective-permute-done | bytes 655392 | tf_op jit(solution)/shard_map/ppermute | solution.py:285
  61.7 0.0 collective-permute-done.7.a1
  61.7 0.0 collective-permute-done.12.b3
  61.7 3.4 %collective-permute-done.11.b2 = bf16[4,2,320,128]{3,2,1,0:T(8,128)(2,1)} collective-permute-done((bf16[4,2,320,128]{3,2,1,0:T(8,128)(2,1)S(1)}, bf16[4,2,320,128]{3,2,1,0:T(8,128)(2,1)}, u32[]{:S(2)}, u32[]{:S(2)}) %collective-permute-start.11) | collective-permute-done | bytes 655392 | tf_op jit(solution)/shard_map/ppermute | solution.py:279
  65.0 0.0 collective-permute-done.10.b1
  65.1 0.0 copy-done.5
  65.1 19.0 %late.1 = (bf16[1,8,128,128]{3,2,1,0:T(8,128)(2,1)}, bf16[1,128,128]{2,1,0:T(8,128)(2,1)}, bf16[32,4,128,128]{3,2,1,0:T(8,128)(2,1)}, bf16[32,128,128]{2,1,0:T(8,128)(2,1)}, bf16[4096,128]{1,0:T(8,128)(2,1)S(1)}) custom-call(s32[1]{0:T(128)} %bitcast.pos, s32[1,8]{1,0:T(1,128)S(1)} %copy-done.5, s32[96]{0:T(128)S(1)} %reshape.20.spos, s32[4096]{0:T(1024)S(1)} %copy-done.4, ...), custom_call_target="tpu_custom_call" | custom-call | flops 3019898880 | bytes 20971520 | tf_op jit(solution)/shard_map/late/pallas_call | solution.py:233
  84.1 38.9 %all_to_all.12 = bf16[32,128,128]{2,1,0:T(8,128)(2,1)S(1)} all-to-all(bf16[32,128,128]{2,1,0:T(8,128)(2,1)S(1)} %bitcast.11), channel_id=1, replica_groups=mesh['grp'=8,'row'=4,'col'=8] {'row','col'}, dimensions={0} | all-to-all | bytes 2097152 | tf_op jit(solution)/shard_map/all_to_all | solution.py:315
  123.0 1.0 copy.17
  (4 shorter events, 0.0 us)
Async XLA Ops:
  0.6 51.9 %copy-start.6 = (s32[32,3]{0,1:T(4,128)S(1)}, s32[32,3]{0,1:T(4,128)}, u32[]{:S(2)}) copy-start(s32[32,3]{0,1:T(4,128)} %param.15) | copy-start | bytes 1156
  0.6 52.1 %copy-start.1 = (bf16[32,128,128]{2,1,0:T(8,128)(2,1)S(1)}, bf16[32,128,128]{2,1,0:T(8,128)(2,1)}, u32[]{:S(2)}) copy-start(bf16[32,128,128]{2,1,0:T(8,128)(2,1)} %si.1) | copy-start | bytes 3145732
  0.7 52.1 %copy-start.3 = (bf16[1,128,128]{2,1,0:T(8,128)(2,1)S(1)}, bf16[1,128,128]{2,1,0:T(8,128)(2,1)}, u32[]{:S(2)}) copy-start(bf16[1,128,128]{2,1,0:T(8,128)(2,1)} %fi.1) | copy-start | bytes 98308
  0.7 52.1 %copy-start.2 = (bf16[1,8,128,128]{3,2,1,0:T(8,128)(2,1)S(1)}, bf16[1,8,128,128]{3,2,1,0:T(8,128)(2,1)}, u32[]{:S(2)}) copy-start(bf16[1,8,128,128]{3,2,1,0:T(8,128)(2,1)} %fp.1) | copy-start | bytes 786436
  2.4 14.0 %collective-permute-start = (bf16[2,320,128]{2,1,0:T(8,128)(2,1)}, bf16[2,320,128]{2,1,0:T(8,128)(2,1)S(1)}, u32[]{:S(2)}, u32[]{:S(2)}) collective-permute-start(bf16[2,320,128]{2,1,0:T(8,128)(2,1)} %pack.1), channel_id=1, source_target_pairs={{0,4},{1,5},{2,6},{3,7},{4,0},{5,1},{6,2},{7,3},{8,12},{9,13},{10,... | collective-permute-start | bytes 491528 | tf_op jit(solution)/shard_map/ppermute | solution.py:306
  16.4 48.6 %copy-start.4 = (s32[4096]{0:T(1024)S(1)}, s32[4096]{0:T(1024)}, u32[]{:S(2)}) copy-start(s32[4096]{0:T(1024)} %order.1) | copy-start | bytes 49156
  16.4 48.6 %copy-start.5 = (s32[1,8]{1,0:T(1,128)S(1)}, s32[1,8]{1,0:T(1,128)}, u32[]{:S(2)}) copy-start(s32[1,8]{1,0:T(1,128)} %fidx.1) | copy-start | bytes 100
  16.4 8.6 %collective-permute-start.3 = (bf16[2,320,128]{2,1,0:T(8,128)(2,1)S(1)}, bf16[2,320,128]{2,1,0:T(8,128)(2,1)S(1)}, u32[]{:S(2)}, u32[]{:S(2)}) collective-permute-start(bf16[2,320,128]{2,1,0:T(8,128)(2,1)S(1)} %get-tuple-element.30), channel_id=1, source_target_pairs={{0,2},{1,3},{2,0},{3,1},{4,6},{5,7},{6,4},{7,5},{8,10},{9,11},{10,... | collective-permute-start | bytes 491528 | tf_op jit(solution)/shard_map/ppermute | solution.py:279
  18.6 8.1 %collective-permute-start.2 = (bf16[2,320,128]{2,1,0:T(8,128)(2,1)S(1)}, bf16[2,320,128]{2,1,0:T(8,128)(2,1)S(1)}, u32[]{:S(2)}, u32[]{:S(2)}) collective-permute-start(bf16[2,320,128]{2,1,0:T(8,128)(2,1)S(1)} %get-tuple-element.30), channel_id=1, source_target_pairs={{0,3},{1,0},{2,1},{3,2},{4,7},{5,4},{6,5},{7,6},{8,11},{9,8},{10,9... | collective-permute-start | bytes 491528 | tf_op jit(solution)/shard_map/ppermute | solution.py:279
  20.1 6.7 %collective-permute-start.1 = (bf16[2,320,128]{2,1,0:T(8,128)(2,1)S(1)}, bf16[2,320,128]{2,1,0:T(8,128)(2,1)S(1)}, u32[]{:S(2)}, u32[]{:S(2)}) collective-permute-start(bf16[2,320,128]{2,1,0:T(8,128)(2,1)S(1)} %get-tuple-element.30), channel_id=1, source_target_pairs={{0,1},{1,2},{2,3},{3,0},{4,5},{5,6},{6,7},{7,4},{8,9},{9,10},{10,1... | collective-permute-start | bytes 491528 | tf_op jit(solution)/shard_map/ppermute | solution.py:279
  20.7 7.9 %collective-permute-start.6 = (bf16[2,320,128]{2,1,0:T(8,128)(2,1)S(1)}, bf16[2,320,128]{2,1,0:T(8,128)(2,1)S(1)}, u32[]{:S(2)}, u32[]{:S(2)}) collective-permute-start(bf16[2,320,128]{2,1,0:T(8,128)(2,1)S(1)} %get-tuple-element.34), channel_id=1, source_target_pairs={{0,16},{8,24},{16,0},{24,8},{1,17},{9,25},{17,1},{25,9},{2,18},{10... | collective-permute-start | bytes 491528 | tf_op jit(solution)/shard_map/ppermute | solution.py:285
  23.9 6.6 %collective-permute-start.5 = (bf16[2,320,128]{2,1,0:T(8,128)(2,1)S(1)}, bf16[2,320,128]{2,1,0:T(8,128)(2,1)S(1)}, u32[]{:S(2)}, u32[]{:S(2)}) collective-permute-start(bf16[2,320,128]{2,1,0:T(8,128)(2,1)S(1)} %get-tuple-element.34), channel_id=1, source_target_pairs={{0,24},{8,0},{16,8},{24,16},{1,25},{9,1},{17,9},{25,17},{2,26},{10... | collective-permute-start | bytes 491528 | tf_op jit(solution)/shard_map/ppermute | solution.py:285
  25.0 6.5 %collective-permute-start.4 = (bf16[2,320,128]{2,1,0:T(8,128)(2,1)S(1)}, bf16[2,320,128]{2,1,0:T(8,128)(2,1)S(1)}, u32[]{:S(2)}, u32[]{:S(2)}) collective-permute-start(bf16[2,320,128]{2,1,0:T(8,128)(2,1)S(1)} %get-tuple-element.34), channel_id=1, source_target_pairs={{0,8},{8,16},{16,24},{24,0},{1,9},{9,17},{17,25},{25,1},{2,10},{10... | collective-permute-start | bytes 491528 | tf_op jit(solution)/shard_map/ppermute | solution.py:285
  31.7 19.3 %collective-permute-start.9 = (bf16[4,2,320,128]{3,2,1,0:T(8,128)(2,1)S(1)}, bf16[4,2,320,128]{3,2,1,0:T(8,128)(2,1)S(1)}, u32[]{:S(2)}, u32[]{:S(2)}) collective-permute-start(bf16[4,2,320,128]{3,2,1,0:T(8,128)(2,1)S(1)} %pad_maximum_fusion.a0), channel_id=1, source_target_pairs={{0,16},{8,24},{16,0},{24,8},{1,17},{9,25},{17,1},{25,9},{2,18},{10... | collective-permute-start | bytes 1966088 | tf_op jit(solution)/shard_map/ppermute | solution.py:285
  33.8 27.9 %collective-permute-start.8 = (bf16[4,2,320,128]{3,2,1,0:T(8,128)(2,1)S(1)}, bf16[4,2,320,128]{3,2,1,0:T(8,128)(2,1)}, u32[]{:S(2)}, u32[]{:S(2)}) collective-permute-start(bf16[4,2,320,128]{3,2,1,0:T(8,128)(2,1)S(1)} %pad_maximum_fusion.a0), channel_id=1, source_target_pairs={{0,24},{8,0},{16,8},{24,16},{1,25},{9,1},{17,9},{25,17},{2,26},{10... | collective-permute-start | bytes 1966088 | tf_op jit(solution)/shard_map/ppermute | solution.py:285
  34.9 26.8 %collective-permute-start.7 = (bf16[4,2,320,128]{3,2,1,0:T(8,128)(2,1)S(1)}, bf16[4,2,320,128]{3,2,1,0:T(8,128)(2,1)}, u32[]{:S(2)}, u32[]{:S(2)}) collective-permute-start(bf16[4,2,320,128]{3,2,1,0:T(8,128)(2,1)S(1)} %pad_maximum_fusion.a0), channel_id=1, source_target_pairs={{0,8},{8,16},{16,24},{24,0},{1,9},{9,17},{17,25},{25,1},{2,10},{10... | collective-permute-start | bytes 1966088 | tf_op jit(solution)/shard_map/ppermute | solution.py:285
  35.8 25.8 %collective-permute-start.12 = (bf16[4,2,320,128]{3,2,1,0:T(8,128)(2,1)S(1)}, bf16[4,2,320,128]{3,2,1,0:T(8,128)(2,1)}, u32[]{:S(2)}, u32[]{:S(2)}) collective-permute-start(bf16[4,2,320,128]{3,2,1,0:T(8,128)(2,1)S(1)} %pad_maximum_fusion.1.b0), channel_id=1, source_target_pairs={{0,2},{1,3},{2,0},{3,1},{4,6},{5,7},{6,4},{7,5},{8,10},{9,11},{10,... | collective-permute-start | bytes 1966088 | tf_op jit(solution)/shard_map/ppermute | solution.py:279
  38.2 26.9 %collective-permute-start.11 = (bf16[4,2,320,128]{3,2,1,0:T(8,128)(2,1)S(1)}, bf16[4,2,320,128]{3,2,1,0:T(8,128)(2,1)}, u32[]{:S(2)}, u32[]{:S(2)}) collective-permute-start(bf16[4,2,320,128]{3,2,1,0:T(8,128)(2,1)S(1)} %pad_maximum_fusion.1.b0), channel_id=1, source_target_pairs={{0,3},{1,0},{2,1},{3,2},{4,7},{5,4},{6,5},{7,6},{8,11},{9,8},{10,9... | collective-permute-start | bytes 1966088 | tf_op jit(solution)/shard_map/ppermute | solution.py:279
  51.0 14.0 %collective-permute-start.10 = (bf16[4,2,320,128]{3,2,1,0:T(8,128)(2,1)S(1)}, bf16[4,2,320,128]{3,2,1,0:T(8,128)(2,1)}, u32[]{:S(2)}, u32[]{:S(2)}) collective-permute-start(bf16[4,2,320,128]{3,2,1,0:T(8,128)(2,1)S(1)} %pad_maximum_fusion.1.b0), channel_id=1, source_target_pairs={{0,1},{1,2},{2,3},{3,0},{4,5},{5,6},{6,7},{7,4},{8,9},{9,10},{10,1... | collective-permute-start | bytes 1966088 | tf_op jit(solution)/shard_map/ppermute | solution.py:279
  52.8 2.2 %copy-start = (bf16[32,4,128,128]{3,2,1,0:T(8,128)(2,1)S(1)}, bf16[32,4,128,128]{3,2,1,0:T(8,128)(2,1)}, u32[]{:S(2)}) copy-start(bf16[32,4,128,128]{3,2,1,0:T(8,128)(2,1)} %sp.1) | copy-start | bytes 12582916
